TPU v7x, 768 devices: a whole 4x8x12 slice. The times are simulated.
768 devices in a mesh: loop: 8 (over z_hi, core), rep: 96 (over x, y, z_lo).
Axes of the slice: x: 4, y: 8, z: 12 (z_hi: 4, z_lo: 3; z = z_hi * 3 + z_lo), core: 2. Of those that a mesh axis runs over, the one named last changes fastest.
Arguments:
- features: float32 [196608, 256], P(('loop', 'rep')), may hold values from -6 to 6
- weight: float32 [256, 256], replicated, may hold values from -0.375 to 0.375
- bias: float32 [256], replicated, may hold values from -3 to 3
- tile_values: float32 [768, 32, 128, 128], P(('loop', 'rep')), may hold values from -0.125 to 0.125
- tile_rows: int32 [768, 32], P(('loop', 'rep')), may hold values from 0 to 9
- tile_cols: int32 [768, 32], P(('loop', 'rep')), may hold values from 0 to 1
- tile_counts: int32 [768, 8], P(('loop', 'rep')), may hold values from 1 to 4, as said below
- cotangent: float32 [196608, 256], P(('loop', 'rep')), may hold values from -60 to 60
Outputs:
- output: float32 [196608, 256], P(('loop', 'rep'))
- grad_features: float32 [196608, 256], P(('loop', 'rep'))
- grad_weight: float32 [256, 256], replicated
- grad_bias: float32 [256], replicated
Inputs may be any that keep to these rules, and one draw needn't show every extreme that they name: `tile_counts`: every entry is at least 1 and at most 4; 4 is reached in every draw. `tile_rows`: within one device, two live slots may name the same tile place; such tiles add.
All inputs are finite; a program needn't handle non-finite values.
Results may differ from a plain program's by a relative error of at most 0.00013.
Values sent between devices are 32-bit elements; how exact they have to be, the bound alone decides.
No kernel may reach another device: no remote copies, remote signals or barrier semaphores. Data moves between devices by JAX's collectives and lax.ppermute only.
A program may use at most 32 MiB of HBM per device.

v0:
```python
import jax
import jax.numpy as jnp
from jax import lax
from jax.sharding import PartitionSpec as P

BAND = 2


EXACT = lax.Precision.HIGHEST


def passed_along(value, axis, by):
    length = lax.axis_size(axis)
    return lax.ppermute(value, axis, [(i, (i + by) % length) for i in range(length)])


def activate(values):
    return jax.nn.gelu(values, approximate=True)


def from_rep(field, offset):
    return passed_along(field, "rep", offset)


def near_rows(field, offset):
    return passed_along(field, "rep", offset)


def per_device(features, weight, bias, tile_values, tile_rows, tile_cols, tile_counts, cotangent):
    node_rows = features.shape[0]
    feature_width = features.shape[1]
    tile_size = tile_values.shape[2]
    row_tiles = node_rows // tile_size
    slot_values = tile_values[0]
    band_index = tile_rows[0]
    slot_total = slot_values.shape[0]
    loop_size = lax.axis_size("loop")
    per_block = slot_total // loop_size
    slot_ids = jnp.arange(slot_total, dtype=jnp.int32)
    live_mask = (slot_ids % per_block < jnp.repeat(tile_counts[0], per_block)).astype(jnp.float32)
    band_size = (2 * BAND + 1) * row_tiles
    band_place = (band_index[None, :] == jnp.arange(band_size, dtype=jnp.int32)[:, None]).astype(
        jnp.float32
    ) * live_mask[None, :]
    column_target = slot_ids // per_block * row_tiles + tile_cols[0]
    piece = lax.all_gather(features, "loop", axis=0, tiled=True)
    blocks = piece.shape[0] // node_rows
    piece_values = slot_values
    piece_columns = column_target
    piece_tiles = piece.reshape(blocks * row_tiles, tile_size, feature_width)
    chosen = jnp.take(piece_tiles, piece_columns, axis=0)
    product = jnp.einsum("kab,kbh->kah", piece_values, chosen, precision=EXACT)
    partial_value = jnp.einsum("rk,kah->rah", band_place, product, precision=EXACT)
    partial_value = partial_value.reshape(2 * BAND + 1, node_rows, feature_width)
    gathered = partial_value[BAND]
    for offset in range(1, BAND + 1):
        gathered = (
            gathered
            + from_rep(partial_value[BAND - offset], -offset)
            + from_rep(partial_value[BAND + offset], offset)
        )
    pre_act = jnp.dot(gathered, weight, precision=EXACT, preferred_element_type=jnp.float32) + bias
    output, pull_back = jax.vjp(activate, pre_act)
    grad_pre = pull_back(cotangent)[0]
    carried = jnp.dot(grad_pre, weight.T, precision=EXACT, preferred_element_type=jnp.float32)
    neighbours = [near_rows(carried, offset) for offset in range(BAND, 0, -1)]
    neighbours = (
        neighbours + [carried] + [near_rows(carried, -offset) for offset in range(1, BAND + 1)]
    )
    band_field = jnp.stack(neighbours).reshape(band_size, tile_size, feature_width)
    blocks = node_rows * lax.axis_size("loop") // node_rows
    piece_values = slot_values
    piece_columns = column_target
    chosen = jnp.take(band_field, band_index, axis=0)
    product = jnp.einsum("kba,kbh->kah", piece_values, chosen, precision=EXACT)
    target = (
        piece_columns[None, :] == jnp.arange(blocks * row_tiles, dtype=jnp.int32)[:, None]
    ).astype(jnp.float32) * live_mask[None, :]
    summed = jnp.einsum("tk,kah->tah", target, product, precision=EXACT)
    spread = lax.psum_scatter(
        summed.reshape(node_rows * lax.axis_size("loop"), feature_width),
        "loop",
        scatter_dimension=0,
        tiled=True,
    )
    weight_term = jnp.dot(gathered.T, grad_pre, precision=EXACT, preferred_element_type=jnp.float32)
    bias_term = jnp.sum(grad_pre, axis=0)
    node_total = node_rows * loop_size * lax.axis_size("rep")
    weight_whole, bias_whole = lax.psum((weight_term, bias_term), ("loop", "rep"))
    return (output, spread, weight_whole / node_total, bias_whole / node_total)


def solution(mesh):
    return jax.shard_map(
        per_device,
        mesh=mesh,
        in_specs=(
            P(("loop", "rep"), None),
            P(),
            P(),
            P(("loop", "rep"), None, None, None),
            P(("loop", "rep"), None),
            P(("loop", "rep"), None),
            P(("loop", "rep"), None),
            P(("loop", "rep"), None),
        ),
        out_specs=(P(("loop", "rep"), None), P(("loop", "rep"), None), P(), P()),
        check_vma=False,
    )
```

profile of v0, /device:TPU:92, one launch (start us, length us, event | category | flops | bytes accessed | tf_op | source)
XLA Modules:
  0.0 672.8 jit_solution(16021934747576391494)
XLA Ops:
  7.2 0.0 copy-start
  7.2 0.0 all-gather.2.cloned.1.call-start
  7.2 0.7 all-gather.2.cloned.1.call-update
  7.9 0.0 all-reduce.2.cloned.1.call-start
  8.0 0.7 broadcast_in_dim.27
  8.7 0.1 reshape.181
  8.8 0.7 fusion.40
  9.4 0.7 compare_and_fusion.1
  10.1 0.7 compare_and_fusion
  10.8 58.1 %all-gather.2.cloned.1.call-done = f32[2048,256]{1,0:T(8,128)} async-done(((f32[256,256]{1,0:T(8,128)}), f32[2048,256]{1,0:T(8,128)}) %all-gather.2.cloned.1.call-update) | async-done | bytes 2097168 | tf_op jit(solution)/shard_map/all_gather | solution.py:46
  68.8 4.3 gather_fusion
  73.2 0.0 copy-done
  73.2 10.6 %fusion.6 = f32[32,256,128]{2,1,0:T(8,128)} fusion(f32[32,128,256]{2,1,0:T(8,128)} %gather_fusion, f32[1,32,128,128]{3,2,1,0:T(8,128)S(1)} %copy-done, pred[32]{0:T(512)(128)(4,1)S(1)} %compare_and_fusion.1), kind=kOutput, calls=%fused_computation.8 | convolution fusion | flops 1611661312 | bytes 10485792 | tf_op jit(solution)/shard_map/kab,kbh->kah/dot_general | solution.py:52
  83.8 0.0 copy-start.2
  83.8 5.5 copy.18
  89.3 0.0 copy-done.2
  89.3 3.9 fusion.2
  93.2 0.0 copy-start.5
  93.2 0.4 fusion.48
  93.6 0.0 copy-start.1
  93.6 0.0 copy-start.3
  93.6 0.0 copy-start.4
  93.7 2.3 collective-permute-start
  96.0 3.7 collective-permute-start.1
  99.7 3.5 collective-permute-start.2
  103.2 4.5 collective-permute-start.3
  107.7 0.0 copy-done.5
  107.8 0.0 collective-permute-done
  107.8 2.0 collective-permute-done.1
  109.8 7.5 %collective-permute-done.2 = f32[256,256]{1,0:T(8,128)S(1)} collective-permute-done((f32[256,256]{1,0:T(8,128)S(1)}, f32[256,256]{1,0:T(8,128)S(1)}, u32[]{:S(2)}, u32[]{:S(2)}) %collective-permute-start.2) | collective-permute-done | bytes 262176 | tf_op jit(solution)/shard_map/ppermute | solution.py:14
  117.3 3.8 collective-permute-done.3
  121.1 0.1 fusion.22
  121.2 0.0 copy-done.1
  121.2 0.0 copy-done.3
  121.2 0.0 copy-done.4
  121.2 1.3 fusion.46
  122.5 1.1 fusion.49
  123.6 5.4 collective-permute-start.4
  129.1 2.5 collective-permute-start.5
  131.6 1.3 fusion.50
  132.9 2.3 collective-permute-start.7
  135.2 3.0 collective-permute-start.6
  138.1 0.0 all-reduce.2.cloned.1.call-update
  138.2 0.2 reduce-scatter.2.cloned.1.call-start
  138.4 7.1 %collective-permute-done.4 = f32[256,256]{1,0:T(8,128)} collective-permute-done((f32[256,256]{1,0:T(8,128)}, f32[256,256]{1,0:T(8,128)}, u32[]{:S(2)}, u32[]{:S(2)}) %collective-permute-start.4) | collective-permute-done | bytes 262176 | tf_op jit(solution)/shard_map/ppermute | solution.py:14
  145.5 1.0 bitcast_dynamic-update-slice_fusion.4
  146.4 0.0 collective-permute-done.5
  146.4 1.0 bitcast_dynamic-update-slice_fusion.3
  147.4 1.0 bitcast_dynamic-update-slice_fusion.2
  148.4 4.1 collective-permute-done.6
  152.5 1.0 bitcast_dynamic-update-slice_fusion.1
  153.4 0.0 collective-permute-done.7
  153.4 1.0 bitcast_dynamic-update-slice_fusion
  154.4 2.8 gather_fusion.1
  157.2 10.5 %fusion.4 = f32[32,256,128]{2,1,0:T(8,128)} fusion(f32[32,128,256]{2,1,0:T(8,128)} %gather_fusion.1, f32[1,32,128,128]{3,2,1,0:T(8,128)S(1)} %copy-done, pred[32]{0:T(512)(128)(4,1)S(1)} %compare_and_fusion), kind=kOutput, calls=%fused_computation.6 | convolution fusion | flops 1611661312 | bytes 10485792 | tf_op jit(solution)/shard_map/kba,kbh->kah/dot_general | solution.py:75
  167.8 5.5 copy.19
  173.2 3.9 fusion
  177.1 2.5 copy.17
  179.7 0.0 reduce-scatter.2.cloned.1.call-update
  179.7 103.6 %psum.15 = f32[256]{0:T(256)S(1)} all-reduce(f32[256]{0:T(256)S(1)} %get-tuple-element.4), channel_id=1, replica_groups=mesh['loop'=8,'rep'=96] {'loop','rep'}, use_global_device_ids=true, to_apply=%region_3.4 | all-reduce | flops 256 | bytes 2048 | tf_op jit(solution)/shard_map/psum | solution.py:89
  283.3 0.6 broadcast_multiply_fusion.1
  283.9 319.5 %all-reduce.2.cloned.1.call-done = f32[256,256]{1,0:T(8,128)} async-done(((f32[256,256]{1,0:T(8,128)}), f32[256,256]{1,0:T(8,128)}) %all-reduce.2.cloned.1.call-update) | async-done | bytes 262160 | tf_op jit(solution)/shard_map/psum | solution.py:89
  603.3 1.7 broadcast_multiply_fusion
  605.0 61.2 %reduce-scatter.2.cloned.1.call-done = f32[256,256]{1,0:T(8,128)} async-done(((f32[2048,256]{1,0:T(8,128)}), f32[256,256]{1,0:T(8,128)}) %reduce-scatter.2.cloned.1.call-update) | async-done | bytes 262160 | tf_op jit(solution)/shard_map/reduce_scatter | solution.py:80
  (10 shorter events, 0.1 us)
Async XLA Ops:
  7.2 66.0 %copy-start = (f32[1,32,128,128]{3,2,1,0:T(8,128)S(1)}, f32[1,32,128,128]{3,2,1,0:T(8,128)}, u32[]{:S(2)}) copy-start(f32[1,32,128,128]{3,2,1,0:T(8,128)} %param.11) | copy-start | bytes 6291460
  7.2 61.7 %all-gather.2.cloned.1.call-start = ((), (), s32[]{:S(2)}) async-start(), calls=%async_computation.1 | async-start | bytes 2359296 | tf_op jit(solution)/shard_map/all_gather | solution.py:46
  7.9 595.4 %all-reduce.2.cloned.1.call-start = ((), (), s32[]{:S(2)}) async-start(), calls=%async_computation.3 | async-start | bytes 524288 | tf_op jit(solution)/shard_map/psum | solution.py:89
  83.8 5.5 copy-start.2
  93.2 14.6 %copy-start.5 = (s32[1,32]{1,0:T(1,128)S(1)}, s32[1,32]{1,0:T(1,128)}, u32[]{:S(2)}) copy-start(s32[1,32]{1,0:T(1,128)} %param.13) | copy-start | bytes 388
  93.6 27.6 %copy-start.1 = (f32[256,256]{1,0:T(8,128)S(1)}, f32[256,256]{1,0:T(8,128)}, u32[]{:S(2)}) copy-start(f32[256,256]{1,0:T(8,128)} %param.9) | copy-start | bytes 786436
  93.6 27.6 %copy-start.3 = (f32[256,256]{1,0:T(8,128)S(1)}, f32[256,256]{1,0:T(8,128)}, u32[]{:S(2)}) copy-start(f32[256,256]{1,0:T(8,128)} %param.15) | copy-start | bytes 786436
  93.6 27.6 %copy-start.4 = (f32[256]{0:T(256)S(1)}, f32[256]{0:T(256)}, u32[]{:S(2)}) copy-start(f32[256]{0:T(256)} %param.10) | copy-start | bytes 3076
  93.7 14.0 %collective-permute-start = (f32[256,256]{1,0:T(8,128)S(1)}, f32[256,256]{1,0:T(8,128)S(1)}, u32[]{:S(2)}, u32[]{:S(2)}) collective-permute-start(f32[256,256]{1,0:T(8,128)S(1)} %bitcast.71), channel_id=1, source_target_pairs={{0,95},{1,0},{2,1},{3,2},{4,3},{5,4},{6,5},{7,6},{8,7},{9,8},{10,9... | collective-permute-start | bytes 786440 | tf_op jit(solution)/shard_map/ppermute | solution.py:14
  96.0 13.8 %collective-permute-start.1 = (f32[256,256]{1,0:T(8,128)S(1)}, f32[256,256]{1,0:T(8,128)S(1)}, u32[]{:S(2)}, u32[]{:S(2)}) collective-permute-start(f32[256,256]{1,0:T(8,128)S(1)} %bitcast.70), channel_id=1, source_target_pairs={{0,1},{1,2},{2,3},{3,4},{4,5},{5,6},{6,7},{7,8},{8,9},{9,10},{10,1... | collective-permute-start | bytes 786440 | tf_op jit(solution)/shard_map/ppermute | solution.py:14
  99.7 17.6 %collective-permute-start.2 = (f32[256,256]{1,0:T(8,128)S(1)}, f32[256,256]{1,0:T(8,128)S(1)}, u32[]{:S(2)}, u32[]{:S(2)}) collective-permute-start(f32[256,256]{1,0:T(8,128)S(1)} %bitcast.69), channel_id=1, source_target_pairs={{0,94},{1,95},{2,0},{3,1},{4,2},{5,3},{6,4},{7,5},{8,6},{9,7},{10,... | collective-permute-start | bytes 786440 | tf_op jit(solution)/shard_map/ppermute | solution.py:14
  103.2 17.9 %collective-permute-start.3 = (f32[256,256]{1,0:T(8,128)S(1)}, f32[256,256]{1,0:T(8,128)S(1)}, u32[]{:S(2)}, u32[]{:S(2)}) collective-permute-start(f32[256,256]{1,0:T(8,128)S(1)} %bitcast.68), channel_id=1, source_target_pairs={{0,2},{1,3},{2,4},{3,5},{4,6},{5,7},{6,8},{7,9},{8,10},{9,11},{10,... | collective-permute-start | bytes 786440 | tf_op jit(solution)/shard_map/ppermute | solution.py:14
  123.6 21.9 %collective-permute-start.4 = (f32[256,256]{1,0:T(8,128)}, f32[256,256]{1,0:T(8,128)}, u32[]{:S(2)}, u32[]{:S(2)}) collective-permute-start(f32[256,256]{1,0:T(8,128)} %fusion.49), channel_id=1, source_target_pairs={{0,2},{1,3},{2,4},{3,5},{4,6},{5,7},{6,8},{7,9},{8,10},{9,11},{10,... | collective-permute-start | bytes 786440 | tf_op jit(solution)/shard_map/ppermute | solution.py:14
  129.1 17.4 %collective-permute-start.5 = (f32[256,256]{1,0:T(8,128)}, f32[256,256]{1,0:T(8,128)}, u32[]{:S(2)}, u32[]{:S(2)}) collective-permute-start(f32[256,256]{1,0:T(8,128)} %fusion.49), channel_id=1, source_target_pairs={{0,1},{1,2},{2,3},{3,4},{4,5},{5,6},{6,7},{7,8},{8,9},{9,10},{10,1... | collective-permute-start | bytes 786440 | tf_op jit(solution)/shard_map/ppermute | solution.py:14
  132.9 20.6 %collective-permute-start.7 = (f32[256,256]{1,0:T(8,128)}, f32[256,256]{1,0:T(8,128)}, u32[]{:S(2)}, u32[]{:S(2)}) collective-permute-start(f32[256,256]{1,0:T(8,128)} %fusion.49), channel_id=1, source_target_pairs={{0,94},{1,95},{2,0},{3,1},{4,2},{5,3},{6,4},{7,5},{8,6},{9,7},{10,... | collective-permute-start | bytes 786440 | tf_op jit(solution)/shard_map/ppermute | solution.py:14
  135.2 17.3 %collective-permute-start.6 = (f32[256,256]{1,0:T(8,128)}, f32[256,256]{1,0:T(8,128)}, u32[]{:S(2)}, u32[]{:S(2)}) collective-permute-start(f32[256,256]{1,0:T(8,128)} %fusion.49), channel_id=1, source_target_pairs={{0,95},{1,0},{2,1},{3,2},{4,3},{5,4},{6,5},{7,6},{8,7},{9,8},{10,9... | collective-permute-start | bytes 786440 | tf_op jit(solution)/shard_map/ppermute | solution.py:14
  138.2 528.1 %reduce-scatter.2.cloned.1.call-start = ((), (), s32[]{:S(2)}) async-start(), calls=%async_computation.2 | async-start | bytes 2359296 | tf_op jit(solution)/shard_map/reduce_scatter | solution.py:80
Sparse Core Ops, SparseCore 0:
  10.5 58.3 all-gather.1
  138.3 465.0 all-reduce.1
  607.4 58.8 reduce-scatter.1
where the time goes:
time: 674 us; the launch traced here: 673 us
  waiting for transfers between devices  464 us (69%)
  blocking collectives  104 us (15%)
  matrix products  32.5 us (5%)
  starting transfers between devices  27.4 us (4%)
  local copies, waits for them, and re-layouts  26.9 us (4%)
  between operations  14 us (2%)
    psum x1, waiting for transfers between devices, per_device(): lax.psum((weight_term, bias_term), ('loop', 'rep'))  319 us
    psum x1, blocking collectives, per_device(): lax.psum((weight_term, bias_term), ('loop', 'rep'))  104 us
    reduce_scatter x1, waiting for transfers between devices, per_device(): lax.psum_scatter(summed.reshape(node_rows * lax.axis_size('loop'), featur...  61.2 us
    all_gather x1, waiting for transfers between devices, per_device(): piece = lax.all_gather(features, 'loop', axis=0, tiled=True)  58.1 us
    ppermute x8, starting transfers between devices, passed_along(): lax.ppermute(value, axis, [(i, (i + by) % length) for i in range(length)])  27.1 us
    ppermute x8, waiting for transfers between devices, passed_along(): lax.ppermute(value, axis, [(i, (i + by) % length) for i in range(length)])  24.5 us
  transfers between devices with their start and end apart: 11, of which 8 were waited for; matrix products, arithmetic and copies ran while one was open for 5% of the time, Pallas kernels for 0%

commit v1 on v0

v1 whole, which is shorter than its diff:
```python
import functools

import jax
import jax.numpy as jnp
from jax import lax
from jax.experimental import pallas as pl
from jax.experimental.pallas import tpu as pltpu
from jax.sharding import Mesh
from jax.sharding import PartitionSpec as P

Z_HI, CORE, X, Y, Z_LO = 4, 2, 4, 8, 3
AXES = ("z_hi", "core", "x", "y", "z_lo")
LOOP = ("z_hi", "core")
REP = ("x", "y", "z_lo")
N_REP = X * Y * Z_LO
COLUMN_BLOCKS = Z_HI * CORE
PER_BLOCK = 4
TILE = 128
ROWS = 256
H = 256
NODES = 196608
VMEM_LIMIT = 48 * 1024 * 1024

BAND_PLACE = ((3, 4, 0, 1, 2), (3, 2, 0, 1, 4), (1, 2, 0, 3, 4))


def split(value):
    high = value.astype(jnp.bfloat16)
    low = (value - high.astype(jnp.float32)).astype(jnp.bfloat16)
    return high, low


def dot(left, right):
    return jnp.dot(left, right, preferred_element_type=jnp.float32)


def dot3(left_high, left_low, right_high, right_low):
    return dot(left_high, right_high) + (dot(left_low, right_high) + dot(left_high, right_low))


def params():
    return pltpu.CompilerParams(vmem_limit_bytes=VMEM_LIMIT)


def cost(flops, size):
    return pl.CostEstimate(flops=flops, bytes_accessed=size, transcendentals=0)


def place_kernel(cols, counts, tiles, high, low, high_t, low_t):
    block = pl.program_id(0)
    for slot in range(PER_BLOCK):
        live = slot < counts[block]
        column = cols[block * PER_BLOCK + slot]
        tile = jnp.where(live, tiles[slot], 0.0)
        tile_t = tile.T
        span = pl.ds(slot * TILE, TILE)
        for half in range(ROWS // TILE):
            half_span = pl.ds(half * TILE, TILE)
            placed_high, placed_low = split(jnp.where(column == half, tile, 0.0))
            high[0, span, half_span] = placed_high
            low[0, span, half_span] = placed_low
            placed_high, placed_low = split(jnp.where(column == half, tile_t, 0.0))
            high_t[0, half_span, span] = placed_high
            low_t[0, half_span, span] = placed_low


def place_tiles(tiles, cols, counts):
    deep = PER_BLOCK * TILE
    plain = jax.ShapeDtypeStruct((COLUMN_BLOCKS, deep, ROWS), jnp.bfloat16)
    turned = jax.ShapeDtypeStruct((COLUMN_BLOCKS, ROWS, deep), jnp.bfloat16)
    plain_spec = pl.BlockSpec((1, deep, ROWS), lambda i, *_: (i, 0, 0))
    turned_spec = pl.BlockSpec((1, ROWS, deep), lambda i, *_: (i, 0, 0))
    return pl.pallas_call(
        place_kernel,
        grid_spec=pltpu.PrefetchScalarGridSpec(
            num_scalar_prefetch=2,
            grid=(COLUMN_BLOCKS,),
            in_specs=[pl.BlockSpec((PER_BLOCK, TILE, TILE), lambda i, *_: (i, 0, 0))],
            out_specs=[plain_spec, plain_spec, turned_spec, turned_spec],
        ),
        out_shape=[plain, plain, turned, turned],
        compiler_params=params(),
        cost_estimate=cost(0, 10 << 20),
        name="place_tiles",
    )(cols, counts, tiles)


def gather_kernel(n, carried, ids, rows, high, low, *refs):
    fields = refs[:n]
    before = refs[n : n + carried]
    outs = refs[n + carried : -1]
    total = refs[-1]
    step = pl.program_id(0)

    @pl.when(step == 0)
    def _():
        for j in range(5):
            total[2 * j : 2 * j + 2] = (
                before[j][...].reshape(2, TILE, H) if carried else jnp.zeros((2, TILE, H), jnp.float32)
            )

    for j in range(n):

        @pl.when(step == j)
        def _(j=j):
            field_high, field_low = split(fields[j][...])
            product = dot3(high[0], low[0], field_high, field_low)
            for slot in range(PER_BLOCK):
                row = rows[ids[j] * PER_BLOCK + slot]
                total[row] += product[slot * TILE : (slot + 1) * TILE]

    @pl.when(step == n - 1)
    def _():
        for j in range(5):
            outs[j][...] = total[2 * j : 2 * j + 2].reshape(ROWS, H)


def gather_terms(ids, rows, high, low, fields, before=()):
    n = len(fields)
    whole = pl.BlockSpec((ROWS, H), lambda i, *_: (0, 0))
    tiles = pl.BlockSpec((1, PER_BLOCK * TILE, ROWS), lambda i, ids, rows: (ids[i], 0, 0))
    return pl.pallas_call(
        functools.partial(gather_kernel, n, len(before)),
        grid_spec=pltpu.PrefetchScalarGridSpec(
            num_scalar_prefetch=2,
            grid=(n,),
            in_specs=[tiles, tiles] + [whole] * (n + len(before)),
            out_specs=[whole] * 5,
            scratch_shapes=[pltpu.VMEM((10, TILE, H), jnp.float32)],
        ),
        out_shape=[jax.ShapeDtypeStruct((ROWS, H), jnp.float32)] * 5,
        compiler_params=params(),
        cost_estimate=cost(n * 6 * 512 * 256 * 256, n << 20),
        name="gather_terms",
    )(ids, rows, high, low, *fields, *before)


def dense_kernel(own, from_a, from_b, weight, bias, cotangent, agg, output, grad_pre, grad_agg):
    total = own[...] + from_a[...] + from_b[...]
    agg[...] = total
    weight_high, weight_low = split(weight[...])
    value = dot3(*split(total), weight_high, weight_low) + bias[...]
    scale = 0.7978845608028654
    square = value * value
    turn = jnp.tanh(scale * (value + 0.044715 * (square * value)))
    half = 0.5 * (1.0 + turn)
    output[...] = value * half
    slope = half + 0.5 * value * (1.0 - turn * turn) * (scale * (1.0 + 3.0 * 0.044715 * square))
    grad = cotangent[...] * slope
    grad_pre[...] = grad
    turned_high, turned_low = split(weight[...].T)
    grad_agg[...] = dot3(*split(grad), turned_high, turned_low)


def dense(own, from_a, from_b, weight, bias, cotangent):
    return pl.pallas_call(
        dense_kernel,
        out_shape=[jax.ShapeDtypeStruct((ROWS, H), jnp.float32)] * 4,
        compiler_params=params(),
        cost_estimate=cost(12 * 256 * 256 * 256, 10 * 256 * 1024),
        name="dense",
    )(own, from_a, from_b, weight, bias.reshape(1, H), cotangent)


def weight_kernel(agg, grad_pre, weight_term, bias_term):
    weight_term[...] = dot3(*split(agg[...].T), *split(grad_pre[...]))
    bias_term[...] = jnp.sum(grad_pre[...], axis=0, keepdims=True)


def weight_terms(agg, grad_pre):
    return pl.pallas_call(
        weight_kernel,
        out_shape=[
            jax.ShapeDtypeStruct((H, H), jnp.float32),
            jax.ShapeDtypeStruct((1, H), jnp.float32),
        ],
        compiler_params=params(),
        cost_estimate=cost(6 * 256 * 256 * 256, 3 * 256 * 1024),
        name="weight_terms",
    )(agg, grad_pre)


def spread_kernel(ids, rows, high_t, low_t, own, a, b, y1, y2, out, band_high, band_low):
    step = pl.program_id(0)

    @pl.when(step == 0)
    def _():
        for j, ref in enumerate((own, a, b, y1, y2)):
            high, low = split(ref[...])
            band_high[2 * j : 2 * j + 2] = high.reshape(2, TILE, H)
            band_low[2 * j : 2 * j + 2] = low.reshape(2, TILE, H)

    first = ids[step] * PER_BLOCK
    places = [rows[first + slot] for slot in range(PER_BLOCK)]
    chosen_high = jnp.concatenate([band_high[place] for place in places], axis=0)
    chosen_low = jnp.concatenate([band_low[place] for place in places], axis=0)
    out[0] = dot3(high_t[0], low_t[0], chosen_high, chosen_low)


def spread_terms(ids, rows, high_t, low_t, band):
    n = ids.shape[0]
    whole = pl.BlockSpec((ROWS, H), lambda i, *_: (0, 0))
    tiles = pl.BlockSpec((1, ROWS, PER_BLOCK * TILE), lambda i, ids, rows: (ids[i], 0, 0))
    return pl.pallas_call(
        spread_kernel,
        grid_spec=pltpu.PrefetchScalarGridSpec(
            num_scalar_prefetch=2,
            grid=(n,),
            in_specs=[tiles, tiles] + [whole] * 5,
            out_specs=pl.BlockSpec((1, ROWS, H), lambda i, *_: (i, 0, 0)),
            scratch_shapes=[pltpu.VMEM((10, TILE, H), jnp.bfloat16)] * 2,
        ),
        out_shape=jax.ShapeDtypeStruct((n, ROWS, H), jnp.float32),
        compiler_params=params(),
        cost_estimate=cost(n * 6 * 512 * 256 * 256, n << 20),
        name="spread_terms",
    )(ids, rows, high_t, low_t, *band)


def other_core(value):
    return lax.ppermute(value, "core", [(0, 1), (1, 0)])


def along_loop(value, sign):
    pairs = []
    for z in range(Z_HI):
        for core in range(CORE):
            by = sign if core == 0 else -sign
            pairs.append((z * CORE + core, (z + by) % Z_HI * CORE + core))
    return lax.ppermute(value, LOOP, pairs)


def in_triple(value, by):
    return lax.ppermute(value, "z_lo", [(i, (i + by) % Z_LO) for i in range(Z_LO)])


def across_triples(value, by):
    pairs = [(r, (r + Z_LO * by[r % Z_LO]) % N_REP) for r in range(N_REP)]
    return lax.ppermute(value, REP, pairs)


def whole_sums(weight_term, bias_term):
    plane = ("x", "y")
    column = ("z_hi", "core", "z_lo")
    n_plane, n_column = X * Y, Z_HI * CORE * Z_LO
    rows = H // n_plane
    part = lax.all_to_all(weight_term.reshape(n_plane, rows, H), plane, 0, 0, tiled=True)
    part = jnp.sum(part, axis=0)
    part = jnp.concatenate([part, jnp.pad(bias_term.reshape(rows, H // rows), ((0, 0), (0, 128 - H // rows)))], axis=1)
    part = lax.all_to_all(
        jnp.broadcast_to(part[None], (n_column,) + part.shape), column, 0, 0, tiled=True
    )
    part = jnp.sum(part, axis=0)
    part = lax.all_to_all(jnp.broadcast_to(part[None], (n_plane,) + part.shape), plane, 0, 0, tiled=True)
    weight_whole = part[:, :, :H].reshape(H, H)
    bias_whole = jnp.sum(part[:, :, H : H + H // rows], axis=0).reshape(H)
    return weight_whole, bias_whole


def per_device(features, weight, bias, tile_values, tile_rows, tile_cols, tile_counts, cotangent):
    z_hi, core, z_lo = lax.axis_index("z_hi"), lax.axis_index("core"), lax.axis_index("z_lo")
    places = jnp.asarray(BAND_PLACE, jnp.int32)[z_lo]
    row_tiles = ROWS // TILE
    rows = jnp.take(places, tile_rows[0] // row_tiles) * row_tiles + tile_rows[0] % row_tiles
    cols = tile_cols[0]
    counts = tile_counts[0]

    turn = 1 - 2 * core
    first = (z_hi - turn) % Z_HI
    second = (z_hi + turn) % Z_HI
    far = (z_hi + 2) % Z_HI

    def block(z, c):
        return z * CORE + c

    field_first = along_loop(features, 1)
    field_second = along_loop(features, -1)
    field_other = other_core(features)
    high, low, high_t, low_t = place_tiles(tile_values[0], cols, counts)
    field_far = along_loop(field_first, 1)
    other_first = other_core(field_first)
    other_second = other_core(field_second)
    near_ids = jnp.stack(
        [
            block(z_hi, core),
            block(z_hi, 1 - core),
            block(first, core),
            block(second, 1 - core),
            block(second, core),
            block(first, 1 - core),
        ]
    )
    terms = gather_terms(
        near_ids,
        rows,
        high,
        low,
        (features, field_other, field_first, other_first, field_second, other_second),
    )
    other_far = other_core(field_far)
    far_ids = jnp.stack([block(far, core), block(far, 1 - core)])
    own, term_a, term_b, term_y1, term_y2 = gather_terms(
        far_ids, rows, high, low, (field_far, other_far), terms
    )

    got_y1 = across_triples(term_y1, (-1, -1, 1))
    got_y2 = across_triples(term_y2, (-1, 1, 1))
    got_a = in_triple(term_a + got_y1, 1)
    got_b = in_triple(term_b + got_y2, 2)
    agg, output, grad_pre, grad_agg = dense(own, got_a, got_b, weight, bias, cotangent)

    band_a = in_triple(grad_agg, -1)
    band_b = in_triple(grad_agg, -2)
    weight_term, bias_term = weight_terms(agg, grad_pre)
    band_y1 = across_triples(band_a, (1, 1, -1))
    band_y2 = across_triples(band_b, (1, -1, -1))
    band = (grad_agg, band_a, band_b, band_y1, band_y2)

    other_ids = jnp.stack(
        [block(far, 1 - core), block(second, 1 - core), block(first, 1 - core), block(z_hi, 1 - core)]
    )
    own_ids = jnp.stack([block(far, core), block(first, core), block(second, core), block(z_hi, core)])
    given = other_core(spread_terms(other_ids, rows, high_t, low_t, band))
    kept = spread_terms(own_ids, rows, high_t, low_t, band)
    got_far = along_loop(kept[0] + given[0], -1)
    got_second = along_loop(kept[2] + given[2], 1)
    got_first = along_loop(kept[1] + given[1] + got_far, -1)
    grad_features = kept[3] + given[3] + got_first + got_second

    weight_whole, bias_whole = whole_sums(weight_term, bias_term)
    return (output, grad_features, weight_whole / NODES, bias_whole / NODES)


def solution(mesh):
    cut = Mesh(mesh.devices.reshape(Z_HI, CORE, X, Y, Z_LO), AXES)
    nodes = P(AXES)
    return jax.shard_map(
        per_device,
        mesh=cut,
        in_specs=(nodes, P(), P(), nodes, nodes, nodes, nodes, nodes),
        out_specs=(nodes, nodes, P(), P()),
        check_vma=False,
    )
```

time: 674 us -> 220 us (0.33)
  the two profiles are of different devices: /device:TPU:92 before, /device:TPU:8 now
where the time goes in v1:
time: 220 us; the launch traced here: 218 us
  starting transfers between devices  115 us (52%)
  waiting for transfers between devices  54.6 us (25%)
  Pallas kernels  26.1 us (12%)
  local copies, waits for them, and re-layouts  10.7 us (5%)
  other arithmetic  10.5 us (5%)
    ppermute x6, starting transfers between devices, along_loop(): return lax.ppermute(value, LOOP, pairs)  48.1 us
    ppermute x4, starting transfers between devices, across_triples(): return lax.ppermute(value, REP, pairs)  18.3 us
    ppermute x6, waiting for transfers between devices, along_loop(): return lax.ppermute(value, LOOP, pairs)  18 us
    ppermute x4, waiting for transfers between devices, in_triple(): lax.ppermute(value, 'z_lo', [(i, (i + by) % Z_LO) for i in range(Z_LO)])  14.5 us
    ppermute x5, starting transfers between devices, other_core(): return lax.ppermute(value, 'core', [(0, 1), (1, 0)])  13.7 us
    all_to_all x1, waiting for transfers between devices, whole_sums(): lax.all_to_all(weight_term.reshape(n_plane, rows, H), plane, 0, 0, tiled=...  11.8 us
    ppermute x4, starting transfers between devices, in_triple(): lax.ppermute(value, 'z_lo', [(i, (i + by) % Z_LO) for i in range(Z_LO)])  11.7 us
    ppermute x4, waiting for transfers between devices, across_triples(): return lax.ppermute(value, REP, pairs)  10.3 us
  transfers between devices with their start and end apart: 22, of which 14 were waited for; matrix products, arithmetic and copies ran while one was open for 6% of the time, Pallas kernels for 8%

profile of v1, /device:TPU:8, one launch (start us, length us, event | category | flops | bytes accessed | tf_op | source)
XLA Modules:
  0.0 217.9 jit_solution(12835296557235058223)
XLA Ops:
  0.6 8.0 %collective-permute-start = (f32[256,256]{1,0:T(8,128)}, f32[256,256]{1,0:T(8,128)S(1)}, u32[]{:S(2)}, u32[]{:S(2)}) collective-permute-start(f32[256,256]{1,0:T(8,128)} %refs_0_.1), channel_id=1, source_target_pairs={{0,192},{96,672},{192,384},{288,96},{384,576},{480,288},{576,0},{6... | collective-permute-start | bytes 786440 | tf_op jit(solution)/shard_map/ppermute | solution.py:230
  8.7 8.6 %collective-permute-start.5 = (f32[256,256]{1,0:T(8,128)}, f32[256,256]{1,0:T(8,128)S(1)}, u32[]{:S(2)}, u32[]{:S(2)}) collective-permute-start(f32[256,256]{1,0:T(8,128)} %refs_0_.1), channel_id=1, source_target_pairs={{0,576},{96,288},{192,0},{288,480},{384,192},{480,672},{576,384},{... | collective-permute-start | bytes 786440 | tf_op jit(solution)/shard_map/ppermute | solution.py:230
  17.3 2.8 %collective-permute-done.refs_2_ = f32[256,256]{1,0:T(8,128)S(1)} collective-permute-done((f32[256,256]{1,0:T(8,128)}, f32[256,256]{1,0:T(8,128)S(1)}, u32[]{:S(2)}, u32[]{:S(2)}) %collective-permute-start) | collective-permute-done | bytes 262176 | tf_op jit(solution)/shard_map/ppermute | solution.py:230
  20.1 14.7 %collective-permute-start.1 = (f32[256,256]{1,0:T(8,128)S(1)}, f32[256,256]{1,0:T(8,128)S(1)}, u32[]{:S(2)}, u32[]{:S(2)}) collective-permute-start(f32[256,256]{1,0:T(8,128)S(1)} %collective-permute-done.refs_2_), channel_id=1, source_target_pairs={{0,192},{96,672},{192,384},{288,96},{384,576},{480,288},{576,0},{6... | collective-permute-start | bytes 786440 | tf_op jit(solution)/shard_map/ppermute | solution.py:230
  34.8 5.6 %collective-permute-start.3 = (f32[256,256]{1,0:T(8,128)}, f32[256,256]{1,0:T(8,128)S(1)}, u32[]{:S(2)}, u32[]{:S(2)}) collective-permute-start(f32[256,256]{1,0:T(8,128)} %refs_0_.1), channel_id=1, source_target_pairs={{0,96},{96,0},{1,97},{97,1},{2,98},{98,2},{3,99},{99,3},{4,100},{1... | collective-permute-start | bytes 786440 | tf_op jit(solution)/shard_map/ppermute | solution.py:221
  40.4 0.7 constant_dynamic-slice_fusion
  41.1 0.7 fusion.10
  41.8 1.9 collective-permute-start.4
  43.7 2.4 %collective-permute-start.6 = (f32[256,256]{1,0:T(8,128)S(1)}, f32[256,256]{1,0:T(8,128)}, u32[]{:S(2)}, u32[]{:S(2)}) collective-permute-start(f32[256,256]{1,0:T(8,128)S(1)} %collective-permute-done.5.refs_4_), channel_id=1, source_target_pairs={{0,96},{96,0},{1,97},{97,1},{2,98},{98,2},{3,99},{99,3},{4,100},{1... | collective-permute-start | bytes 786440 | tf_op jit(solution)/shard_map/ppermute | solution.py:221
  46.1 0.9 collective-permute-done.1.refs_0_
  47.0 1.9 collective-permute-start.2
  48.9 3.9 %fusion.8.rows = s32[32]{0:T(128)S(1)} fusion(s32[1,32]{1,0:T(1,128)} %param.13, s32[]{:T(128)} %bitcast.4, s32[]{:T(128)} %bitcast.5, s32[]{:T(128)} %bitcast.6, s32[]{:T(128)} %bitcast.8, s32[]{:T(128)} %bitcast.7), kind=kLoop, calls=%fused_computation.33 | loop fusion | flops 1728 | bytes 276 | tf_op jit(solution)/shard_map/add | solution.py:264
  52.9 0.6 copy-done.14
  53.6 0.7 copy-done.15
  54.2 7.2 %place_tiles.1 = (bf16[8,512,256]{2,1,0:T(8,128)(2,1)S(1)}, bf16[8,512,256]{2,1,0:T(8,128)(2,1)S(1)}, bf16[8,256,512]{2,1,0:T(8,128)(2,1)}, bf16[8,256,512]{2,1,0:T(8,128)(2,1)}) custom-call(s32[32]{0:T(128)S(1)} %bitcast.66, s32[8]{0:T(128)S(1)} %bitcast.67, f32[32,128,128]{2,1,0:T(8,128)} %bitcast.68), custom_call_target="tpu_custom_call" | custom-call | bytes 10485760 | tf_op jit(solution)/shard_map/place_tiles/pallas_call | solution.py:73
  61.4 1.4 copy-done
  62.8 0.1 stack.53.ids
  63.0 5.4 %gather_terms.2 = (f32[256,256]{1,0:T(8,128)S(1)}, f32[256,256]{1,0:T(8,128)S(1)}, f32[256,256]{1,0:T(8,128)S(1)}, f32[256,256]{1,0:T(8,128)S(1)}, f32[256,256]{1,0:T(8,128)S(1)}) custom-call(s32[6]{0:T(128)S(1)} %stack.53.ids, s32[32]{0:T(128)S(1)} %fusion.8.rows, bf16[8,512,256]{2,1,0:T(8,128)(2,1)S(1)} %get-tuple-element.24.high, ...), custom_call_target="tpu_custom_call" | custom-call | flops 1207959552 | bytes 6291456 | tf_op jit(solution)/shard_map/gather_terms/pallas_call | solution.py:122
  68.4 2.5 %gather_terms.3 = (f32[256,256]{1,0:T(8,128)S(1)}, f32[256,256]{1,0:T(8,128)S(1)}, f32[256,256]{1,0:T(8,128)S(1)}, f32[256,256]{1,0:T(8,128)S(1)}, f32[256,256]{1,0:T(8,128)S(1)}) custom-call(s32[2]{0:T(128)S(1)} %pad_add_fusion.ids, s32[32]{0:T(128)S(1)} %fusion.8.rows, bf16[8,512,256]{2,1,0:T(8,128)(2,1)S(1)} %get-tuple-element.24.high, ...), custom_call_target="tpu_custom_call" | custom-call | flops 402653184 | bytes 2097152 | tf_op jit(solution)/shard_map/gather_terms/pallas_call | solution.py:122
  71.0 2.1 collective-permute-start.7
  73.0 8.0 %collective-permute-start.9 = (f32[256,256]{1,0:T(8,128)S(1)}, f32[256,256]{1,0:T(8,128)S(1)}, u32[]{:S(2)}, u32[]{:S(2)}) collective-permute-start(f32[256,256]{1,0:T(8,128)S(1)} %get-tuple-element.35), channel_id=1, source_target_pairs={{0,93},{1,4},{2,5},{3,0},{4,7},{5,8},{6,3},{7,10},{8,11},{9,6},{10... | collective-permute-start | bytes 786440 | tf_op jit(solution)/shard_map/ppermute | solution.py:239
  81.0 1.0 collective-permute-done.7
  82.1 3.1 %collective-permute-start.8 = (f32[256,256]{1,0:T(8,128)S(1)}, f32[256,256]{1,0:T(8,128)S(1)}, u32[]{:S(2)}, u32[]{:S(2)}) collective-permute-start(f32[256,256]{1,0:T(8,128)S(1)} %add.152), channel_id=1, source_target_pairs={{0,1},{1,2},{2,0},{3,4},{4,5},{5,3},{6,7},{7,8},{8,6},{9,10},{10,1... | collective-permute-start | bytes 786440 | tf_op jit(solution)/shard_map/ppermute | solution.py:234
  85.2 2.1 collective-permute-done.9
  87.4 1.9 collective-permute-start.10
  89.3 3.2 %collective-permute-done.8.from_a = f32[256,256]{1,0:T(8,128)S(1)} collective-permute-done((f32[256,256]{1,0:T(8,128)S(1)}, f32[256,256]{1,0:T(8,128)S(1)}, u32[]{:S(2)}, u32[]{:S(2)}) %collective-permute-start.8) | collective-permute-done | bytes 262176 | tf_op jit(solution)/shard_map/ppermute | solution.py:234
  92.5 5.5 %collective-permute-done.10.from_b = f32[256,256]{1,0:T(8,128)S(1)} collective-permute-done((f32[256,256]{1,0:T(8,128)S(1)}, f32[256,256]{1,0:T(8,128)S(1)}, u32[]{:S(2)}, u32[]{:S(2)}) %collective-permute-start.10) | collective-permute-done | bytes 262176 | tf_op jit(solution)/shard_map/ppermute | solution.py:234
  98.1 1.2 dense.1
  99.3 2.9 %collective-permute-start.12 = (f32[256,256]{1,0:T(8,128)S(1)}, f32[256,256]{1,0:T(8,128)S(1)}, u32[]{:S(2)}, u32[]{:S(2)}) collective-permute-start(f32[256,256]{1,0:T(8,128)S(1)} %get-tuple-element.39.own), channel_id=1, source_target_pairs={{0,1},{1,2},{2,0},{3,4},{4,5},{5,3},{6,7},{7,8},{8,6},{9,10},{10,1... | collective-permute-start | bytes 786440 | tf_op jit(solution)/shard_map/ppermute | solution.py:234
  102.3 3.8 %collective-permute-start.11 = (f32[256,256]{1,0:T(8,128)S(1)}, f32[256,256]{1,0:T(8,128)S(1)}, u32[]{:S(2)}, u32[]{:S(2)}) collective-permute-start(f32[256,256]{1,0:T(8,128)S(1)} %get-tuple-element.39.own), channel_id=1, source_target_pairs={{0,2},{1,0},{2,1},{3,5},{4,3},{5,4},{6,8},{7,6},{8,7},{9,11},{10,9... | collective-permute-start | bytes 786440 | tf_op jit(solution)/shard_map/ppermute | solution.py:234
  106.1 5.3 %collective-permute-done.12.b = f32[256,256]{1,0:T(8,128)S(1)} collective-permute-done((f32[256,256]{1,0:T(8,128)S(1)}, f32[256,256]{1,0:T(8,128)S(1)}, u32[]{:S(2)}, u32[]{:S(2)}) %collective-permute-start.12) | collective-permute-done | bytes 262176 | tf_op jit(solution)/shard_map/ppermute | solution.py:234
  111.4 3.9 %collective-permute-start.14 = (f32[256,256]{1,0:T(8,128)S(1)}, f32[256,256]{1,0:T(8,128)S(1)}, u32[]{:S(2)}, u32[]{:S(2)}) collective-permute-start(f32[256,256]{1,0:T(8,128)S(1)} %collective-permute-done.12.b), channel_id=1, source_target_pairs={{0,3},{1,94},{2,95},{3,6},{4,1},{5,2},{6,9},{7,4},{8,5},{9,12},{10... | collective-permute-start | bytes 786440 | tf_op jit(solution)/shard_map/ppermute | solution.py:239
  115.3 0.4 collective-permute-done.11.a
  115.7 4.3 %collective-permute-start.13 = (f32[256,256]{1,0:T(8,128)S(1)}, f32[256,256]{1,0:T(8,128)S(1)}, u32[]{:S(2)}, u32[]{:S(2)}) collective-permute-start(f32[256,256]{1,0:T(8,128)S(1)} %collective-permute-done.11.a), channel_id=1, source_target_pairs={{0,3},{1,4},{2,95},{3,6},{4,7},{5,2},{6,9},{7,10},{8,5},{9,12},{10... | collective-permute-start | bytes 786440 | tf_op jit(solution)/shard_map/ppermute | solution.py:239
  120.1 2.4 %collective-permute-done.14.y2 = f32[256,256]{1,0:T(8,128)S(1)} collective-permute-done((f32[256,256]{1,0:T(8,128)S(1)}, f32[256,256]{1,0:T(8,128)S(1)}, u32[]{:S(2)}, u32[]{:S(2)}) %collective-permute-start.14) | collective-permute-done | bytes 262176 | tf_op jit(solution)/shard_map/ppermute | solution.py:239
  122.4 4.8 %collective-permute-done.13.y1 = f32[256,256]{1,0:T(8,128)S(1)} collective-permute-done((f32[256,256]{1,0:T(8,128)S(1)}, f32[256,256]{1,0:T(8,128)S(1)}, u32[]{:S(2)}, u32[]{:S(2)}) %collective-permute-start.13) | collective-permute-done | bytes 262176 | tf_op jit(solution)/shard_map/ppermute | solution.py:239
  127.3 4.9 %spread_terms.3 = f32[4,256,256]{2,1,0:T(8,128)} custom-call(s32[4]{0:T(128)S(1)} %pad_add_fusion.2.ids, s32[32]{0:T(128)S(1)} %fusion.8.rows, bf16[8,256,512]{2,1,0:T(8,128)(2,1)S(1)} %copy-done.1, bf16[8,256,512]{2,1,0:T(8,128)(2,1)} %get-tuple-element.38.low_t, f32[256,256]{1,0:T(8,128)S(1)} %get-tuple-element.39.own, ...), custom_call_target="tpu_custom_call" | custom-call | flops 805306368 | bytes 4194304 | tf_op jit(solution)/shard_map/spread_terms/pallas_call | solution.py:204
  132.1 1.9 collective-permute-start.15
  134.1 1.0 weight_terms.1
  135.1 10.0 %all-to-all-start = ((f32[32,8,256]{2,1,0:T(8,128)}), f32[32,8,256]{2,1,0:T(8,128)S(1)}, u32[]{:S(2)}, u32[]{:S(2)}) async-start(f32[32,8,256]{2,1,0:T(8,128)} %bitcast.24), calls=%async_computation | async-start | bytes 524288 | tf_op jit(solution)/shard_map/all_to_all | solution.py:247
  145.2 0.5 broadcast.166
  145.7 0.7 reduce.3
  146.4 11.8 %all-to-all-done = f32[32,8,256]{2,1,0:T(8,128)S(1)} async-done(((f32[32,8,256]{2,1,0:T(8,128)}), f32[32,8,256]{2,1,0:T(8,128)S(1)}, u32[]{:S(2)}, u32[]{:S(2)}) %all-to-all-start) | async-done | bytes 262176 | tf_op jit(solution)/shard_map/all_to_all | solution.py:247
  158.3 0.7 broadcast_in_dim.11
  159.0 8.5 %all-to-all-start.1 = ((f32[24,8,384]{2,1,0:T(8,128)}), f32[24,8,384]{2,1,0:T(8,128)}, u32[]{:S(2)}, u32[]{:S(2)}) async-start(f32[24,8,384]{2,1,0:T(8,128)} %broadcast_in_dim.11), calls=%async_computation.1 | async-start | bytes 589824 | tf_op jit(solution)/shard_map/all_to_all | solution.py:250
  167.6 0.9 copy-done.3
  168.5 0.9 copy-done.5
  169.5 0.9 copy-done.7
  170.4 0.9 copy-done.9
  171.4 3.9 %spread_terms.2 = f32[4,256,256]{2,1,0:T(8,128)S(1)} custom-call(s32[4]{0:T(128)S(1)} %pad_add_fusion.1.ids, s32[32]{0:T(128)S(1)} %fusion.8.rows, bf16[8,256,512]{2,1,0:T(8,128)(2,1)S(1)} %copy-done.1, bf16[8,256,512]{2,1,0:T(8,128)(2,1)} %get-tuple-element.38.low_t, f32[256,256]{1,0:T(8,128)S(1)} %get-tuple-element.39.own, f32[256,256]{1,0:T(8,128)S(1)} %copy-done.5, ...), custom_call_target="tpu_custom_call" | custom-call | flops 805306368 | bytes 4194304 | tf_op jit(solution)/shard_map/spread_terms/pallas_call | solution.py:204
  175.3 1.1 fusion.2
  176.4 6.7 %collective-permute-start.16 = (f32[256,256]{1,0:T(8,128)S(1)}, f32[256,256]{1,0:T(8,128)S(1)}, u32[]{:S(2)}, u32[]{:S(2)}) collective-permute-start(f32[256,256]{1,0:T(8,128)S(1)} %get-tuple-element.44), channel_id=1, source_target_pairs={{0,576},{96,288},{192,0},{288,480},{384,192},{480,672},{576,384},{... | collective-permute-start | bytes 786440 | tf_op jit(solution)/shard_map/ppermute | solution.py:230
  183.1 1.0 reduce_sum.28
  184.1 0.8 broadcast_in_dim.20
  184.9 4.6 %all-to-all-start.2 = ((f32[32,8,384]{2,1,0:T(8,128)}), f32[32,8,384]{2,1,0:T(8,128)S(1)}, u32[]{:S(2)}, u32[]{:S(2)}) async-start(f32[32,8,384]{2,1,0:T(8,128)} %broadcast_in_dim.20), calls=%async_computation.2 | async-start | bytes 786432 | tf_op jit(solution)/shard_map/all_to_all | solution.py:254
  189.5 2.5 %collective-permute-start.18 = (f32[256,256]{1,0:T(8,128)S(1)}, f32[256,256]{1,0:T(8,128)S(1)}, u32[]{:S(2)}, u32[]{:S(2)}) collective-permute-start(f32[256,256]{1,0:T(8,128)S(1)} %get-tuple-element.45), channel_id=1, source_target_pairs={{0,192},{96,672},{192,384},{288,96},{384,576},{480,288},{576,0},{6... | collective-permute-start | bytes 786440 | tf_op jit(solution)/shard_map/ppermute | solution.py:230
  192.0 0.6 collective-permute-done.16
  192.6 1.0 fusion.4
  193.6 7.5 %collective-permute-start.17 = (f32[256,256]{1,0:T(8,128)S(1)}, f32[256,256]{1,0:T(8,128)S(1)}, u32[]{:S(2)}, u32[]{:S(2)}) collective-permute-start(f32[256,256]{1,0:T(8,128)S(1)} %fusion.4), channel_id=1, source_target_pairs={{0,576},{96,288},{192,0},{288,480},{384,192},{480,672},{576,384},{... | collective-permute-start | bytes 786440 | tf_op jit(solution)/shard_map/ppermute | solution.py:230
  201.1 8.5 %collective-permute-done.18 = f32[256,256]{1,0:T(8,128)S(1)} collective-permute-done((f32[256,256]{1,0:T(8,128)S(1)}, f32[256,256]{1,0:T(8,128)S(1)}, u32[]{:S(2)}, u32[]{:S(2)}) %collective-permute-start.18) | collective-permute-done | bytes 262176 | tf_op jit(solution)/shard_map/ppermute | solution.py:230
  209.6 5.2 %collective-permute-done.17 = f32[256,256]{1,0:T(8,128)S(1)} collective-permute-done((f32[256,256]{1,0:T(8,128)S(1)}, f32[256,256]{1,0:T(8,128)S(1)}, u32[]{:S(2)}, u32[]{:S(2)}) %collective-permute-start.17) | collective-permute-done | bytes 262176 | tf_op jit(solution)/shard_map/ppermute | solution.py:230
  214.8 1.7 fusion.7
  216.6 0.6 div.43
  217.2 0.7 fusion
  (43 shorter events, 0.5 us)
Async XLA Ops:
  0.6 62.4 %copy-start.10 = (f32[256,256]{1,0:T(8,128)S(1)}, f32[256,256]{1,0:T(8,128)}, u32[]{:S(2)}) copy-start(f32[256,256]{1,0:T(8,128)} %refs_0_.1) | copy-start | bytes 786436
  0.6 19.4 %collective-permute-start = (f32[256,256]{1,0:T(8,128)}, f32[256,256]{1,0:T(8,128)S(1)}, u32[]{:S(2)}, u32[]{:S(2)}) collective-permute-start(f32[256,256]{1,0:T(8,128)} %refs_0_.1), channel_id=1, source_target_pairs={{0,192},{96,672},{192,384},{288,96},{384,576},{480,288},{576,0},{6... | collective-permute-start | bytes 786440 | tf_op jit(solution)/shard_map/ppermute | solution.py:230
  8.7 35.0 %collective-permute-start.5 = (f32[256,256]{1,0:T(8,128)}, f32[256,256]{1,0:T(8,128)S(1)}, u32[]{:S(2)}, u32[]{:S(2)}) collective-permute-start(f32[256,256]{1,0:T(8,128)} %refs_0_.1), channel_id=1, source_target_pairs={{0,576},{96,288},{192,0},{288,480},{384,192},{480,672},{576,384},{... | collective-permute-start | bytes 786440 | tf_op jit(solution)/shard_map/ppermute | solution.py:230
  20.1 26.9 %collective-permute-start.1 = (f32[256,256]{1,0:T(8,128)S(1)}, f32[256,256]{1,0:T(8,128)S(1)}, u32[]{:S(2)}, u32[]{:S(2)}) collective-permute-start(f32[256,256]{1,0:T(8,128)S(1)} %collective-permute-done.refs_2_), channel_id=1, source_target_pairs={{0,192},{96,672},{192,384},{288,96},{384,576},{480,288},{576,0},{6... | collective-permute-start | bytes 786440 | tf_op jit(solution)/shard_map/ppermute | solution.py:230
  34.8 28.1 %collective-permute-start.3 = (f32[256,256]{1,0:T(8,128)}, f32[256,256]{1,0:T(8,128)S(1)}, u32[]{:S(2)}, u32[]{:S(2)}) collective-permute-start(f32[256,256]{1,0:T(8,128)} %refs_0_.1), channel_id=1, source_target_pairs={{0,96},{96,0},{1,97},{97,1},{2,98},{98,2},{3,99},{99,3},{4,100},{1... | collective-permute-start | bytes 786440 | tf_op jit(solution)/shard_map/ppermute | solution.py:221
  41.8 21.2 %collective-permute-start.4 = (f32[256,256]{1,0:T(8,128)S(1)}, f32[256,256]{1,0:T(8,128)}, u32[]{:S(2)}, u32[]{:S(2)}) collective-permute-start(f32[256,256]{1,0:T(8,128)S(1)} %collective-permute-done.refs_2_), channel_id=1, source_target_pairs={{0,96},{96,0},{1,97},{97,1},{2,98},{98,2},{3,99},{99,3},{4,100},{1... | collective-permute-start | bytes 786440 | tf_op jit(solution)/shard_map/ppermute | solution.py:221
  43.7 19.3 %collective-permute-start.6 = (f32[256,256]{1,0:T(8,128)S(1)}, f32[256,256]{1,0:T(8,128)}, u32[]{:S(2)}, u32[]{:S(2)}) collective-permute-start(f32[256,256]{1,0:T(8,128)S(1)} %collective-permute-done.5.refs_4_), channel_id=1, source_target_pairs={{0,96},{96,0},{1,97},{97,1},{2,98},{98,2},{3,99},{99,3},{4,100},{1... | collective-permute-start | bytes 786440 | tf_op jit(solution)/shard_map/ppermute | solution.py:221
  47.0 21.4 %collective-permute-start.2 = (f32[256,256]{1,0:T(8,128)S(1)}, f32[256,256]{1,0:T(8,128)}, u32[]{:S(2)}, u32[]{:S(2)}) collective-permute-start(f32[256,256]{1,0:T(8,128)S(1)} %collective-permute-done.1.refs_0_), channel_id=1, source_target_pairs={{0,96},{96,0},{1,97},{97,1},{2,98},{98,2},{3,99},{99,3},{4,100},{1... | collective-permute-start | bytes 786440 | tf_op jit(solution)/shard_map/ppermute | solution.py:221
  52.9 0.7 copy-start.14
  53.6 0.7 copy-start.15
  61.4 1.4 copy-start
  68.4 29.7 %copy-start.11 = (f32[256,256]{1,0:T(8,128)S(1)}, f32[256,256]{1,0:T(8,128)}, u32[]{:S(2)}) copy-start(f32[256,256]{1,0:T(8,128)} %weight.1) | copy-start | bytes 786436
  68.4 29.7 %copy-start.12 = (f32[256,256]{1,0:T(8,128)S(1)}, f32[256,256]{1,0:T(8,128)}, u32[]{:S(2)}) copy-start(f32[256,256]{1,0:T(8,128)} %cotangent.1) | copy-start | bytes 786436
  68.4 29.7 %copy-start.13 = (f32[256]{0:T(256)S(1)}, f32[256]{0:T(256)}, u32[]{:S(2)}) copy-start(f32[256]{0:T(256)} %param.11) | copy-start | bytes 3076
  71.0 56.3 %copy-start.1 = (bf16[8,256,512]{2,1,0:T(8,128)(2,1)S(1)}, bf16[8,256,512]{2,1,0:T(8,128)(2,1)}, u32[]{:S(2)}) copy-start(bf16[8,256,512]{2,1,0:T(8,128)(2,1)} %get-tuple-element.37.high_t) | copy-start | bytes 6291460
  71.0 11.1 %collective-permute-start.7 = (f32[256,256]{1,0:T(8,128)S(1)}, f32[256,256]{1,0:T(8,128)S(1)}, u32[]{:S(2)}, u32[]{:S(2)}) collective-permute-start(f32[256,256]{1,0:T(8,128)S(1)} %get-tuple-element.33), channel_id=1, source_target_pairs={{0,93},{1,94},{2,5},{3,0},{4,1},{5,8},{6,3},{7,4},{8,11},{9,6},{10... | collective-permute-start | bytes 786440 | tf_op jit(solution)/shard_map/ppermute | solution.py:239
  73.0 14.3 %collective-permute-start.9 = (f32[256,256]{1,0:T(8,128)S(1)}, f32[256,256]{1,0:T(8,128)S(1)}, u32[]{:S(2)}, u32[]{:S(2)}) collective-permute-start(f32[256,256]{1,0:T(8,128)S(1)} %get-tuple-element.35), channel_id=1, source_target_pairs={{0,93},{1,4},{2,5},{3,0},{4,7},{5,8},{6,3},{7,10},{8,11},{9,6},{10... | collective-permute-start | bytes 786440 | tf_op jit(solution)/shard_map/ppermute | solution.py:239
  82.1 10.4 %collective-permute-start.8 = (f32[256,256]{1,0:T(8,128)S(1)}, f32[256,256]{1,0:T(8,128)S(1)}, u32[]{:S(2)}, u32[]{:S(2)}) collective-permute-start(f32[256,256]{1,0:T(8,128)S(1)} %add.152), channel_id=1, source_target_pairs={{0,1},{1,2},{2,0},{3,4},{4,5},{5,3},{6,7},{7,8},{8,6},{9,10},{10,1... | collective-permute-start | bytes 786440 | tf_op jit(solution)/shard_map/ppermute | solution.py:234
  87.4 10.7 %collective-permute-start.10 = (f32[256,256]{1,0:T(8,128)S(1)}, f32[256,256]{1,0:T(8,128)S(1)}, u32[]{:S(2)}, u32[]{:S(2)}) collective-permute-start(f32[256,256]{1,0:T(8,128)S(1)} %add.153), channel_id=1, source_target_pairs={{0,2},{1,0},{2,1},{3,5},{4,3},{5,4},{6,8},{7,6},{8,7},{9,11},{10,9... | collective-permute-start | bytes 786440 | tf_op jit(solution)/shard_map/ppermute | solution.py:234
  99.3 12.0 %collective-permute-start.12 = (f32[256,256]{1,0:T(8,128)S(1)}, f32[256,256]{1,0:T(8,128)S(1)}, u32[]{:S(2)}, u32[]{:S(2)}) collective-permute-start(f32[256,256]{1,0:T(8,128)S(1)} %get-tuple-element.39.own), channel_id=1, source_target_pairs={{0,1},{1,2},{2,0},{3,4},{4,5},{5,3},{6,7},{7,8},{8,6},{9,10},{10,1... | collective-permute-start | bytes 786440 | tf_op jit(solution)/shard_map/ppermute | solution.py:234
  102.3 13.4 %collective-permute-start.11 = (f32[256,256]{1,0:T(8,128)S(1)}, f32[256,256]{1,0:T(8,128)S(1)}, u32[]{:S(2)}, u32[]{:S(2)}) collective-permute-start(f32[256,256]{1,0:T(8,128)S(1)} %get-tuple-element.39.own), channel_id=1, source_target_pairs={{0,2},{1,0},{2,1},{3,5},{4,3},{5,4},{6,8},{7,6},{8,7},{9,11},{10,9... | collective-permute-start | bytes 786440 | tf_op jit(solution)/shard_map/ppermute | solution.py:234
  111.4 20.8 %copy-start.2 = (f32[256,256]{1,0:T(8,128)}, f32[256,256]{1,0:T(8,128)S(1)}, u32[]{:S(2)}) copy-start(f32[256,256]{1,0:T(8,128)S(1)} %collective-permute-done.12.b) | copy-start | bytes 786436
  111.4 11.1 %collective-permute-start.14 = (f32[256,256]{1,0:T(8,128)S(1)}, f32[256,256]{1,0:T(8,128)S(1)}, u32[]{:S(2)}, u32[]{:S(2)}) collective-permute-start(f32[256,256]{1,0:T(8,128)S(1)} %collective-permute-done.12.b), channel_id=1, source_target_pairs={{0,3},{1,94},{2,95},{3,6},{4,1},{5,2},{6,9},{7,4},{8,5},{9,12},{10... | collective-permute-start | bytes 786440 | tf_op jit(solution)/shard_map/ppermute | solution.py:239
  115.7 16.4 %copy-start.4 = (f32[256,256]{1,0:T(8,128)}, f32[256,256]{1,0:T(8,128)S(1)}, u32[]{:S(2)}) copy-start(f32[256,256]{1,0:T(8,128)S(1)} %collective-permute-done.11.a) | copy-start | bytes 786436
  115.7 11.6 %collective-permute-start.13 = (f32[256,256]{1,0:T(8,128)S(1)}, f32[256,256]{1,0:T(8,128)S(1)}, u32[]{:S(2)}, u32[]{:S(2)}) collective-permute-start(f32[256,256]{1,0:T(8,128)S(1)} %collective-permute-done.11.a), channel_id=1, source_target_pairs={{0,3},{1,4},{2,95},{3,6},{4,7},{5,2},{6,9},{7,10},{8,5},{9,12},{10... | collective-permute-start | bytes 786440 | tf_op jit(solution)/shard_map/ppermute | solution.py:239
  122.4 9.7 %copy-start.6 = (f32[256,256]{1,0:T(8,128)}, f32[256,256]{1,0:T(8,128)S(1)}, u32[]{:S(2)}) copy-start(f32[256,256]{1,0:T(8,128)S(1)} %collective-permute-done.14.y2) | copy-start | bytes 786436
  127.3 4.9 %copy-start.8 = (f32[256,256]{1,0:T(8,128)}, f32[256,256]{1,0:T(8,128)S(1)}, u32[]{:S(2)}) copy-start(f32[256,256]{1,0:T(8,128)S(1)} %collective-permute-done.13.y1) | copy-start | bytes 786436
  132.1 43.1 %collective-permute-start.15 = (f32[4,256,256]{2,1,0:T(8,128)}, f32[4,256,256]{2,1,0:T(8,128)}, u32[]{:S(2)}, u32[]{:S(2)}) collective-permute-start(f32[4,256,256]{2,1,0:T(8,128)} %spread_terms.3), channel_id=1, source_target_pairs={{0,96},{96,0},{1,97},{97,1},{2,98},{98,2},{3,99},{99,3},{4,100},{1... | collective-permute-start | bytes 3145736 | tf_op jit(solution)/shard_map/ppermute | solution.py:221
  135.1 23.1 %all-to-all-start = ((f32[32,8,256]{2,1,0:T(8,128)}), f32[32,8,256]{2,1,0:T(8,128)S(1)}, u32[]{:S(2)}, u32[]{:S(2)}) async-start(f32[32,8,256]{2,1,0:T(8,128)} %bitcast.24), calls=%async_computation | async-start | bytes 524288 | tf_op jit(solution)/shard_map/all_to_all | solution.py:247
  159.0 24.1 %all-to-all-start.1 = ((f32[24,8,384]{2,1,0:T(8,128)}), f32[24,8,384]{2,1,0:T(8,128)}, u32[]{:S(2)}, u32[]{:S(2)}) async-start(f32[24,8,384]{2,1,0:T(8,128)} %broadcast_in_dim.11), calls=%async_computation.1 | async-start | bytes 589824 | tf_op jit(solution)/shard_map/all_to_all | solution.py:250
  167.6 1.0 copy-start.3
  168.5 0.9 copy-start.5
  169.5 0.9 copy-start.7
  170.4 0.9 copy-start.9
  176.4 16.2 %collective-permute-start.16 = (f32[256,256]{1,0:T(8,128)S(1)}, f32[256,256]{1,0:T(8,128)S(1)}, u32[]{:S(2)}, u32[]{:S(2)}) collective-permute-start(f32[256,256]{1,0:T(8,128)S(1)} %get-tuple-element.44), channel_id=1, source_target_pairs={{0,576},{96,288},{192,0},{288,480},{384,192},{480,672},{576,384},{... | collective-permute-start | bytes 786440 | tf_op jit(solution)/shard_map/ppermute | solution.py:230
  184.9 31.7 %all-to-all-start.2 = ((f32[32,8,384]{2,1,0:T(8,128)}), f32[32,8,384]{2,1,0:T(8,128)S(1)}, u32[]{:S(2)}, u32[]{:S(2)}) async-start(f32[32,8,384]{2,1,0:T(8,128)} %broadcast_in_dim.20), calls=%async_computation.2 | async-start | bytes 786432 | tf_op jit(solution)/shard_map/all_to_all | solution.py:254
  189.5 20.1 %collective-permute-start.18 = (f32[256,256]{1,0:T(8,128)S(1)}, f32[256,256]{1,0:T(8,128)S(1)}, u32[]{:S(2)}, u32[]{:S(2)}) collective-permute-start(f32[256,256]{1,0:T(8,128)S(1)} %get-tuple-element.45), channel_id=1, source_target_pairs={{0,192},{96,672},{192,384},{288,96},{384,576},{480,288},{576,0},{6... | collective-permute-start | bytes 786440 | tf_op jit(solution)/shard_map/ppermute | solution.py:230
  193.6 21.2 %collective-permute-start.17 = (f32[256,256]{1,0:T(8,128)S(1)}, f32[256,256]{1,0:T(8,128)S(1)}, u32[]{:S(2)}, u32[]{:S(2)}) collective-permute-start(f32[256,256]{1,0:T(8,128)S(1)} %fusion.4), channel_id=1, source_target_pairs={{0,576},{96,288},{192,0},{288,480},{384,192},{480,672},{576,384},{... | collective-permute-start | bytes 786440 | tf_op jit(solution)/shard_map/ppermute | solution.py:230

commit v2 on v1

v2 whole, which is shorter than its diff:
```python
import functools

import jax
import jax.numpy as jnp
from jax import lax
from jax.experimental import pallas as pl
from jax.experimental.pallas import tpu as pltpu
from jax.sharding import Mesh
from jax.sharding import PartitionSpec as P

Z_HI, CORE, X, Y, Z_LO = 4, 2, 4, 8, 3
AXES = ("z_hi", "core", "x", "y", "z_lo")
LOOP = ("z_hi", "core")
REP = ("x", "y", "z_lo")
N_REP = X * Y * Z_LO
COLUMN_BLOCKS = Z_HI * CORE
PER_BLOCK = 4
TILE = 128
ROWS = 256
H = 256
NODES = 196608
PLANE = ("x", "y")
COLUMN = ("z_hi", "core", "z_lo")
N_PLANE = X * Y
N_COLUMN = Z_HI * CORE * Z_LO
PART = 256 // N_PLANE
VMEM_LIMIT = 16 * 1024 * 1024

BAND_PLACE = ((3, 4, 0, 1, 2), (3, 2, 0, 1, 4), (1, 2, 0, 3, 4))


def split(value):
    high = value.astype(jnp.bfloat16)
    low = (value - high.astype(jnp.float32)).astype(jnp.bfloat16)
    return high, low


def dot(left, right):
    return jnp.dot(left, right, preferred_element_type=jnp.float32)


def dot3(left_high, left_low, right_high, right_low):
    return dot(left_high, right_high) + (dot(left_low, right_high) + dot(left_high, right_low))


def in_hbm(value):
    return pltpu.with_memory_space_constraint(value, pltpu.HBM)


def params():
    return pltpu.CompilerParams(vmem_limit_bytes=VMEM_LIMIT)


LONG = pl.CostEstimate(flops=1 << 40, bytes_accessed=1 << 32, transcendentals=1 << 30)
SHORT = pl.CostEstimate(flops=1 << 10, bytes_accessed=1 << 10, transcendentals=0)


def cost(flops, size):
    return pl.CostEstimate(flops=flops, bytes_accessed=size, transcendentals=0)


def place_kernel(info, tiles, high, low):
    block = pl.program_id(0)
    for slot in range(PER_BLOCK):
        column, live = column_and_live(info, block, slot)
        tile = jnp.where(live, tiles[slot], 0.0).T
        span = pl.ds(slot * TILE, TILE)
        for half in range(ROWS // TILE):
            half_span = pl.ds(half * TILE, TILE)
            high[0, half_span, span], low[0, half_span, span] = split(jnp.where(column == half, tile, 0.0))


def place_tiles(info, tiles):
    shape = (ROWS, PER_BLOCK * TILE)
    spec = pl.BlockSpec((1,) + shape, lambda i, *_: (i, 0, 0))
    return pl.pallas_call(
        place_kernel,
        grid_spec=pltpu.PrefetchScalarGridSpec(
            num_scalar_prefetch=1,
            grid=(COLUMN_BLOCKS,),
            in_specs=[pl.BlockSpec((PER_BLOCK, TILE, TILE), lambda i, *_: (i, 0, 0))],
            out_specs=[spec, spec],
        ),
        out_shape=[pltpu.HBM((COLUMN_BLOCKS,) + shape, jnp.bfloat16)] * 2,
        compiler_params=params(),
        cost_estimate=cost(0, 6 << 20),
        name="place_tiles",
    )(info, in_hbm(tiles))


GATHER_NEAR, GATHER_MIDDLE, GATHER_FAR, SPREAD_OTHER, SPREAD_OWN = 0, 3, 6, 8, 12
PLACES_AT = 16
ROWS_AT = PLACES_AT + 5
COLS_AT = ROWS_AT + COLUMN_BLOCKS * PER_BLOCK
COUNTS_AT = COLS_AT + COLUMN_BLOCKS * PER_BLOCK


def band_row(info, block, slot):
    row = info[ROWS_AT + block * PER_BLOCK + slot]
    return info[PLACES_AT + (row >> 1)] * 2 + (row & 1)


def column_and_live(info, block, slot):
    return info[COLS_AT + block * PER_BLOCK + slot], slot < info[COUNTS_AT + block]


def gather_kernel(n, carried, at, info, tiles, *refs):
    fields = refs[:n]
    before = refs[n : n + carried]
    outs = refs[n + carried : -1]
    total = refs[-1]
    step = pl.program_id(0)

    @pl.when(step == 0)
    def _():
        for j in range(5):
            total[2 * j : 2 * j + 2] = (
                before[j][...].reshape(2, TILE, H) if carried else jnp.zeros((2, TILE, H), jnp.float32)
            )

    for j in range(n):

        @pl.when(step == j)
        def _(j=j):
            block = info[at + j]
            field_high, field_low = split(fields[j][...])
            placed = []
            for slot in range(PER_BLOCK):
                column, live = column_and_live(info, block, slot)
                tile = jnp.where(live, tiles[slot], 0.0)
                halves = [jnp.where(column == half, tile, 0.0) for half in range(ROWS // TILE)]
                placed.append(jnp.concatenate(halves, axis=1))
            high, low = split(jnp.concatenate(placed, axis=0))
            product = dot3(high, low, field_high, field_low)
            for slot in range(PER_BLOCK):
                row = band_row(info, block, slot)
                total[row] += product[slot * TILE : (slot + 1) * TILE]

    @pl.when(step == n - 1)
    def _():
        for j in range(5):
            outs[j][...] = total[2 * j : 2 * j + 2].reshape(ROWS, H)


def gather_terms(at, info, tiles, fields, before=()):
    n = len(fields)
    whole = pl.BlockSpec((ROWS, H), lambda i, *_: (0, 0))
    block = pl.BlockSpec((PER_BLOCK, TILE, TILE), lambda i, info: (info[at + i], 0, 0))
    return pl.pallas_call(
        functools.partial(gather_kernel, n, len(before), at),
        grid_spec=pltpu.PrefetchScalarGridSpec(
            num_scalar_prefetch=1,
            grid=(n,),
            in_specs=[block] + [whole] * (n + len(before)),
            out_specs=[whole] * 5,
            scratch_shapes=[pltpu.VMEM((10, TILE, H), jnp.float32)],
        ),
        out_shape=[jax.ShapeDtypeStruct((ROWS, H), jnp.float32)] * 5,
        compiler_params=params(),
        cost_estimate=SHORT,
        name="gather_terms",
    )(info, in_hbm(tiles), *fields, *before)


def dense_kernel(own, *refs):
    got, (weight, bias, cotangent, agg, output, grad_pre, grad_agg) = refs[:-7], refs[-7:]
    total = own[...]
    for ref in got:
        total += ref[...]
    agg[...] = total
    weight_high, weight_low = split(weight[...])
    value = dot3(*split(total), weight_high, weight_low) + bias[...]
    scale = 0.7978845608028654
    square = value * value
    turn = jnp.tanh(scale * (value + 0.044715 * (square * value)))
    half = 0.5 * (1.0 + turn)
    output[...] = value * half
    slope = half + 0.5 * value * (1.0 - turn * turn) * (scale * (1.0 + 3.0 * 0.044715 * square))
    grad = cotangent[...] * slope
    grad_pre[...] = grad
    turned_high, turned_low = split(weight[...].T)
    grad_agg[...] = dot3(*split(grad), turned_high, turned_low)


def dense(own, got, weight, bias, cotangent):
    return pl.pallas_call(
        dense_kernel,
        out_shape=[jax.ShapeDtypeStruct((ROWS, H), jnp.float32)] * 4,
        compiler_params=params(),
        cost_estimate=cost(12 * 256 * 256 * 256, 10 * 256 * 1024),
        name="dense",
    )(own, *got, weight, bias.reshape(1, H), cotangent)


def weight_kernel(agg, grad_pre, weight_term, bias_term):
    weight_term[...] = dot3(*split(agg[...].T), *split(grad_pre[...]))
    total = jnp.sum(grad_pre[...], axis=0, keepdims=True)
    wide = H // PART
    bias_term[...] = jnp.zeros_like(bias_term)
    for j in range(PART):
        bias_term[j : j + 1, :wide] = total[:, j * wide : (j + 1) * wide]


def weight_terms(agg, grad_pre):
    return pl.pallas_call(
        weight_kernel,
        out_shape=[
            pltpu.HBM((H, H), jnp.float32),
            pltpu.HBM((PART, 128), jnp.float32),
        ],
        compiler_params=params(),
        cost_estimate=cost(6 * 256 * 256 * 256, 3 * 256 * 1024),
        name="weight_terms",
    )(agg, grad_pre)


def spread_kernel(at, info, high_t, low_t, own, a, b, y1, y2, *refs):
    outs, (band_high, band_low) = refs[:-2], refs[-2:]
    step = pl.program_id(0)

    @pl.when(step == 0)
    def _():
        for j, ref in enumerate((own, a, b, y1, y2)):
            high, low = split(ref[...])
            band_high[2 * j : 2 * j + 2] = high.reshape(2, TILE, H)
            band_low[2 * j : 2 * j + 2] = low.reshape(2, TILE, H)

    block = info[at + step]
    chosen = [band_row(info, block, slot) for slot in range(PER_BLOCK)]
    chosen_high = jnp.concatenate([band_high[row] for row in chosen], axis=0)
    chosen_low = jnp.concatenate([band_low[row] for row in chosen], axis=0)
    product = dot3(high_t[0], low_t[0], chosen_high, chosen_low)
    if len(outs) == 1:
        outs[0][0] = product
    else:
        for j, out in enumerate(outs):

            @pl.when(step == j)
            def _(out=out):
                out[...] = product


def spread_terms(at, n, info, high_t, low_t, band, apart=False):
    whole = pl.BlockSpec((ROWS, H), lambda i, *_: (0, 0))
    tiles = pl.BlockSpec((1, ROWS, PER_BLOCK * TILE), lambda i, info: (info[at + i], 0, 0))
    return pl.pallas_call(
        functools.partial(spread_kernel, at),
        grid_spec=pltpu.PrefetchScalarGridSpec(
            num_scalar_prefetch=1,
            grid=(n,),
            in_specs=[tiles, tiles] + [whole] * 5,
            out_specs=[whole] * n if apart else pl.BlockSpec((1, ROWS, H), lambda i, *_: (i, 0, 0)),
            scratch_shapes=[pltpu.VMEM((10, TILE, H), jnp.bfloat16)] * 2,
        ),
        out_shape=[pltpu.HBM((ROWS, H), jnp.float32)] * n if apart else pltpu.HBM((n, ROWS, H), jnp.float32),
        compiler_params=params(),
        cost_estimate=LONG,
        name="spread_terms",
    )(info, in_hbm(high_t), in_hbm(low_t), *band)


def turn_kernel(kept_first, given_first, far, kept, given, second, passed, held):
    passed[...] = kept_first[...] + given_first[0] + far[...]
    held[...] = kept[...] + given[0] + second[...]


def turn_terms(kept_first, kept, given, far, second):
    whole = pl.BlockSpec((ROWS, H), lambda i: (0, 0))
    return pl.pallas_call(
        turn_kernel,
        grid=(1,),
        in_specs=[
            whole,
            pl.BlockSpec((1, ROWS, H), lambda i: (1, 0, 0)),
            whole,
            whole,
            pl.BlockSpec((1, ROWS, H), lambda i: (3, 0, 0)),
            whole,
        ],
        out_specs=[whole, whole],
        out_shape=[jax.ShapeDtypeStruct((ROWS, H), jnp.float32)] * 2,
        compiler_params=params(),
        cost_estimate=LONG,
        name="turn_terms",
    )(kept_first, given, far, kept, given, second)


def other_core(value):
    return lax.ppermute(value, "core", [(0, 1), (1, 0)])


def along_loop(value, sign):
    pairs = []
    for z in range(Z_HI):
        for core in range(CORE):
            by = sign if core == 0 else -sign
            pairs.append((z * CORE + core, (z + by) % Z_HI * CORE + core))
    return lax.ppermute(value, LOOP, pairs)


def in_triple(value, by):
    return lax.ppermute(value, "z_lo", [(i, (i + by) % Z_LO) for i in range(Z_LO)])


def across_triples(value, by):
    pairs = [(r, (r + Z_LO * by[r % Z_LO]) % N_REP) for r in range(N_REP)]
    return lax.ppermute(value, REP, pairs)


def swap(value, axes):
    return lax.all_to_all(value, axes, 0, 0, tiled=True)


def copy_kernel(parts, bias_part, out):
    total = jnp.sum(parts[...], axis=0)
    if bias_part is not None:
        total = jnp.concatenate([total, bias_part[...]], axis=1)
    for j in range(out.shape[0]):
        out[j] = total


def sum_and_copy(parts, copies, bias_part=None):
    width = parts.shape[2] + (0 if bias_part is None else bias_part.shape[1])
    if bias_part is None:
        kernel = lambda parts, out: copy_kernel(parts, None, out)
    else:
        kernel = copy_kernel
    return pl.pallas_call(
        kernel,
        out_shape=jax.ShapeDtypeStruct((copies, PART, width), jnp.float32),
        compiler_params=params(),
        cost_estimate=cost(1 << 10, 1 << 10),
        name="sum_and_copy",
    )(*((parts,) if bias_part is None else (parts, bias_part)))


def read_kernel(whole, weight_whole, bias_whole):
    for j in range(N_PLANE):
        weight_whole[j * PART : (j + 1) * PART, :] = whole[j, :, :H] / NODES
    bias_part = jnp.sum(whole[:, :, H:], axis=0) / NODES
    wide = H // PART
    for j in range(PART):
        bias_whole[:, j * wide : (j + 1) * wide] = bias_part[j : j + 1, :wide]


def read_sums(whole):
    weight_whole, bias_whole = pl.pallas_call(
        read_kernel,
        out_shape=[jax.ShapeDtypeStruct((H, H), jnp.float32), jax.ShapeDtypeStruct((1, H), jnp.float32)],
        compiler_params=params(),
        name="read_sums",
    )(whole)
    return weight_whole, bias_whole.reshape(H)


def after(value, *others):
    return lax.optimization_barrier((value,) + others)


def per_device(features, weight, bias, tile_values, tile_rows, tile_cols, tile_counts, cotangent):
    z_hi, core, z_lo = lax.axis_index("z_hi"), lax.axis_index("core"), lax.axis_index("z_lo")

    turn = 1 - 2 * core
    first = (z_hi - turn) % Z_HI
    second = (z_hi + turn) % Z_HI
    far = (z_hi + 2) % Z_HI

    def block(z, c):
        return z * CORE + c

    blocks = [
        block(z_hi, core),
        block(z_hi, 1 - core),
        block(first, core),
        block(second, 1 - core),
        block(second, core),
        block(first, 1 - core),
        block(far, core),
        block(far, 1 - core),
        block(far, 1 - core),
        block(second, 1 - core),
        block(first, 1 - core),
        block(z_hi, 1 - core),
        block(far, core),
        block(first, core),
        block(second, core),
        block(z_hi, core),
    ]
    places = [
        jnp.where(z_lo == 0, line[0], jnp.where(z_lo == 1, line[1], line[2])) for line in zip(*BAND_PLACE)
    ]
    (scalars,) = after(jnp.stack(blocks + places))
    info = jnp.concatenate([scalars, tile_rows[0], tile_cols[0], tile_counts[0]])

    first_upper = along_loop(features[:TILE], 1)
    first_lower = along_loop(features[TILE:], 1)
    field_second = along_loop(features, -1)
    field_other = other_core(features)
    first_upper, info = after(first_upper, info)
    far_upper = along_loop(first_upper, 1)
    far_lower = along_loop(first_lower, 1)
    field_first = jnp.concatenate([first_upper, first_lower])
    field_far = jnp.concatenate([far_upper, far_lower])
    other_first = other_core(field_first)
    terms = gather_terms(GATHER_NEAR, info, tile_values[0], (features, field_other, field_first))
    far_upper, field_second, *terms = after(far_upper, field_second, *terms)
    other_second = other_core(field_second)
    other_far = other_core(field_far)
    terms = gather_terms(GATHER_MIDDLE, info, tile_values[0], (other_first, field_second, other_second), terms)
    own, term_a, term_b, term_y1, term_y2 = gather_terms(
        GATHER_FAR, info, tile_values[0], (field_far, other_far), terms
    )

    high_t, low_t = place_tiles(info, tile_values[0])
    got_y1 = across_triples(term_y1, (-1, -1, 1))
    got_y2 = across_triples(term_y2, (-1, 1, 1))
    got_a = in_triple(term_a + got_y1, 1)
    got_b = in_triple(term_b + got_y2, 2)
    got_a, got_b, high_t, low_t = after(got_a, got_b, high_t, low_t)
    agg, output, grad_pre, grad_agg = dense(own, (got_a, got_b), weight, bias, cotangent)
    band_a = in_triple(grad_agg, -1)
    band_b = in_triple(grad_agg, -2)
    weight_term, bias_term = weight_terms(agg, grad_pre)
    band_a, band_b, _ = after(band_a, band_b, weight_term)
    band_y1 = across_triples(band_a, (1, 1, -1))
    band_y2 = across_triples(band_b, (1, -1, -1))
    sums = swap(weight_term.reshape(N_PLANE, PART, H), PLANE)
    sums = sum_and_copy(sums, N_COLUMN, bias_term)
    band = (grad_agg, band_a, band_b, band_y1, band_y2)
    sums = sum_and_copy(swap(sums, COLUMN), N_PLANE)

    given = other_core(spread_terms(SPREAD_OTHER, 4, info, high_t, low_t, band))
    kept_far, kept_first, kept_second, kept = spread_terms(SPREAD_OWN, 4, info, high_t, low_t, band, apart=True)
    got_far = along_loop(kept_far + given[0], -1)
    got_second = along_loop(kept_second + given[2], 1)
    passed, held = turn_terms(kept_first, kept, given, got_far, got_second)
    grad_features = held + along_loop(passed, -1)
    weight_whole, bias_whole = read_sums(swap(sums, PLANE))
    return (output, grad_features, weight_whole, bias_whole)


def solution(mesh):
    cut = Mesh(mesh.devices.reshape(Z_HI, CORE, X, Y, Z_LO), AXES)
    nodes = P(AXES)
    return jax.shard_map(
        per_device,
        mesh=cut,
        in_specs=(nodes, P(), P(), nodes, nodes, nodes, nodes, nodes),
        out_specs=(nodes, nodes, P(), P()),
        check_vma=False,
    )
```

time: 220 us -> 188 us (0.85)
  the two profiles are of different devices: /device:TPU:8 before, /device:TPU:2 now
where the time goes in v2:
time: 188 us; the launch traced here: 186 us
  starting transfers between devices  116 us (62%)
  Pallas kernels  33.9 us (18%)
  waiting for transfers between devices  29.3 us (16%)
  other arithmetic  2.89 us (2%)
  local copies, waits for them, and re-layouts  2.79 us (1%)
    ppermute x8, starting transfers between devices, along_loop(): return lax.ppermute(value, LOOP, pairs)  46.4 us
    all_to_all x3, starting transfers between devices, swap(): return lax.all_to_all(value, axes, 0, 0, tiled=True)  28.3 us
    ppermute x8, waiting for transfers between devices, along_loop(): return lax.ppermute(value, LOOP, pairs)  19.7 us
    ppermute x4, starting transfers between devices, across_triples(): return lax.ppermute(value, REP, pairs)  15.5 us
    ppermute x5, starting transfers between devices, other_core(): return lax.ppermute(value, 'core', [(0, 1), (1, 0)])  13 us
    ppermute x4, starting transfers between devices, in_triple(): lax.ppermute(value, 'z_lo', [(i, (i + by) % Z_LO) for i in range(Z_LO)])  12.9 us
    pallas_call x2, Pallas kernels, spread_terms(): pl.pallas_call(functools.partial(spread_kernel, at), grid_spec=pltpu.Pref...  10.1 us
    pallas_call x3, Pallas kernels, gather_terms(): pl.pallas_call(functools.partial(gather_kernel, n, len(before), at), grid...  9.13 us
  transfers between devices with their start and end apart: 24, of which 7 were waited for; matrix products, arithmetic and copies ran while one was open for 2% of the time, Pallas kernels for 15%

profile of v2, /device:TPU:2, one launch (start us, length us, event | category | flops | bytes accessed | tf_op | source)
XLA Modules:
  0.0 186.2 jit_solution(8779202066071672210)
XLA Ops:
  0.6 1.0 fusion.2
  1.6 7.9 %collective-permute-start = (f32[128,256]{1,0:T(8,128)S(1)}, f32[128,256]{1,0:T(8,128)S(1)}, u32[]{:S(2)}, u32[]{:S(2)}) collective-permute-start(f32[128,256]{1,0:T(8,128)S(1)} %get-tuple-element.97), channel_id=1, source_target_pairs={{0,192},{96,672},{192,384},{288,96},{384,576},{480,288},{576,0},{6... | collective-permute-start | bytes 393224 | tf_op jit(solution)/shard_map/ppermute | solution.py:298
  9.5 8.6 %collective-permute-start.6 = (f32[256,256]{1,0:T(8,128)}, f32[256,256]{1,0:T(8,128)S(1)}, u32[]{:S(2)}, u32[]{:S(2)}) collective-permute-start(f32[256,256]{1,0:T(8,128)} %refs_0_.1), channel_id=1, source_target_pairs={{0,576},{96,288},{192,0},{288,480},{384,192},{480,672},{576,384},{... | collective-permute-start | bytes 786440 | tf_op jit(solution)/shard_map/ppermute | solution.py:298
  18.1 1.9 %collective-permute-start.7 = (f32[256,256]{1,0:T(8,128)}, f32[256,256]{1,0:T(8,128)S(1)}, u32[]{:S(2)}, u32[]{:S(2)}) collective-permute-start(f32[256,256]{1,0:T(8,128)} %refs_0_.1), channel_id=1, source_target_pairs={{0,96},{96,0},{1,97},{97,1},{2,98},{98,2},{3,99},{99,3},{4,100},{1... | collective-permute-start | bytes 786440 | tf_op jit(solution)/shard_map/ppermute | solution.py:289
  20.1 2.4 %collective-permute-start.2 = (f32[128,256]{1,0:T(8,128)S(1)}, f32[128,256]{1,0:T(8,128)S(1)}, u32[]{:S(2)}, u32[]{:S(2)}) collective-permute-start(f32[128,256]{1,0:T(8,128)S(1)} %get-tuple-element.96), channel_id=1, source_target_pairs={{0,192},{96,672},{192,384},{288,96},{384,576},{480,288},{576,0},{6... | collective-permute-start | bytes 393224 | tf_op jit(solution)/shard_map/ppermute | solution.py:298
  22.6 0.1 stack.60
  22.7 0.8 pad_add_fusion.info
  23.5 0.0 collective-permute-done
  23.5 6.9 %collective-permute-start.1 = (f32[128,256]{1,0:T(8,128)S(1)}, f32[128,256]{1,0:T(8,128)S(1)}, u32[]{:S(2)}, u32[]{:S(2)}) collective-permute-start(f32[128,256]{1,0:T(8,128)S(1)} %collective-permute-done), channel_id=1, source_target_pairs={{0,192},{96,672},{192,384},{288,96},{384,576},{480,288},{576,0},{6... | collective-permute-start | bytes 393224 | tf_op jit(solution)/shard_map/ppermute | solution.py:298
  30.4 3.5 %collective-permute-done.2 = f32[128,256]{1,0:T(8,128)S(1)} collective-permute-done((f32[128,256]{1,0:T(8,128)S(1)}, f32[128,256]{1,0:T(8,128)S(1)}, u32[]{:S(2)}, u32[]{:S(2)}) %collective-permute-start.2) | collective-permute-done | bytes 131104 | tf_op jit(solution)/shard_map/ppermute | solution.py:298
  34.0 4.5 %collective-permute-start.3 = (f32[128,256]{1,0:T(8,128)S(1)}, f32[128,256]{1,0:T(8,128)S(1)}, u32[]{:S(2)}, u32[]{:S(2)}) collective-permute-start(f32[128,256]{1,0:T(8,128)S(1)} %collective-permute-done.2), channel_id=1, source_target_pairs={{0,192},{96,672},{192,384},{288,96},{384,576},{480,288},{576,0},{6... | collective-permute-start | bytes 393224 | tf_op jit(solution)/shard_map/ppermute | solution.py:298
  38.5 4.6 %collective-permute-start.5 = (f32[256,256]{1,0:T(8,128)S(1)}, f32[256,256]{1,0:T(8,128)S(1)}, u32[]{:S(2)}, u32[]{:S(2)}) collective-permute-start(f32[256,256]{1,0:T(8,128)S(1)} %constant_dynamic-update-slice_fusion.2.refs_2_), channel_id=1, source_target_pairs={{0,96},{96,0},{1,97},{97,1},{2,98},{98,2},{3,99},{99,3},{4,100},{1... | collective-permute-start | bytes 786440 | tf_op jit(solution)/shard_map/ppermute | solution.py:289
  43.1 0.0 collective-permute-done.7.refs_1_
  43.1 0.0 copy-start
  43.1 0.9 copy-done
  44.1 3.3 %gather_terms.3 = (f32[256,256]{1,0:T(8,128)S(1)}, f32[256,256]{1,0:T(8,128)S(1)}, f32[256,256]{1,0:T(8,128)S(1)}, f32[256,256]{1,0:T(8,128)S(1)}, f32[256,256]{1,0:T(8,128)S(1)}) custom-call(s32[93]{0:T(128)S(1)} %pad_add_fusion.info, f32[32,128,128]{2,1,0:T(8,128)} %bitcast.28, f32[256,256]{1,0:T(8,128)S(1)} %copy-done, ...), custom_call_target="tpu_custom_call" | custom-call | flops 1024 | bytes 1024 | tf_op jit(solution)/shard_map/gather_terms/pallas_call | solution.py:149
  47.4 0.0 collective-permute-done.1
  47.4 0.0 collective-permute-done.6.refs_1_
  47.4 1.9 %collective-permute-start.8 = (f32[256,256]{1,0:T(8,128)S(1)}, f32[256,256]{1,0:T(8,128)S(1)}, u32[]{:S(2)}, u32[]{:S(2)}) collective-permute-start(f32[256,256]{1,0:T(8,128)S(1)} %collective-permute-done.6.refs_1_), channel_id=1, source_target_pairs={{0,96},{96,0},{1,97},{97,1},{2,98},{98,2},{3,99},{99,3},{4,100},{1... | collective-permute-start | bytes 786440 | tf_op jit(solution)/shard_map/ppermute | solution.py:289
  49.4 0.0 collective-permute-done.3
  49.4 2.4 %collective-permute-start.4 = (f32[256,256]{1,0:T(8,128)S(1)}, f32[256,256]{1,0:T(8,128)S(1)}, u32[]{:S(2)}, u32[]{:S(2)}) collective-permute-start(f32[256,256]{1,0:T(8,128)S(1)} %constant_dynamic-update-slice_fusion.refs_0_), channel_id=1, source_target_pairs={{0,96},{96,0},{1,97},{97,1},{2,98},{98,2},{3,99},{99,3},{4,100},{1... | collective-permute-start | bytes 786440 | tf_op jit(solution)/shard_map/ppermute | solution.py:289
  51.8 0.0 collective-permute-done.8.refs_2_
  51.8 3.4 %gather_terms.4 = (f32[256,256]{1,0:T(8,128)S(1)}, f32[256,256]{1,0:T(8,128)S(1)}, f32[256,256]{1,0:T(8,128)S(1)}, f32[256,256]{1,0:T(8,128)S(1)}, f32[256,256]{1,0:T(8,128)S(1)}) custom-call(s32[93]{0:T(128)S(1)} %pad_add_fusion.info, f32[32,128,128]{2,1,0:T(8,128)} %bitcast.29, f32[256,256]{1,0:T(8,128)S(1)} %collective-permute-done.5.refs_0_, ...), custom_call_target="tpu_custom_call" | custom-call | flops 1024 | bytes 1024 | tf_op jit(solution)/shard_map/gather_terms/pallas_call | solution.py:149
  55.2 0.0 collective-permute-done.4.refs_1_
  55.2 2.4 %gather_terms.5 = (f32[256,256]{1,0:T(8,128)S(1)}, f32[256,256]{1,0:T(8,128)S(1)}, f32[256,256]{1,0:T(8,128)S(1)}, f32[256,256]{1,0:T(8,128)S(1)}, f32[256,256]{1,0:T(8,128)S(1)}) custom-call(s32[93]{0:T(128)S(1)} %pad_add_fusion.info, f32[32,128,128]{2,1,0:T(8,128)} %bitcast.30, f32[256,256]{1,0:T(8,128)S(1)} %constant_dynamic-update-slice_fusion.refs_0_, ...), custom_call_target="tpu_custom_call" | custom-call | flops 1024 | bytes 1024 | tf_op jit(solution)/shard_map/gather_terms/pallas_call | solution.py:149
  57.7 0.0 copy-start.1
  57.7 0.0 copy-start.2
  57.7 0.0 copy-start.4
  57.7 5.5 %collective-permute-start.9 = (f32[256,256]{1,0:T(8,128)S(1)}, f32[256,256]{1,0:T(8,128)S(1)}, u32[]{:S(2)}, u32[]{:S(2)}) collective-permute-start(f32[256,256]{1,0:T(8,128)S(1)} %get-tuple-element.69), channel_id=1, source_target_pairs={{0,93},{1,94},{2,5},{3,0},{4,1},{5,8},{6,3},{7,4},{8,11},{9,6},{10... | collective-permute-start | bytes 786440 | tf_op jit(solution)/shard_map/ppermute | solution.py:307
  63.2 3.3 %collective-permute-start.11 = (f32[256,256]{1,0:T(8,128)S(1)}, f32[256,256]{1,0:T(8,128)S(1)}, u32[]{:S(2)}, u32[]{:S(2)}) collective-permute-start(f32[256,256]{1,0:T(8,128)S(1)} %get-tuple-element.71), channel_id=1, source_target_pairs={{0,93},{1,4},{2,5},{3,0},{4,7},{5,8},{6,3},{7,10},{8,11},{9,6},{10... | collective-permute-start | bytes 786440 | tf_op jit(solution)/shard_map/ppermute | solution.py:307
  66.4 3.4 %collective-permute-done.9 = f32[256,256]{1,0:T(8,128)S(1)} collective-permute-done((f32[256,256]{1,0:T(8,128)S(1)}, f32[256,256]{1,0:T(8,128)S(1)}, u32[]{:S(2)}, u32[]{:S(2)}) %collective-permute-start.9) | collective-permute-done | bytes 262176 | tf_op jit(solution)/shard_map/ppermute | solution.py:307
  69.9 3.0 %collective-permute-start.10 = (f32[256,256]{1,0:T(8,128)S(1)}, f32[256,256]{1,0:T(8,128)S(1)}, u32[]{:S(2)}, u32[]{:S(2)}) collective-permute-start(f32[256,256]{1,0:T(8,128)S(1)} %add.76), channel_id=1, source_target_pairs={{0,1},{1,2},{2,0},{3,4},{4,5},{5,3},{6,7},{7,8},{8,6},{9,10},{10,1... | collective-permute-start | bytes 786440 | tf_op jit(solution)/shard_map/ppermute | solution.py:302
  72.9 1.6 collective-permute-done.11
  74.6 3.2 %collective-permute-start.12 = (f32[256,256]{1,0:T(8,128)S(1)}, f32[256,256]{1,0:T(8,128)S(1)}, u32[]{:S(2)}, u32[]{:S(2)}) collective-permute-start(f32[256,256]{1,0:T(8,128)S(1)} %add.77), channel_id=1, source_target_pairs={{0,2},{1,0},{2,1},{3,5},{4,3},{5,4},{6,8},{7,6},{8,7},{9,11},{10,9... | collective-permute-start | bytes 786440 | tf_op jit(solution)/shard_map/ppermute | solution.py:302
  77.7 7.1 %place_tiles.1 = (bf16[8,256,512]{2,1,0:T(8,128)(2,1)}, bf16[8,256,512]{2,1,0:T(8,128)(2,1)}) custom-call(s32[93]{0:T(128)S(1)} %pad_add_fusion.info, f32[32,128,128]{2,1,0:T(8,128)} %bitcast.31), custom_call_target="tpu_custom_call" | custom-call | bytes 6291456 | tf_op jit(solution)/shard_map/place_tiles/pallas_call | solution.py:76
  84.8 0.0 collective-permute-done.12.refs_1_
  84.8 1.2 dense.1
  86.1 3.3 %collective-permute-start.14 = (f32[256,256]{1,0:T(8,128)S(1)}, f32[256,256]{1,0:T(8,128)S(1)}, u32[]{:S(2)}, u32[]{:S(2)}) collective-permute-start(f32[256,256]{1,0:T(8,128)S(1)} %get-tuple-element.79.own), channel_id=1, source_target_pairs={{0,1},{1,2},{2,0},{3,4},{4,5},{5,3},{6,7},{7,8},{8,6},{9,10},{10,1... | collective-permute-start | bytes 786440 | tf_op jit(solution)/shard_map/ppermute | solution.py:302
  89.4 3.4 %collective-permute-start.13 = (f32[256,256]{1,0:T(8,128)S(1)}, f32[256,256]{1,0:T(8,128)S(1)}, u32[]{:S(2)}, u32[]{:S(2)}) collective-permute-start(f32[256,256]{1,0:T(8,128)S(1)} %get-tuple-element.79.own), channel_id=1, source_target_pairs={{0,2},{1,0},{2,1},{3,5},{4,3},{5,4},{6,8},{7,6},{8,7},{9,11},{10,9... | collective-permute-start | bytes 786440 | tf_op jit(solution)/shard_map/ppermute | solution.py:302
  92.8 1.0 weight_terms.1
  93.8 10.9 %all-to-all-start = ((f32[32,8,256]{2,1,0:T(8,128)}), f32[32,8,256]{2,1,0:T(8,128)S(1)}, u32[]{:S(2)}, u32[]{:S(2)}) async-start(f32[32,8,256]{2,1,0:T(8,128)} %bitcast.32), calls=%async_computation | async-start | bytes 524288 | tf_op jit(solution)/shard_map/all_to_all | solution.py:311
  104.7 0.0 collective-permute-done.14.b
  104.7 3.4 %collective-permute-start.15 = (f32[256,256]{1,0:T(8,128)S(1)}, f32[256,256]{1,0:T(8,128)S(1)}, u32[]{:S(2)}, u32[]{:S(2)}) collective-permute-start(f32[256,256]{1,0:T(8,128)S(1)} %collective-permute-done.13.a), channel_id=1, source_target_pairs={{0,3},{1,4},{2,95},{3,6},{4,7},{5,2},{6,9},{7,10},{8,5},{9,12},{10... | collective-permute-start | bytes 786440 | tf_op jit(solution)/shard_map/ppermute | solution.py:307
  108.1 3.4 %collective-permute-start.16 = (f32[256,256]{1,0:T(8,128)S(1)}, f32[256,256]{1,0:T(8,128)S(1)}, u32[]{:S(2)}, u32[]{:S(2)}) collective-permute-start(f32[256,256]{1,0:T(8,128)S(1)} %collective-permute-done.14.b), channel_id=1, source_target_pairs={{0,3},{1,94},{2,95},{3,6},{4,1},{5,2},{6,9},{7,4},{8,5},{9,12},{10... | collective-permute-start | bytes 786440 | tf_op jit(solution)/shard_map/ppermute | solution.py:307
  111.5 4.6 %all-to-all-done.parts = f32[32,8,256]{2,1,0:T(8,128)S(1)} async-done(((f32[32,8,256]{2,1,0:T(8,128)}), f32[32,8,256]{2,1,0:T(8,128)S(1)}, u32[]{:S(2)}, u32[]{:S(2)}) %all-to-all-start) | async-done | bytes 262176 | tf_op jit(solution)/shard_map/all_to_all | solution.py:311
  116.1 0.7 copy-done.3
  116.8 0.8 sum_and_copy.2
  117.5 11.5 %all-to-all-start.1 = ((f32[24,8,384]{2,1,0:T(8,128)}), f32[24,8,384]{2,1,0:T(8,128)}, u32[]{:S(2)}, u32[]{:S(2)}) async-start(f32[24,8,384]{2,1,0:T(8,128)} %sum_and_copy.2), calls=%async_computation.1 | async-start | bytes 589824 | tf_op jit(solution)/shard_map/all_to_all | solution.py:311
  129.0 5.0 %spread_terms.3 = f32[4,256,256]{2,1,0:T(8,128)} custom-call(s32[93]{0:T(128)S(1)} %pad_add_fusion.info, bf16[8,256,512]{2,1,0:T(8,128)(2,1)} %get-tuple-element.77.high_t, bf16[8,256,512]{2,1,0:T(8,128)(2,1)} %get-tuple-element.78.low_t, f32[256,256]{1,0:T(8,128)S(1)} %get-tuple-element.79.own, f32[256,256]{1,0:T(8,128)S(1)} %collective-permute-done.13.a, ...), custom_call_target="tpu_custom_call" | custom-call | flops 1099511627776 | bytes 4294967296 | tf_op jit(solution)/shard_map/spread_terms/pallas_call | solution.py:246
  134.0 2.2 %collective-permute-start.17 = (f32[4,256,256]{2,1,0:T(8,128)}, f32[4,256,256]{2,1,0:T(8,128)}, u32[]{:S(2)}, u32[]{:S(2)}) collective-permute-start(f32[4,256,256]{2,1,0:T(8,128)} %spread_terms.3), channel_id=1, source_target_pairs={{0,96},{96,0},{1,97},{97,1},{2,98},{98,2},{3,99},{99,3},{4,100},{1... | collective-permute-start | bytes 3145736 | tf_op jit(solution)/shard_map/ppermute | solution.py:289
  136.2 5.1 %spread_terms.2 = (f32[256,256]{1,0:T(8,128)}, f32[256,256]{1,0:T(8,128)}, f32[256,256]{1,0:T(8,128)}, f32[256,256]{1,0:T(8,128)}) custom-call(s32[93]{0:T(128)S(1)} %pad_add_fusion.info, bf16[8,256,512]{2,1,0:T(8,128)(2,1)} %get-tuple-element.77.high_t, bf16[8,256,512]{2,1,0:T(8,128)(2,1)} %get-tuple-element.78.low_t, ...), custom_call_target="tpu_custom_call" | custom-call | flops 1099511627776 | bytes 4294967296 | tf_op jit(solution)/shard_map/spread_terms/pallas_call | solution.py:246
  141.3 0.0 collective-permute-done.17.given_first.given
  141.3 1.3 fusion
  142.6 5.4 %collective-permute-start.19 = (f32[256,256]{1,0:T(8,128)S(1)}, f32[256,256]{1,0:T(8,128)S(1)}, u32[]{:S(2)}, u32[]{:S(2)}) collective-permute-start(f32[256,256]{1,0:T(8,128)S(1)} %get-tuple-element.94), channel_id=1, source_target_pairs={{0,192},{96,672},{192,384},{288,96},{384,576},{480,288},{576,0},{6... | collective-permute-start | bytes 786440 | tf_op jit(solution)/shard_map/ppermute | solution.py:298
  148.0 3.5 %collective-permute-start.18 = (f32[256,256]{1,0:T(8,128)S(1)}, f32[256,256]{1,0:T(8,128)S(1)}, u32[]{:S(2)}, u32[]{:S(2)}) collective-permute-start(f32[256,256]{1,0:T(8,128)S(1)} %get-tuple-element.95), channel_id=1, source_target_pairs={{0,576},{96,288},{192,0},{288,480},{384,192},{480,672},{576,384},{... | collective-permute-start | bytes 786440 | tf_op jit(solution)/shard_map/ppermute | solution.py:298
  151.5 1.8 sum_and_copy.3
  153.3 6.0 %all-to-all-start.2 = ((f32[32,8,384]{2,1,0:T(8,128)}), f32[32,8,384]{2,1,0:T(8,128)}, u32[]{:S(2)}, u32[]{:S(2)}) async-start(f32[32,8,384]{2,1,0:T(8,128)} %sum_and_copy.3), calls=%async_computation.2 | async-start | bytes 786432 | tf_op jit(solution)/shard_map/all_to_all | solution.py:311
  159.3 0.9 collective-permute-done.19.second
  160.2 6.5 %collective-permute-done.18.far = f32[256,256]{1,0:T(8,128)S(1)} collective-permute-done((f32[256,256]{1,0:T(8,128)S(1)}, f32[256,256]{1,0:T(8,128)S(1)}, u32[]{:S(2)}, u32[]{:S(2)}) %collective-permute-start.18) | collective-permute-done | bytes 262176 | tf_op jit(solution)/shard_map/ppermute | solution.py:298
  166.7 1.1 turn_terms.1
  167.9 7.2 %collective-permute-start.20 = (f32[256,256]{1,0:T(8,128)S(1)}, f32[256,256]{1,0:T(8,128)S(1)}, u32[]{:S(2)}, u32[]{:S(2)}) collective-permute-start(f32[256,256]{1,0:T(8,128)S(1)} %get-tuple-element.90), channel_id=1, source_target_pairs={{0,576},{96,288},{192,0},{288,480},{384,192},{480,672},{576,384},{... | collective-permute-start | bytes 786440 | tf_op jit(solution)/shard_map/ppermute | solution.py:298
  175.0 8.7 %collective-permute-done.20 = f32[256,256]{1,0:T(8,128)S(1)} collective-permute-done((f32[256,256]{1,0:T(8,128)S(1)}, f32[256,256]{1,0:T(8,128)S(1)}, u32[]{:S(2)}, u32[]{:S(2)}) %collective-permute-start.20) | collective-permute-done | bytes 262176 | tf_op jit(solution)/shard_map/ppermute | solution.py:298
  183.7 0.7 add.80
  184.5 1.7 read_sums.1
  (21 shorter events, 0.1 us)
Async XLA Ops:
  1.6 21.8 %collective-permute-start = (f32[128,256]{1,0:T(8,128)S(1)}, f32[128,256]{1,0:T(8,128)S(1)}, u32[]{:S(2)}, u32[]{:S(2)}) collective-permute-start(f32[128,256]{1,0:T(8,128)S(1)} %get-tuple-element.97), channel_id=1, source_target_pairs={{0,192},{96,672},{192,384},{288,96},{384,576},{480,288},{576,0},{6... | collective-permute-start | bytes 393224 | tf_op jit(solution)/shard_map/ppermute | solution.py:298
  9.5 37.9 %collective-permute-start.6 = (f32[256,256]{1,0:T(8,128)}, f32[256,256]{1,0:T(8,128)S(1)}, u32[]{:S(2)}, u32[]{:S(2)}) collective-permute-start(f32[256,256]{1,0:T(8,128)} %refs_0_.1), channel_id=1, source_target_pairs={{0,576},{96,288},{192,0},{288,480},{384,192},{480,672},{576,384},{... | collective-permute-start | bytes 786440 | tf_op jit(solution)/shard_map/ppermute | solution.py:298
  18.1 25.0 %collective-permute-start.7 = (f32[256,256]{1,0:T(8,128)}, f32[256,256]{1,0:T(8,128)S(1)}, u32[]{:S(2)}, u32[]{:S(2)}) collective-permute-start(f32[256,256]{1,0:T(8,128)} %refs_0_.1), channel_id=1, source_target_pairs={{0,96},{96,0},{1,97},{97,1},{2,98},{98,2},{3,99},{99,3},{4,100},{1... | collective-permute-start | bytes 786440 | tf_op jit(solution)/shard_map/ppermute | solution.py:289
  20.1 13.9 %collective-permute-start.2 = (f32[128,256]{1,0:T(8,128)S(1)}, f32[128,256]{1,0:T(8,128)S(1)}, u32[]{:S(2)}, u32[]{:S(2)}) collective-permute-start(f32[128,256]{1,0:T(8,128)S(1)} %get-tuple-element.96), channel_id=1, source_target_pairs={{0,192},{96,672},{192,384},{288,96},{384,576},{480,288},{576,0},{6... | collective-permute-start | bytes 393224 | tf_op jit(solution)/shard_map/ppermute | solution.py:298
  23.5 24.0 %collective-permute-start.1 = (f32[128,256]{1,0:T(8,128)S(1)}, f32[128,256]{1,0:T(8,128)S(1)}, u32[]{:S(2)}, u32[]{:S(2)}) collective-permute-start(f32[128,256]{1,0:T(8,128)S(1)} %collective-permute-done), channel_id=1, source_target_pairs={{0,192},{96,672},{192,384},{288,96},{384,576},{480,288},{576,0},{6... | collective-permute-start | bytes 393224 | tf_op jit(solution)/shard_map/ppermute | solution.py:298
  34.0 15.4 %collective-permute-start.3 = (f32[128,256]{1,0:T(8,128)S(1)}, f32[128,256]{1,0:T(8,128)S(1)}, u32[]{:S(2)}, u32[]{:S(2)}) collective-permute-start(f32[128,256]{1,0:T(8,128)S(1)} %collective-permute-done.2), channel_id=1, source_target_pairs={{0,192},{96,672},{192,384},{288,96},{384,576},{480,288},{576,0},{6... | collective-permute-start | bytes 393224 | tf_op jit(solution)/shard_map/ppermute | solution.py:298
  38.5 13.4 %collective-permute-start.5 = (f32[256,256]{1,0:T(8,128)S(1)}, f32[256,256]{1,0:T(8,128)S(1)}, u32[]{:S(2)}, u32[]{:S(2)}) collective-permute-start(f32[256,256]{1,0:T(8,128)S(1)} %constant_dynamic-update-slice_fusion.2.refs_2_), channel_id=1, source_target_pairs={{0,96},{96,0},{1,97},{97,1},{2,98},{98,2},{3,99},{99,3},{4,100},{1... | collective-permute-start | bytes 786440 | tf_op jit(solution)/shard_map/ppermute | solution.py:289
  43.1 1.0 copy-start
  47.4 4.4 %collective-permute-start.8 = (f32[256,256]{1,0:T(8,128)S(1)}, f32[256,256]{1,0:T(8,128)S(1)}, u32[]{:S(2)}, u32[]{:S(2)}) collective-permute-start(f32[256,256]{1,0:T(8,128)S(1)} %collective-permute-done.6.refs_1_), channel_id=1, source_target_pairs={{0,96},{96,0},{1,97},{97,1},{2,98},{98,2},{3,99},{99,3},{4,100},{1... | collective-permute-start | bytes 786440 | tf_op jit(solution)/shard_map/ppermute | solution.py:289
  49.4 5.8 %collective-permute-start.4 = (f32[256,256]{1,0:T(8,128)S(1)}, f32[256,256]{1,0:T(8,128)S(1)}, u32[]{:S(2)}, u32[]{:S(2)}) collective-permute-start(f32[256,256]{1,0:T(8,128)S(1)} %constant_dynamic-update-slice_fusion.refs_0_), channel_id=1, source_target_pairs={{0,96},{96,0},{1,97},{97,1},{2,98},{98,2},{3,99},{99,3},{4,100},{1... | collective-permute-start | bytes 786440 | tf_op jit(solution)/shard_map/ppermute | solution.py:289
  57.7 27.1 %copy-start.1 = (f32[256,256]{1,0:T(8,128)S(1)}, f32[256,256]{1,0:T(8,128)}, u32[]{:S(2)}) copy-start(f32[256,256]{1,0:T(8,128)} %refs_2_.1) | copy-start | bytes 786436
  57.7 27.1 %copy-start.2 = (f32[256,256]{1,0:T(8,128)S(1)}, f32[256,256]{1,0:T(8,128)}, u32[]{:S(2)}) copy-start(f32[256,256]{1,0:T(8,128)} %refs_4_.1) | copy-start | bytes 786436
  57.7 27.1 %copy-start.4 = (f32[256]{0:T(256)S(1)}, f32[256]{0:T(256)}, u32[]{:S(2)}) copy-start(f32[256]{0:T(256)} %param.10) | copy-start | bytes 3076
  57.7 12.1 %collective-permute-start.9 = (f32[256,256]{1,0:T(8,128)S(1)}, f32[256,256]{1,0:T(8,128)S(1)}, u32[]{:S(2)}, u32[]{:S(2)}) collective-permute-start(f32[256,256]{1,0:T(8,128)S(1)} %get-tuple-element.69), channel_id=1, source_target_pairs={{0,93},{1,94},{2,5},{3,0},{4,1},{5,8},{6,3},{7,4},{8,11},{9,6},{10... | collective-permute-start | bytes 786440 | tf_op jit(solution)/shard_map/ppermute | solution.py:307
  63.2 11.3 %collective-permute-start.11 = (f32[256,256]{1,0:T(8,128)S(1)}, f32[256,256]{1,0:T(8,128)S(1)}, u32[]{:S(2)}, u32[]{:S(2)}) collective-permute-start(f32[256,256]{1,0:T(8,128)S(1)} %get-tuple-element.71), channel_id=1, source_target_pairs={{0,93},{1,4},{2,5},{3,0},{4,7},{5,8},{6,3},{7,10},{8,11},{9,6},{10... | collective-permute-start | bytes 786440 | tf_op jit(solution)/shard_map/ppermute | solution.py:307
  69.9 14.9 %collective-permute-start.10 = (f32[256,256]{1,0:T(8,128)S(1)}, f32[256,256]{1,0:T(8,128)S(1)}, u32[]{:S(2)}, u32[]{:S(2)}) collective-permute-start(f32[256,256]{1,0:T(8,128)S(1)} %add.76), channel_id=1, source_target_pairs={{0,1},{1,2},{2,0},{3,4},{4,5},{5,3},{6,7},{7,8},{8,6},{9,10},{10,1... | collective-permute-start | bytes 786440 | tf_op jit(solution)/shard_map/ppermute | solution.py:302
  74.6 10.2 %collective-permute-start.12 = (f32[256,256]{1,0:T(8,128)S(1)}, f32[256,256]{1,0:T(8,128)S(1)}, u32[]{:S(2)}, u32[]{:S(2)}) collective-permute-start(f32[256,256]{1,0:T(8,128)S(1)} %add.77), channel_id=1, source_target_pairs={{0,2},{1,0},{2,1},{3,5},{4,3},{5,4},{6,8},{7,6},{8,7},{9,11},{10,9... | collective-permute-start | bytes 786440 | tf_op jit(solution)/shard_map/ppermute | solution.py:302
  86.1 18.6 %collective-permute-start.14 = (f32[256,256]{1,0:T(8,128)S(1)}, f32[256,256]{1,0:T(8,128)S(1)}, u32[]{:S(2)}, u32[]{:S(2)}) collective-permute-start(f32[256,256]{1,0:T(8,128)S(1)} %get-tuple-element.79.own), channel_id=1, source_target_pairs={{0,1},{1,2},{2,0},{3,4},{4,5},{5,3},{6,7},{7,8},{8,6},{9,10},{10,1... | collective-permute-start | bytes 786440 | tf_op jit(solution)/shard_map/ppermute | solution.py:302
  89.4 15.3 %collective-permute-start.13 = (f32[256,256]{1,0:T(8,128)S(1)}, f32[256,256]{1,0:T(8,128)S(1)}, u32[]{:S(2)}, u32[]{:S(2)}) collective-permute-start(f32[256,256]{1,0:T(8,128)S(1)} %get-tuple-element.79.own), channel_id=1, source_target_pairs={{0,2},{1,0},{2,1},{3,5},{4,3},{5,4},{6,8},{7,6},{8,7},{9,11},{10,9... | collective-permute-start | bytes 786440 | tf_op jit(solution)/shard_map/ppermute | solution.py:302
  93.8 22.2 %all-to-all-start = ((f32[32,8,256]{2,1,0:T(8,128)}), f32[32,8,256]{2,1,0:T(8,128)S(1)}, u32[]{:S(2)}, u32[]{:S(2)}) async-start(f32[32,8,256]{2,1,0:T(8,128)} %bitcast.32), calls=%async_computation | async-start | bytes 524288 | tf_op jit(solution)/shard_map/all_to_all | solution.py:311
  104.7 24.3 %collective-permute-start.15 = (f32[256,256]{1,0:T(8,128)S(1)}, f32[256,256]{1,0:T(8,128)S(1)}, u32[]{:S(2)}, u32[]{:S(2)}) collective-permute-start(f32[256,256]{1,0:T(8,128)S(1)} %collective-permute-done.13.a), channel_id=1, source_target_pairs={{0,3},{1,4},{2,95},{3,6},{4,7},{5,2},{6,9},{7,10},{8,5},{9,12},{10... | collective-permute-start | bytes 786440 | tf_op jit(solution)/shard_map/ppermute | solution.py:307
  108.1 20.9 %collective-permute-start.16 = (f32[256,256]{1,0:T(8,128)S(1)}, f32[256,256]{1,0:T(8,128)S(1)}, u32[]{:S(2)}, u32[]{:S(2)}) collective-permute-start(f32[256,256]{1,0:T(8,128)S(1)} %collective-permute-done.14.b), channel_id=1, source_target_pairs={{0,3},{1,94},{2,95},{3,6},{4,1},{5,2},{6,9},{7,4},{8,5},{9,12},{10... | collective-permute-start | bytes 786440 | tf_op jit(solution)/shard_map/ppermute | solution.py:307
  116.1 0.7 copy-start.3
  117.5 34.0 %all-to-all-start.1 = ((f32[24,8,384]{2,1,0:T(8,128)}), f32[24,8,384]{2,1,0:T(8,128)}, u32[]{:S(2)}, u32[]{:S(2)}) async-start(f32[24,8,384]{2,1,0:T(8,128)} %sum_and_copy.2), calls=%async_computation.1 | async-start | bytes 589824 | tf_op jit(solution)/shard_map/all_to_all | solution.py:311
  134.0 7.3 %collective-permute-start.17 = (f32[4,256,256]{2,1,0:T(8,128)}, f32[4,256,256]{2,1,0:T(8,128)}, u32[]{:S(2)}, u32[]{:S(2)}) collective-permute-start(f32[4,256,256]{2,1,0:T(8,128)} %spread_terms.3), channel_id=1, source_target_pairs={{0,96},{96,0},{1,97},{97,1},{2,98},{98,2},{3,99},{99,3},{4,100},{1... | collective-permute-start | bytes 3145736 | tf_op jit(solution)/shard_map/ppermute | solution.py:289
  141.3 25.4 %copy-start.5 = (f32[256,256]{1,0:T(8,128)S(1)}, f32[256,256]{1,0:T(8,128)}, u32[]{:S(2)}) copy-start(f32[256,256]{1,0:T(8,128)} %get-tuple-element.85.kept_first) | copy-start | bytes 786436
  141.3 25.4 %copy-start.6 = (f32[256,256]{1,0:T(8,128)S(1)}, f32[256,256]{1,0:T(8,128)}, u32[]{:S(2)}) copy-start(f32[256,256]{1,0:T(8,128)} %get-tuple-element.87.kept) | copy-start | bytes 786436
  142.6 17.6 %collective-permute-start.19 = (f32[256,256]{1,0:T(8,128)S(1)}, f32[256,256]{1,0:T(8,128)S(1)}, u32[]{:S(2)}, u32[]{:S(2)}) collective-permute-start(f32[256,256]{1,0:T(8,128)S(1)} %get-tuple-element.94), channel_id=1, source_target_pairs={{0,192},{96,672},{192,384},{288,96},{384,576},{480,288},{576,0},{6... | collective-permute-start | bytes 786440 | tf_op jit(solution)/shard_map/ppermute | solution.py:298
  148.0 18.7 %collective-permute-start.18 = (f32[256,256]{1,0:T(8,128)S(1)}, f32[256,256]{1,0:T(8,128)S(1)}, u32[]{:S(2)}, u32[]{:S(2)}) collective-permute-start(f32[256,256]{1,0:T(8,128)S(1)} %get-tuple-element.95), channel_id=1, source_target_pairs={{0,576},{96,288},{192,0},{288,480},{384,192},{480,672},{576,384},{... | collective-permute-start | bytes 786440 | tf_op jit(solution)/shard_map/ppermute | solution.py:298
  153.3 31.2 %all-to-all-start.2 = ((f32[32,8,384]{2,1,0:T(8,128)}), f32[32,8,384]{2,1,0:T(8,128)}, u32[]{:S(2)}, u32[]{:S(2)}) async-start(f32[32,8,384]{2,1,0:T(8,128)} %sum_and_copy.3), calls=%async_computation.2 | async-start | bytes 786432 | tf_op jit(solution)/shard_map/all_to_all | solution.py:311
  167.9 15.9 %collective-permute-start.20 = (f32[256,256]{1,0:T(8,128)S(1)}, f32[256,256]{1,0:T(8,128)S(1)}, u32[]{:S(2)}, u32[]{:S(2)}) collective-permute-start(f32[256,256]{1,0:T(8,128)S(1)} %get-tuple-element.90), channel_id=1, source_target_pairs={{0,576},{96,288},{192,0},{288,480},{384,192},{480,672},{576,384},{... | collective-permute-start | bytes 786440 | tf_op jit(solution)/shard_map/ppermute | solution.py:298

commit v3 on v2

--- a/solution.py
+++ b/solution.py
@@ -24,7 +24,7 @@
 N_PLANE = X * Y
 N_COLUMN = Z_HI * CORE * Z_LO
 PART = 256 // N_PLANE
-VMEM_LIMIT = 16 * 1024 * 1024
+VMEM_LIMIT = 20 * 1024 * 1024
 
 BAND_PLACE = ((3, 4, 0, 1, 2), (3, 2, 0, 1, 4), (1, 2, 0, 3, 4))
 
@@ -104,54 +104,44 @@
     return info[COLS_AT + block * PER_BLOCK + slot], slot < info[COUNTS_AT + block]
 
 
-def gather_kernel(n, carried, at, info, tiles, *refs):
-    fields = refs[:n]
-    before = refs[n : n + carried]
-    outs = refs[n + carried : -1]
-    total = refs[-1]
-    step = pl.program_id(0)
-
-    @pl.when(step == 0)
-    def _():
-        for j in range(5):
-            total[2 * j : 2 * j + 2] = (
-                before[j][...].reshape(2, TILE, H) if carried else jnp.zeros((2, TILE, H), jnp.float32)
-            )
-
+def gather_kernel(n, carried, at, info, *refs):
+    tiles, fields = refs[:n], refs[n : 2 * n]
+    before = refs[2 * n : 2 * n + carried]
+    outs, total = refs[2 * n + carried : -1], refs[-1]
+    for j in range(5):
+        total[2 * j : 2 * j + 2] = (
+            before[j][...].reshape(2, TILE, H) if carried else jnp.zeros((2, TILE, H), jnp.float32)
+        )
     for j in range(n):
-
-        @pl.when(step == j)
-        def _(j=j):
-            block = info[at + j]
-            field_high, field_low = split(fields[j][...])
-            placed = []
-            for slot in range(PER_BLOCK):
-                column, live = column_and_live(info, block, slot)
-                tile = jnp.where(live, tiles[slot], 0.0)
-                halves = [jnp.where(column == half, tile, 0.0) for half in range(ROWS // TILE)]
-                placed.append(jnp.concatenate(halves, axis=1))
-            high, low = split(jnp.concatenate(placed, axis=0))
-            product = dot3(high, low, field_high, field_low)
-            for slot in range(PER_BLOCK):
-                row = band_row(info, block, slot)
-                total[row] += product[slot * TILE : (slot + 1) * TILE]
-
-    @pl.when(step == n - 1)
-    def _():
-        for j in range(5):
-            outs[j][...] = total[2 * j : 2 * j + 2].reshape(ROWS, H)
+        block = info[at + j]
+        field_high, field_low = split(fields[j][...])
+        placed = []
+        for slot in range(PER_BLOCK):
+            column, live = column_and_live(info, block, slot)
+            tile = jnp.where(live, tiles[j][slot], 0.0)
+            halves = [jnp.where(column == half, tile, 0.0) for half in range(ROWS // TILE)]
+            placed.append(jnp.concatenate(halves, axis=1))
+        high, low = split(jnp.concatenate(placed, axis=0))
+        product = dot3(high, low, field_high, field_low)
+        for slot in range(PER_BLOCK):
+            row = band_row(info, block, slot)
+            total[row] += product[slot * TILE : (slot + 1) * TILE]
+    for j in range(5):
+        outs[j][...] = total[2 * j : 2 * j + 2].reshape(ROWS, H)
 
 
 def gather_terms(at, info, tiles, fields, before=()):
     n = len(fields)
     whole = pl.BlockSpec((ROWS, H), lambda i, *_: (0, 0))
-    block = pl.BlockSpec((PER_BLOCK, TILE, TILE), lambda i, info: (info[at + i], 0, 0))
+    blocks = [
+        pl.BlockSpec((PER_BLOCK, TILE, TILE), lambda i, info, j=j: (info[at + j], 0, 0)) for j in range(n)
+    ]
     return pl.pallas_call(
         functools.partial(gather_kernel, n, len(before), at),
         grid_spec=pltpu.PrefetchScalarGridSpec(
             num_scalar_prefetch=1,
-            grid=(n,),
-            in_specs=[block] + [whole] * (n + len(before)),
+            grid=(1,),
+            in_specs=blocks + [whole] * (n + len(before)),
             out_specs=[whole] * 5,
             scratch_shapes=[pltpu.VMEM((10, TILE, H), jnp.float32)],
         ),
@@ -159,7 +149,7 @@
         compiler_params=params(),
         cost_estimate=SHORT,
         name="gather_terms",
-    )(info, in_hbm(tiles), *fields, *before)
+    )(info, *([in_hbm(tiles)] * n), *fields, *before)
 
 
 def dense_kernel(own, *refs):
@@ -214,49 +204,43 @@
     )(agg, grad_pre)
 
 
-def spread_kernel(at, info, high_t, low_t, own, a, b, y1, y2, *refs):
-    outs, (band_high, band_low) = refs[:-2], refs[-2:]
-    step = pl.program_id(0)
-
-    @pl.when(step == 0)
-    def _():
-        for j, ref in enumerate((own, a, b, y1, y2)):
-            high, low = split(ref[...])
-            band_high[2 * j : 2 * j + 2] = high.reshape(2, TILE, H)
-            band_low[2 * j : 2 * j + 2] = low.reshape(2, TILE, H)
-
-    block = info[at + step]
-    chosen = [band_row(info, block, slot) for slot in range(PER_BLOCK)]
-    chosen_high = jnp.concatenate([band_high[row] for row in chosen], axis=0)
-    chosen_low = jnp.concatenate([band_low[row] for row in chosen], axis=0)
-    product = dot3(high_t[0], low_t[0], chosen_high, chosen_low)
-    if len(outs) == 1:
-        outs[0][0] = product
-    else:
-        for j, out in enumerate(outs):
-
-            @pl.when(step == j)
-            def _(out=out):
-                out[...] = product
+def spread_kernel(at, n, info, *refs):
+    highs, lows = refs[:n], refs[n : 2 * n]
+    band, outs, (band_high, band_low) = refs[2 * n : 2 * n + 5], refs[2 * n + 5 : -2], refs[-2:]
+    for j, ref in enumerate(band):
+        high, low = split(ref[...])
+        band_high[2 * j : 2 * j + 2] = high.reshape(2, TILE, H)
+        band_low[2 * j : 2 * j + 2] = low.reshape(2, TILE, H)
+    for j in range(n):
+        chosen = [band_row(info, info[at + j], slot) for slot in range(PER_BLOCK)]
+        chosen_high = jnp.concatenate([band_high[row] for row in chosen], axis=0)
+        chosen_low = jnp.concatenate([band_low[row] for row in chosen], axis=0)
+        product = dot3(highs[j][0], lows[j][0], chosen_high, chosen_low)
+        if len(outs) == 1:
+            outs[0][j] = product
+        else:
+            outs[j][...] = product
 
 
 def spread_terms(at, n, info, high_t, low_t, band, apart=False):
     whole = pl.BlockSpec((ROWS, H), lambda i, *_: (0, 0))
-    tiles = pl.BlockSpec((1, ROWS, PER_BLOCK * TILE), lambda i, info: (info[at + i], 0, 0))
-    return pl.pallas_call(
-        functools.partial(spread_kernel, at),
+    tiles = [
+        pl.BlockSpec((1, ROWS, PER_BLOCK * TILE), lambda i, info, j=j: (info[at + j], 0, 0)) for j in range(n)
+    ]
+    return pl.pallas_call(
+        functools.partial(spread_kernel, at, n),
         grid_spec=pltpu.PrefetchScalarGridSpec(
             num_scalar_prefetch=1,
-            grid=(n,),
-            in_specs=[tiles, tiles] + [whole] * 5,
-            out_specs=[whole] * n if apart else pl.BlockSpec((1, ROWS, H), lambda i, *_: (i, 0, 0)),
+            grid=(1,),
+            in_specs=tiles * 2 + [whole] * 5,
+            out_specs=[whole] * n if apart else pl.BlockSpec((n, ROWS, H), lambda i, *_: (0, 0, 0)),
             scratch_shapes=[pltpu.VMEM((10, TILE, H), jnp.bfloat16)] * 2,
         ),
         out_shape=[pltpu.HBM((ROWS, H), jnp.float32)] * n if apart else pltpu.HBM((n, ROWS, H), jnp.float32),
         compiler_params=params(),
         cost_estimate=LONG,
         name="spread_terms",
-    )(info, in_hbm(high_t), in_hbm(low_t), *band)
+    )(info, *([in_hbm(high_t)] * n), *([in_hbm(low_t)] * n), *band)
 
 
 def turn_kernel(kept_first, given_first, far, kept, given, second, passed, held):
@@ -395,8 +379,8 @@
     first_upper = along_loop(features[:TILE], 1)
     first_lower = along_loop(features[TILE:], 1)
     field_second = along_loop(features, -1)
-    field_other = other_core(features)
-    first_upper, info = after(first_upper, info)
+    first_upper, own_field, info = after(first_upper, features, info)
+    field_other = other_core(own_field)
     far_upper = along_loop(first_upper, 1)
     far_lower = along_loop(first_lower, 1)
     field_first = jnp.concatenate([first_upper, first_lower])
@@ -434,8 +418,9 @@
     got_far = along_loop(kept_far + given[0], -1)
     got_second = along_loop(kept_second + given[2], 1)
     passed, held = turn_terms(kept_first, kept, given, got_far, got_second)
+    weight_whole, bias_whole = read_sums(swap(sums, PLANE))
+    held, weight_whole, bias_whole = after(held, weight_whole, bias_whole)
     grad_features = held + along_loop(passed, -1)
-    weight_whole, bias_whole = read_sums(swap(sums, PLANE))
     return (output, grad_features, weight_whole, bias_whole)
 
 

time: 188 us -> 179 us (0.952)
  Pallas kernels: 33.9 us -> 30.7 us
  waiting for transfers between devices: 29.3 us -> 26.6 us
  starting transfers between devices: 116 us -> 114 us
    all_to_all x3, starting transfers between devices: 28.3 us -> 23.5 us  [swap(): return lax.all_to_all(value, axes, 0, 0, tiled=True)]
    ppermute x8, waiting for transfers between devices: 19.7 us -> 15.9 us  [along_loop(): return lax.ppermute(value, LOOP, pairs)]
    ppermute x5, starting transfers between devices: 13 us -> 15.5 us  [other_core(): return lax.ppermute(value, 'core', [(0, 1), (1, 0)])]
  transfers between devices with their start and end apart: 24 -> 24, of which waited for: 7 -> 7; matrix products, arithmetic and copies ran while one was open for 2% -> 1% of each run, Pallas kernels for 15% -> 15%
where the time goes in v3:
time: 179 us; the launch traced here: 178 us
  starting transfers between devices  114 us (64%)
  Pallas kernels  30.7 us (17%)
  waiting for transfers between devices  26.6 us (15%)
  other arithmetic  2.89 us (2%)
  local copies, waits for them, and re-layouts  2.79 us (2%)
    ppermute x8, starting transfers between devices, along_loop(): return lax.ppermute(value, LOOP, pairs)  46.5 us
    all_to_all x3, starting transfers between devices, swap(): return lax.all_to_all(value, axes, 0, 0, tiled=True)  23.5 us
    ppermute x8, waiting for transfers between devices, along_loop(): return lax.ppermute(value, LOOP, pairs)  15.9 us
    ppermute x4, starting transfers between devices, across_triples(): return lax.ppermute(value, REP, pairs)  15.5 us
    ppermute x5, starting transfers between devices, other_core(): return lax.ppermute(value, 'core', [(0, 1), (1, 0)])  15.5 us
    ppermute x4, starting transfers between devices, in_triple(): lax.ppermute(value, 'z_lo', [(i, (i + by) % Z_LO) for i in range(Z_LO)])  12.9 us
    pallas_call x2, Pallas kernels, spread_terms(): pl.pallas_call(functools.partial(spread_kernel, at, n), grid_spec=pltpu.P...  8.3 us
    pallas_call x3, Pallas kernels, gather_terms(): pl.pallas_call(functools.partial(gather_kernel, n, len(before), at), grid...  7.7 us
  transfers between devices with their start and end apart: 24, of which 7 were waited for; matrix products, arithmetic and copies ran while one was open for 1% of the time, Pallas kernels for 15%

profile of v3, /device:TPU:2, one launch (start us, length us, event | category | flops | bytes accessed | tf_op | source)
XLA Modules:
  0.0 177.9 jit_solution(3511049530609335841)
XLA Ops:
  0.6 1.0 fusion.2
  1.6 7.9 %collective-permute-start = (f32[128,256]{1,0:T(8,128)S(1)}, f32[128,256]{1,0:T(8,128)S(1)}, u32[]{:S(2)}, u32[]{:S(2)}) collective-permute-start(f32[128,256]{1,0:T(8,128)S(1)} %get-tuple-element.105), channel_id=1, source_target_pairs={{0,192},{96,672},{192,384},{288,96},{384,576},{480,288},{576,0},{6... | collective-permute-start | bytes 393224 | tf_op jit(solution)/shard_map/ppermute | solution.py:282
  9.5 8.6 %collective-permute-start.6 = (f32[256,256]{1,0:T(8,128)}, f32[256,256]{1,0:T(8,128)S(1)}, u32[]{:S(2)}, u32[]{:S(2)}) collective-permute-start(f32[256,256]{1,0:T(8,128)} %refs_3_.1), channel_id=1, source_target_pairs={{0,576},{96,288},{192,0},{288,480},{384,192},{480,672},{576,384},{... | collective-permute-start | bytes 786440 | tf_op jit(solution)/shard_map/ppermute | solution.py:282
  18.1 2.4 %collective-permute-start.2 = (f32[128,256]{1,0:T(8,128)S(1)}, f32[128,256]{1,0:T(8,128)S(1)}, u32[]{:S(2)}, u32[]{:S(2)}) collective-permute-start(f32[128,256]{1,0:T(8,128)S(1)} %get-tuple-element.104), channel_id=1, source_target_pairs={{0,192},{96,672},{192,384},{288,96},{384,576},{480,288},{576,0},{6... | collective-permute-start | bytes 393224 | tf_op jit(solution)/shard_map/ppermute | solution.py:282
  20.7 0.1 stack.60
  20.8 0.8 pad_add_fusion.info
  21.5 0.0 collective-permute-done
  21.5 6.9 %collective-permute-start.1 = (f32[128,256]{1,0:T(8,128)S(1)}, f32[128,256]{1,0:T(8,128)S(1)}, u32[]{:S(2)}, u32[]{:S(2)}) collective-permute-start(f32[128,256]{1,0:T(8,128)S(1)} %collective-permute-done), channel_id=1, source_target_pairs={{0,192},{96,672},{192,384},{288,96},{384,576},{480,288},{576,0},{6... | collective-permute-start | bytes 393224 | tf_op jit(solution)/shard_map/ppermute | solution.py:282
  28.5 1.9 %collective-permute-start.7 = (f32[256,256]{1,0:T(8,128)}, f32[256,256]{1,0:T(8,128)S(1)}, u32[]{:S(2)}, u32[]{:S(2)}) collective-permute-start(f32[256,256]{1,0:T(8,128)} %refs_3_.1), channel_id=1, source_target_pairs={{0,96},{96,0},{1,97},{97,1},{2,98},{98,2},{3,99},{99,3},{4,100},{1... | collective-permute-start | bytes 786440 | tf_op jit(solution)/shard_map/ppermute | solution.py:273
  30.4 1.4 collective-permute-done.2
  31.8 4.4 %collective-permute-start.3 = (f32[128,256]{1,0:T(8,128)S(1)}, f32[128,256]{1,0:T(8,128)S(1)}, u32[]{:S(2)}, u32[]{:S(2)}) collective-permute-start(f32[128,256]{1,0:T(8,128)S(1)} %collective-permute-done.2), channel_id=1, source_target_pairs={{0,192},{96,672},{192,384},{288,96},{384,576},{480,288},{576,0},{6... | collective-permute-start | bytes 393224 | tf_op jit(solution)/shard_map/ppermute | solution.py:282
  36.2 7.0 %collective-permute-start.5 = (f32[256,256]{1,0:T(8,128)S(1)}, f32[256,256]{1,0:T(8,128)S(1)}, u32[]{:S(2)}, u32[]{:S(2)}) collective-permute-start(f32[256,256]{1,0:T(8,128)S(1)} %constant_dynamic-update-slice_fusion.2.refs_5_), channel_id=1, source_target_pairs={{0,96},{96,0},{1,97},{97,1},{2,98},{98,2},{3,99},{99,3},{4,100},{1... | collective-permute-start | bytes 786440 | tf_op jit(solution)/shard_map/ppermute | solution.py:273
  43.3 0.0 collective-permute-done.7.refs_4_
  43.3 0.0 copy-start
  43.4 0.9 copy-done
  44.3 2.6 %gather_terms.3 = (f32[256,256]{1,0:T(8,128)S(1)}, f32[256,256]{1,0:T(8,128)S(1)}, f32[256,256]{1,0:T(8,128)S(1)}, f32[256,256]{1,0:T(8,128)S(1)}, f32[256,256]{1,0:T(8,128)S(1)}) custom-call(s32[93]{0:T(128)S(1)} %pad_add_fusion.info, f32[32,128,128]{2,1,0:T(8,128)} %bitcast.28, f32[32,128,128]{2,1,0:T(8,128)} %bitcast.29, f32[32,128,128]{2,1,0:T(8,128)} %bitcast.30, ...), custom_call_target="tpu_custom_call" | custom-call | flops 1024 | bytes 1024 | tf_op jit(solution)/shard_map/gather_terms/pallas_call | solution.py:139
  46.9 0.0 collective-permute-done.6.refs_4_
  47.0 1.9 %collective-permute-start.8 = (f32[256,256]{1,0:T(8,128)S(1)}, f32[256,256]{1,0:T(8,128)S(1)}, u32[]{:S(2)}, u32[]{:S(2)}) collective-permute-start(f32[256,256]{1,0:T(8,128)S(1)} %collective-permute-done.6.refs_4_), channel_id=1, source_target_pairs={{0,96},{96,0},{1,97},{97,1},{2,98},{98,2},{3,99},{99,3},{4,100},{1... | collective-permute-start | bytes 786440 | tf_op jit(solution)/shard_map/ppermute | solution.py:273
  48.9 2.4 %collective-permute-start.4 = (f32[256,256]{1,0:T(8,128)S(1)}, f32[256,256]{1,0:T(8,128)S(1)}, u32[]{:S(2)}, u32[]{:S(2)}) collective-permute-start(f32[256,256]{1,0:T(8,128)S(1)} %constant_dynamic-update-slice_fusion.refs_2_), channel_id=1, source_target_pairs={{0,96},{96,0},{1,97},{97,1},{2,98},{98,2},{3,99},{99,3},{4,100},{1... | collective-permute-start | bytes 786440 | tf_op jit(solution)/shard_map/ppermute | solution.py:273
  51.3 0.0 collective-permute-done.5.refs_3_
  51.3 0.0 collective-permute-done.8.refs_5_
  51.3 2.7 %gather_terms.4 = (f32[256,256]{1,0:T(8,128)S(1)}, f32[256,256]{1,0:T(8,128)S(1)}, f32[256,256]{1,0:T(8,128)S(1)}, f32[256,256]{1,0:T(8,128)S(1)}, f32[256,256]{1,0:T(8,128)S(1)}) custom-call(s32[93]{0:T(128)S(1)} %pad_add_fusion.info, f32[32,128,128]{2,1,0:T(8,128)} %bitcast.31, f32[32,128,128]{2,1,0:T(8,128)} %bitcast.32, f32[32,128,128]{2,1,0:T(8,128)} %bitcast.33, ...), custom_call_target="tpu_custom_call" | custom-call | flops 1024 | bytes 1024 | tf_op jit(solution)/shard_map/gather_terms/pallas_call | solution.py:139
  54.0 0.0 collective-permute-done.4.refs_3_
  54.0 2.4 %gather_terms.5 = (f32[256,256]{1,0:T(8,128)S(1)}, f32[256,256]{1,0:T(8,128)S(1)}, f32[256,256]{1,0:T(8,128)S(1)}, f32[256,256]{1,0:T(8,128)S(1)}, f32[256,256]{1,0:T(8,128)S(1)}) custom-call(s32[93]{0:T(128)S(1)} %pad_add_fusion.info, f32[32,128,128]{2,1,0:T(8,128)} %bitcast.34, f32[32,128,128]{2,1,0:T(8,128)} %bitcast.35, ...), custom_call_target="tpu_custom_call" | custom-call | flops 1024 | bytes 1024 | tf_op jit(solution)/shard_map/gather_terms/pallas_call | solution.py:139
  56.4 0.0 copy-start.1
  56.4 0.0 copy-start.2
  56.5 0.0 copy-start.4
  56.5 5.5 %collective-permute-start.9 = (f32[256,256]{1,0:T(8,128)S(1)}, f32[256,256]{1,0:T(8,128)S(1)}, u32[]{:S(2)}, u32[]{:S(2)}) collective-permute-start(f32[256,256]{1,0:T(8,128)S(1)} %get-tuple-element.74), channel_id=1, source_target_pairs={{0,93},{1,94},{2,5},{3,0},{4,1},{5,8},{6,3},{7,4},{8,11},{9,6},{10... | collective-permute-start | bytes 786440 | tf_op jit(solution)/shard_map/ppermute | solution.py:291
  62.0 3.2 %collective-permute-start.11 = (f32[256,256]{1,0:T(8,128)S(1)}, f32[256,256]{1,0:T(8,128)S(1)}, u32[]{:S(2)}, u32[]{:S(2)}) collective-permute-start(f32[256,256]{1,0:T(8,128)S(1)} %get-tuple-element.76), channel_id=1, source_target_pairs={{0,93},{1,4},{2,5},{3,0},{4,7},{5,8},{6,3},{7,10},{8,11},{9,6},{10... | collective-permute-start | bytes 786440 | tf_op jit(solution)/shard_map/ppermute | solution.py:291
  65.2 3.4 %collective-permute-done.9 = f32[256,256]{1,0:T(8,128)S(1)} collective-permute-done((f32[256,256]{1,0:T(8,128)S(1)}, f32[256,256]{1,0:T(8,128)S(1)}, u32[]{:S(2)}, u32[]{:S(2)}) %collective-permute-start.9) | collective-permute-done | bytes 262176 | tf_op jit(solution)/shard_map/ppermute | solution.py:291
  68.7 1.9 %collective-permute-start.10 = (f32[256,256]{1,0:T(8,128)S(1)}, f32[256,256]{1,0:T(8,128)S(1)}, u32[]{:S(2)}, u32[]{:S(2)}) collective-permute-start(f32[256,256]{1,0:T(8,128)S(1)} %add.76), channel_id=1, source_target_pairs={{0,1},{1,2},{2,0},{3,4},{4,5},{5,3},{6,7},{7,8},{8,6},{9,10},{10,1... | collective-permute-start | bytes 786440 | tf_op jit(solution)/shard_map/ppermute | solution.py:286
  70.6 2.7 %collective-permute-done.11 = f32[256,256]{1,0:T(8,128)S(1)} collective-permute-done((f32[256,256]{1,0:T(8,128)S(1)}, f32[256,256]{1,0:T(8,128)S(1)}, u32[]{:S(2)}, u32[]{:S(2)}) %collective-permute-start.11) | collective-permute-done | bytes 262176 | tf_op jit(solution)/shard_map/ppermute | solution.py:291
  73.3 4.2 %collective-permute-start.12 = (f32[256,256]{1,0:T(8,128)S(1)}, f32[256,256]{1,0:T(8,128)S(1)}, u32[]{:S(2)}, u32[]{:S(2)}) collective-permute-start(f32[256,256]{1,0:T(8,128)S(1)} %add.77), channel_id=1, source_target_pairs={{0,2},{1,0},{2,1},{3,5},{4,3},{5,4},{6,8},{7,6},{8,7},{9,11},{10,9... | collective-permute-start | bytes 786440 | tf_op jit(solution)/shard_map/ppermute | solution.py:286
  77.6 7.1 %place_tiles.1 = (bf16[8,256,512]{2,1,0:T(8,128)(2,1)}, bf16[8,256,512]{2,1,0:T(8,128)(2,1)}) custom-call(s32[93]{0:T(128)S(1)} %pad_add_fusion.info, f32[32,128,128]{2,1,0:T(8,128)} %bitcast.36), custom_call_target="tpu_custom_call" | custom-call | bytes 6291456 | tf_op jit(solution)/shard_map/place_tiles/pallas_call | solution.py:76
  84.7 0.0 collective-permute-done.10.refs_0_
  84.7 0.0 collective-permute-done.12.refs_1_
  84.7 1.2 dense.1
  85.9 1.9 %collective-permute-start.14 = (f32[256,256]{1,0:T(8,128)S(1)}, f32[256,256]{1,0:T(8,128)S(1)}, u32[]{:S(2)}, u32[]{:S(2)}) collective-permute-start(f32[256,256]{1,0:T(8,128)S(1)} %get-tuple-element.84.refs_8_), channel_id=1, source_target_pairs={{0,1},{1,2},{2,0},{3,4},{4,5},{5,3},{6,7},{7,8},{8,6},{9,10},{10,1... | collective-permute-start | bytes 786440 | tf_op jit(solution)/shard_map/ppermute | solution.py:286
  87.8 4.8 %collective-permute-start.13 = (f32[256,256]{1,0:T(8,128)S(1)}, f32[256,256]{1,0:T(8,128)S(1)}, u32[]{:S(2)}, u32[]{:S(2)}) collective-permute-start(f32[256,256]{1,0:T(8,128)S(1)} %get-tuple-element.84.refs_8_), channel_id=1, source_target_pairs={{0,2},{1,0},{2,1},{3,5},{4,3},{5,4},{6,8},{7,6},{8,7},{9,11},{10,9... | collective-permute-start | bytes 786440 | tf_op jit(solution)/shard_map/ppermute | solution.py:286
  92.7 1.0 weight_terms.1
  93.7 9.8 %all-to-all-start = ((f32[32,8,256]{2,1,0:T(8,128)}), f32[32,8,256]{2,1,0:T(8,128)S(1)}, u32[]{:S(2)}, u32[]{:S(2)}) async-start(f32[32,8,256]{2,1,0:T(8,128)} %bitcast.37), calls=%async_computation | async-start | bytes 524288 | tf_op jit(solution)/shard_map/all_to_all | solution.py:295
  103.5 0.0 collective-permute-done.14.refs_10_
  103.5 3.4 %collective-permute-start.15 = (f32[256,256]{1,0:T(8,128)S(1)}, f32[256,256]{1,0:T(8,128)S(1)}, u32[]{:S(2)}, u32[]{:S(2)}) collective-permute-start(f32[256,256]{1,0:T(8,128)S(1)} %collective-permute-done.13.refs_9_), channel_id=1, source_target_pairs={{0,3},{1,4},{2,95},{3,6},{4,7},{5,2},{6,9},{7,10},{8,5},{9,12},{10... | collective-permute-start | bytes 786440 | tf_op jit(solution)/shard_map/ppermute | solution.py:291
  106.9 3.4 %collective-permute-start.16 = (f32[256,256]{1,0:T(8,128)S(1)}, f32[256,256]{1,0:T(8,128)S(1)}, u32[]{:S(2)}, u32[]{:S(2)}) collective-permute-start(f32[256,256]{1,0:T(8,128)S(1)} %collective-permute-done.14.refs_10_), channel_id=1, source_target_pairs={{0,3},{1,94},{2,95},{3,6},{4,1},{5,2},{6,9},{7,4},{8,5},{9,12},{10... | collective-permute-start | bytes 786440 | tf_op jit(solution)/shard_map/ppermute | solution.py:291
  110.2 4.6 %all-to-all-done.parts = f32[32,8,256]{2,1,0:T(8,128)S(1)} async-done(((f32[32,8,256]{2,1,0:T(8,128)}), f32[32,8,256]{2,1,0:T(8,128)S(1)}, u32[]{:S(2)}, u32[]{:S(2)}) %all-to-all-start) | async-done | bytes 262176 | tf_op jit(solution)/shard_map/all_to_all | solution.py:295
  114.8 0.7 copy-done.3
  115.5 0.8 sum_and_copy.2
  116.3 7.8 %all-to-all-start.1 = ((f32[24,8,384]{2,1,0:T(8,128)}), f32[24,8,384]{2,1,0:T(8,128)}, u32[]{:S(2)}, u32[]{:S(2)}) async-start(f32[24,8,384]{2,1,0:T(8,128)} %sum_and_copy.2), calls=%async_computation.1 | async-start | bytes 589824 | tf_op jit(solution)/shard_map/all_to_all | solution.py:295
  124.1 0.0 collective-permute-done.16.refs_12_
  124.2 4.3 %spread_terms.3 = f32[4,256,256]{2,1,0:T(8,128)} custom-call(s32[93]{0:T(128)S(1)} %pad_add_fusion.info, bf16[8,256,512]{2,1,0:T(8,128)(2,1)} %get-tuple-element.82.refs_0_.refs_1_.refs_2_.refs_3_, bf16[8,256,512]{2,1,0:T(8,128)(2,1)} %get-tuple-element.82.refs_0_.refs_1_.refs_2_.refs_3_, ...), custom_call_target="tpu_custom_call" | custom-call | flops 1099511627776 | bytes 4294967296 | tf_op jit(solution)/shard_map/spread_terms/pallas_call | solution.py:230
  128.4 2.2 %collective-permute-start.17 = (f32[4,256,256]{2,1,0:T(8,128)}, f32[4,256,256]{2,1,0:T(8,128)}, u32[]{:S(2)}, u32[]{:S(2)}) collective-permute-start(f32[4,256,256]{2,1,0:T(8,128)} %spread_terms.3), channel_id=1, source_target_pairs={{0,96},{96,0},{1,97},{97,1},{2,98},{98,2},{3,99},{99,3},{4,100},{1... | collective-permute-start | bytes 3145736 | tf_op jit(solution)/shard_map/ppermute | solution.py:273
  130.6 4.0 %spread_terms.2 = (f32[256,256]{1,0:T(8,128)}, f32[256,256]{1,0:T(8,128)}, f32[256,256]{1,0:T(8,128)}, f32[256,256]{1,0:T(8,128)}) custom-call(s32[93]{0:T(128)S(1)} %pad_add_fusion.info, bf16[8,256,512]{2,1,0:T(8,128)(2,1)} %get-tuple-element.82.refs_0_.refs_1_.refs_2_.refs_3_, bf16[8,256,512]{2,1,0:T(8,128)(2,1)} %get-tuple-element.82.refs_0_.refs_1_.refs_2_.refs_3_, ...), custom_call_target="tpu_custom_call" | custom-call | flops 1099511627776 | bytes 4294967296 | tf_op jit(solution)/shard_map/spread_terms/pallas_call | solution.py:230
  134.6 1.3 fusion
  136.0 5.4 %collective-permute-start.19 = (f32[256,256]{1,0:T(8,128)S(1)}, f32[256,256]{1,0:T(8,128)S(1)}, u32[]{:S(2)}, u32[]{:S(2)}) collective-permute-start(f32[256,256]{1,0:T(8,128)S(1)} %get-tuple-element.102), channel_id=1, source_target_pairs={{0,192},{96,672},{192,384},{288,96},{384,576},{480,288},{576,0},{6... | collective-permute-start | bytes 786440 | tf_op jit(solution)/shard_map/ppermute | solution.py:282
  141.3 3.5 %collective-permute-start.18 = (f32[256,256]{1,0:T(8,128)S(1)}, f32[256,256]{1,0:T(8,128)S(1)}, u32[]{:S(2)}, u32[]{:S(2)}) collective-permute-start(f32[256,256]{1,0:T(8,128)S(1)} %get-tuple-element.103), channel_id=1, source_target_pairs={{0,576},{96,288},{192,0},{288,480},{384,192},{480,672},{576,384},{... | collective-permute-start | bytes 786440 | tf_op jit(solution)/shard_map/ppermute | solution.py:282
  144.8 1.8 sum_and_copy.3
  146.6 5.9 %all-to-all-start.2 = ((f32[32,8,384]{2,1,0:T(8,128)}), f32[32,8,384]{2,1,0:T(8,128)}, u32[]{:S(2)}, u32[]{:S(2)}) async-start(f32[32,8,384]{2,1,0:T(8,128)} %sum_and_copy.3), calls=%async_computation.2 | async-start | bytes 786432 | tf_op jit(solution)/shard_map/all_to_all | solution.py:295
  152.5 1.1 collective-permute-done.19.second
  153.6 6.4 %collective-permute-done.18.far = f32[256,256]{1,0:T(8,128)S(1)} collective-permute-done((f32[256,256]{1,0:T(8,128)S(1)}, f32[256,256]{1,0:T(8,128)S(1)}, u32[]{:S(2)}, u32[]{:S(2)}) %collective-permute-start.18) | collective-permute-done | bytes 262176 | tf_op jit(solution)/shard_map/ppermute | solution.py:282
  159.9 1.1 turn_terms.1
  161.0 7.3 %collective-permute-start.20 = (f32[256,256]{1,0:T(8,128)S(1)}, f32[256,256]{1,0:T(8,128)S(1)}, u32[]{:S(2)}, u32[]{:S(2)}) collective-permute-start(f32[256,256]{1,0:T(8,128)S(1)} %get-tuple-element.99), channel_id=1, source_target_pairs={{0,576},{96,288},{192,0},{288,480},{384,192},{480,672},{576,384},{... | collective-permute-start | bytes 786440 | tf_op jit(solution)/shard_map/ppermute | solution.py:282
  168.4 1.7 read_sums.1
  170.1 7.1 %collective-permute-done.20 = f32[256,256]{1,0:T(8,128)S(1)} collective-permute-done((f32[256,256]{1,0:T(8,128)S(1)}, f32[256,256]{1,0:T(8,128)S(1)}, u32[]{:S(2)}, u32[]{:S(2)}) %collective-permute-start.20) | collective-permute-done | bytes 262176 | tf_op jit(solution)/shard_map/ppermute | solution.py:282
  177.2 0.7 add.80
  (21 shorter events, 0.1 us)
Async XLA Ops:
  1.6 19.9 %collective-permute-start = (f32[128,256]{1,0:T(8,128)S(1)}, f32[128,256]{1,0:T(8,128)S(1)}, u32[]{:S(2)}, u32[]{:S(2)}) collective-permute-start(f32[128,256]{1,0:T(8,128)S(1)} %get-tuple-element.105), channel_id=1, source_target_pairs={{0,192},{96,672},{192,384},{288,96},{384,576},{480,288},{576,0},{6... | collective-permute-start | bytes 393224 | tf_op jit(solution)/shard_map/ppermute | solution.py:282
  9.5 37.4 %collective-permute-start.6 = (f32[256,256]{1,0:T(8,128)}, f32[256,256]{1,0:T(8,128)S(1)}, u32[]{:S(2)}, u32[]{:S(2)}) collective-permute-start(f32[256,256]{1,0:T(8,128)} %refs_3_.1), channel_id=1, source_target_pairs={{0,576},{96,288},{192,0},{288,480},{384,192},{480,672},{576,384},{... | collective-permute-start | bytes 786440 | tf_op jit(solution)/shard_map/ppermute | solution.py:282
  18.1 13.7 %collective-permute-start.2 = (f32[128,256]{1,0:T(8,128)S(1)}, f32[128,256]{1,0:T(8,128)S(1)}, u32[]{:S(2)}, u32[]{:S(2)}) collective-permute-start(f32[128,256]{1,0:T(8,128)S(1)} %get-tuple-element.104), channel_id=1, source_target_pairs={{0,192},{96,672},{192,384},{288,96},{384,576},{480,288},{576,0},{6... | collective-permute-start | bytes 393224 | tf_op jit(solution)/shard_map/ppermute | solution.py:282
  21.5 21.8 %collective-permute-start.1 = (f32[128,256]{1,0:T(8,128)S(1)}, f32[128,256]{1,0:T(8,128)S(1)}, u32[]{:S(2)}, u32[]{:S(2)}) collective-permute-start(f32[128,256]{1,0:T(8,128)S(1)} %collective-permute-done), channel_id=1, source_target_pairs={{0,192},{96,672},{192,384},{288,96},{384,576},{480,288},{576,0},{6... | collective-permute-start | bytes 393224 | tf_op jit(solution)/shard_map/ppermute | solution.py:282
  28.5 14.9 %collective-permute-start.7 = (f32[256,256]{1,0:T(8,128)}, f32[256,256]{1,0:T(8,128)S(1)}, u32[]{:S(2)}, u32[]{:S(2)}) collective-permute-start(f32[256,256]{1,0:T(8,128)} %refs_3_.1), channel_id=1, source_target_pairs={{0,96},{96,0},{1,97},{97,1},{2,98},{98,2},{3,99},{99,3},{4,100},{1... | collective-permute-start | bytes 786440 | tf_op jit(solution)/shard_map/ppermute | solution.py:273
  31.8 17.1 %collective-permute-start.3 = (f32[128,256]{1,0:T(8,128)S(1)}, f32[128,256]{1,0:T(8,128)S(1)}, u32[]{:S(2)}, u32[]{:S(2)}) collective-permute-start(f32[128,256]{1,0:T(8,128)S(1)} %collective-permute-done.2), channel_id=1, source_target_pairs={{0,192},{96,672},{192,384},{288,96},{384,576},{480,288},{576,0},{6... | collective-permute-start | bytes 393224 | tf_op jit(solution)/shard_map/ppermute | solution.py:282
  36.2 15.1 %collective-permute-start.5 = (f32[256,256]{1,0:T(8,128)S(1)}, f32[256,256]{1,0:T(8,128)S(1)}, u32[]{:S(2)}, u32[]{:S(2)}) collective-permute-start(f32[256,256]{1,0:T(8,128)S(1)} %constant_dynamic-update-slice_fusion.2.refs_5_), channel_id=1, source_target_pairs={{0,96},{96,0},{1,97},{97,1},{2,98},{98,2},{3,99},{99,3},{4,100},{1... | collective-permute-start | bytes 786440 | tf_op jit(solution)/shard_map/ppermute | solution.py:273
  43.3 1.0 copy-start
  47.0 4.4 %collective-permute-start.8 = (f32[256,256]{1,0:T(8,128)S(1)}, f32[256,256]{1,0:T(8,128)S(1)}, u32[]{:S(2)}, u32[]{:S(2)}) collective-permute-start(f32[256,256]{1,0:T(8,128)S(1)} %collective-permute-done.6.refs_4_), channel_id=1, source_target_pairs={{0,96},{96,0},{1,97},{97,1},{2,98},{98,2},{3,99},{99,3},{4,100},{1... | collective-permute-start | bytes 786440 | tf_op jit(solution)/shard_map/ppermute | solution.py:273
  48.9 5.1 %collective-permute-start.4 = (f32[256,256]{1,0:T(8,128)S(1)}, f32[256,256]{1,0:T(8,128)S(1)}, u32[]{:S(2)}, u32[]{:S(2)}) collective-permute-start(f32[256,256]{1,0:T(8,128)S(1)} %constant_dynamic-update-slice_fusion.refs_2_), channel_id=1, source_target_pairs={{0,96},{96,0},{1,97},{97,1},{2,98},{98,2},{3,99},{99,3},{4,100},{1... | collective-permute-start | bytes 786440 | tf_op jit(solution)/shard_map/ppermute | solution.py:273
  56.4 28.2 %copy-start.1 = (f32[256,256]{1,0:T(8,128)S(1)}, f32[256,256]{1,0:T(8,128)}, u32[]{:S(2)}) copy-start(f32[256,256]{1,0:T(8,128)} %refs_2_.1) | copy-start | bytes 786436
  56.4 28.2 %copy-start.2 = (f32[256,256]{1,0:T(8,128)S(1)}, f32[256,256]{1,0:T(8,128)}, u32[]{:S(2)}) copy-start(f32[256,256]{1,0:T(8,128)} %refs_4_.1) | copy-start | bytes 786436
  56.5 28.2 %copy-start.4 = (f32[256]{0:T(256)S(1)}, f32[256]{0:T(256)}, u32[]{:S(2)}) copy-start(f32[256]{0:T(256)} %param.10) | copy-start | bytes 3076
  56.5 12.2 %collective-permute-start.9 = (f32[256,256]{1,0:T(8,128)S(1)}, f32[256,256]{1,0:T(8,128)S(1)}, u32[]{:S(2)}, u32[]{:S(2)}) collective-permute-start(f32[256,256]{1,0:T(8,128)S(1)} %get-tuple-element.74), channel_id=1, source_target_pairs={{0,93},{1,94},{2,5},{3,0},{4,1},{5,8},{6,3},{7,4},{8,11},{9,6},{10... | collective-permute-start | bytes 786440 | tf_op jit(solution)/shard_map/ppermute | solution.py:291
  62.0 11.3 %collective-permute-start.11 = (f32[256,256]{1,0:T(8,128)S(1)}, f32[256,256]{1,0:T(8,128)S(1)}, u32[]{:S(2)}, u32[]{:S(2)}) collective-permute-start(f32[256,256]{1,0:T(8,128)S(1)} %get-tuple-element.76), channel_id=1, source_target_pairs={{0,93},{1,4},{2,5},{3,0},{4,7},{5,8},{6,3},{7,10},{8,11},{9,6},{10... | collective-permute-start | bytes 786440 | tf_op jit(solution)/shard_map/ppermute | solution.py:291
  68.7 16.0 %collective-permute-start.10 = (f32[256,256]{1,0:T(8,128)S(1)}, f32[256,256]{1,0:T(8,128)S(1)}, u32[]{:S(2)}, u32[]{:S(2)}) collective-permute-start(f32[256,256]{1,0:T(8,128)S(1)} %add.76), channel_id=1, source_target_pairs={{0,1},{1,2},{2,0},{3,4},{4,5},{5,3},{6,7},{7,8},{8,6},{9,10},{10,1... | collective-permute-start | bytes 786440 | tf_op jit(solution)/shard_map/ppermute | solution.py:286
  73.3 11.3 %collective-permute-start.12 = (f32[256,256]{1,0:T(8,128)S(1)}, f32[256,256]{1,0:T(8,128)S(1)}, u32[]{:S(2)}, u32[]{:S(2)}) collective-permute-start(f32[256,256]{1,0:T(8,128)S(1)} %add.77), channel_id=1, source_target_pairs={{0,2},{1,0},{2,1},{3,5},{4,3},{5,4},{6,8},{7,6},{8,7},{9,11},{10,9... | collective-permute-start | bytes 786440 | tf_op jit(solution)/shard_map/ppermute | solution.py:286
  85.9 17.5 %collective-permute-start.14 = (f32[256,256]{1,0:T(8,128)S(1)}, f32[256,256]{1,0:T(8,128)S(1)}, u32[]{:S(2)}, u32[]{:S(2)}) collective-permute-start(f32[256,256]{1,0:T(8,128)S(1)} %get-tuple-element.84.refs_8_), channel_id=1, source_target_pairs={{0,1},{1,2},{2,0},{3,4},{4,5},{5,3},{6,7},{7,8},{8,6},{9,10},{10,1... | collective-permute-start | bytes 786440 | tf_op jit(solution)/shard_map/ppermute | solution.py:286
  87.8 15.6 %collective-permute-start.13 = (f32[256,256]{1,0:T(8,128)S(1)}, f32[256,256]{1,0:T(8,128)S(1)}, u32[]{:S(2)}, u32[]{:S(2)}) collective-permute-start(f32[256,256]{1,0:T(8,128)S(1)} %get-tuple-element.84.refs_8_), channel_id=1, source_target_pairs={{0,2},{1,0},{2,1},{3,5},{4,3},{5,4},{6,8},{7,6},{8,7},{9,11},{10,9... | collective-permute-start | bytes 786440 | tf_op jit(solution)/shard_map/ppermute | solution.py:286
  93.7 21.1 %all-to-all-start = ((f32[32,8,256]{2,1,0:T(8,128)}), f32[32,8,256]{2,1,0:T(8,128)S(1)}, u32[]{:S(2)}, u32[]{:S(2)}) async-start(f32[32,8,256]{2,1,0:T(8,128)} %bitcast.37), calls=%async_computation | async-start | bytes 524288 | tf_op jit(solution)/shard_map/all_to_all | solution.py:295
  103.5 20.6 %collective-permute-start.15 = (f32[256,256]{1,0:T(8,128)S(1)}, f32[256,256]{1,0:T(8,128)S(1)}, u32[]{:S(2)}, u32[]{:S(2)}) collective-permute-start(f32[256,256]{1,0:T(8,128)S(1)} %collective-permute-done.13.refs_9_), channel_id=1, source_target_pairs={{0,3},{1,4},{2,95},{3,6},{4,7},{5,2},{6,9},{7,10},{8,5},{9,12},{10... | collective-permute-start | bytes 786440 | tf_op jit(solution)/shard_map/ppermute | solution.py:291
  106.9 17.3 %collective-permute-start.16 = (f32[256,256]{1,0:T(8,128)S(1)}, f32[256,256]{1,0:T(8,128)S(1)}, u32[]{:S(2)}, u32[]{:S(2)}) collective-permute-start(f32[256,256]{1,0:T(8,128)S(1)} %collective-permute-done.14.refs_10_), channel_id=1, source_target_pairs={{0,3},{1,94},{2,95},{3,6},{4,1},{5,2},{6,9},{7,4},{8,5},{9,12},{10... | collective-permute-start | bytes 786440 | tf_op jit(solution)/shard_map/ppermute | solution.py:291
  114.8 0.7 copy-start.3
  116.3 28.5 %all-to-all-start.1 = ((f32[24,8,384]{2,1,0:T(8,128)}), f32[24,8,384]{2,1,0:T(8,128)}, u32[]{:S(2)}, u32[]{:S(2)}) async-start(f32[24,8,384]{2,1,0:T(8,128)} %sum_and_copy.2), calls=%async_computation.1 | async-start | bytes 589824 | tf_op jit(solution)/shard_map/all_to_all | solution.py:295
  128.4 6.2 %collective-permute-start.17 = (f32[4,256,256]{2,1,0:T(8,128)}, f32[4,256,256]{2,1,0:T(8,128)}, u32[]{:S(2)}, u32[]{:S(2)}) collective-permute-start(f32[4,256,256]{2,1,0:T(8,128)} %spread_terms.3), channel_id=1, source_target_pairs={{0,96},{96,0},{1,97},{97,1},{2,98},{98,2},{3,99},{99,3},{4,100},{1... | collective-permute-start | bytes 3145736 | tf_op jit(solution)/shard_map/ppermute | solution.py:273
  134.6 25.3 %copy-start.5 = (f32[256,256]{1,0:T(8,128)S(1)}, f32[256,256]{1,0:T(8,128)}, u32[]{:S(2)}) copy-start(f32[256,256]{1,0:T(8,128)} %get-tuple-element.90.kept_first) | copy-start | bytes 786436
  134.6 25.3 %copy-start.6 = (f32[256,256]{1,0:T(8,128)S(1)}, f32[256,256]{1,0:T(8,128)}, u32[]{:S(2)}) copy-start(f32[256,256]{1,0:T(8,128)} %get-tuple-element.92.kept) | copy-start | bytes 786436
  136.0 17.6 %collective-permute-start.19 = (f32[256,256]{1,0:T(8,128)S(1)}, f32[256,256]{1,0:T(8,128)S(1)}, u32[]{:S(2)}, u32[]{:S(2)}) collective-permute-start(f32[256,256]{1,0:T(8,128)S(1)} %get-tuple-element.102), channel_id=1, source_target_pairs={{0,192},{96,672},{192,384},{288,96},{384,576},{480,288},{576,0},{6... | collective-permute-start | bytes 786440 | tf_op jit(solution)/shard_map/ppermute | solution.py:282
  141.3 18.6 %collective-permute-start.18 = (f32[256,256]{1,0:T(8,128)S(1)}, f32[256,256]{1,0:T(8,128)S(1)}, u32[]{:S(2)}, u32[]{:S(2)}) collective-permute-start(f32[256,256]{1,0:T(8,128)S(1)} %get-tuple-element.103), channel_id=1, source_target_pairs={{0,576},{96,288},{192,0},{288,480},{384,192},{480,672},{576,384},{... | collective-permute-start | bytes 786440 | tf_op jit(solution)/shard_map/ppermute | solution.py:282
  146.6 21.8 %all-to-all-start.2 = ((f32[32,8,384]{2,1,0:T(8,128)}), f32[32,8,384]{2,1,0:T(8,128)}, u32[]{:S(2)}, u32[]{:S(2)}) async-start(f32[32,8,384]{2,1,0:T(8,128)} %sum_and_copy.3), calls=%async_computation.2 | async-start | bytes 786432 | tf_op jit(solution)/shard_map/all_to_all | solution.py:295
  161.0 16.1 %collective-permute-start.20 = (f32[256,256]{1,0:T(8,128)S(1)}, f32[256,256]{1,0:T(8,128)S(1)}, u32[]{:S(2)}, u32[]{:S(2)}) collective-permute-start(f32[256,256]{1,0:T(8,128)S(1)} %get-tuple-element.99), channel_id=1, source_target_pairs={{0,576},{96,288},{192,0},{288,480},{384,192},{480,672},{576,384},{... | collective-permute-start | bytes 786440 | tf_op jit(solution)/shard_map/ppermute | solution.py:282

commit v4 on v3

--- a/solution.py
+++ b/solution.py
@@ -16,6 +16,7 @@
 COLUMN_BLOCKS = Z_HI * CORE
 PER_BLOCK = 4
 TILE = 128
+PLACED = 2
 ROWS = 256
 H = 256
 NODES = 196608
@@ -60,25 +61,26 @@
 
 
 def place_kernel(info, tiles, high, low):
-    block = pl.program_id(0)
-    for slot in range(PER_BLOCK):
-        column, live = column_and_live(info, block, slot)
-        tile = jnp.where(live, tiles[slot], 0.0).T
-        span = pl.ds(slot * TILE, TILE)
-        for half in range(ROWS // TILE):
-            half_span = pl.ds(half * TILE, TILE)
-            high[0, half_span, span], low[0, half_span, span] = split(jnp.where(column == half, tile, 0.0))
+    for j in range(PLACED):
+        block = pl.program_id(0) * PLACED + j
+        for slot in range(PER_BLOCK):
+            column, live = column_and_live(info, block, slot)
+            tile = jnp.where(live, tiles[j * PER_BLOCK + slot], 0.0).T
+            span = pl.ds(slot * TILE, TILE)
+            for half in range(ROWS // TILE):
+                half_span = pl.ds(half * TILE, TILE)
+                high[j, half_span, span], low[j, half_span, span] = split(jnp.where(column == half, tile, 0.0))
 
 
 def place_tiles(info, tiles):
     shape = (ROWS, PER_BLOCK * TILE)
-    spec = pl.BlockSpec((1,) + shape, lambda i, *_: (i, 0, 0))
+    spec = pl.BlockSpec((PLACED,) + shape, lambda i, *_: (i, 0, 0))
     return pl.pallas_call(
         place_kernel,
         grid_spec=pltpu.PrefetchScalarGridSpec(
             num_scalar_prefetch=1,
-            grid=(COLUMN_BLOCKS,),
-            in_specs=[pl.BlockSpec((PER_BLOCK, TILE, TILE), lambda i, *_: (i, 0, 0))],
+            grid=(COLUMN_BLOCKS // PLACED,),
+            in_specs=[pl.BlockSpec((PLACED * PER_BLOCK, TILE, TILE), lambda i, *_: (i, 0, 0))],
             out_specs=[spec, spec],
         ),
         out_shape=[pltpu.HBM((COLUMN_BLOCKS,) + shape, jnp.bfloat16)] * 2,
@@ -196,7 +198,7 @@
         weight_kernel,
         out_shape=[
             pltpu.HBM((H, H), jnp.float32),
-            pltpu.HBM((PART, 128), jnp.float32),
+            jax.ShapeDtypeStruct((PART, 128), jnp.float32),
         ],
         compiler_params=params(),
         cost_estimate=cost(6 * 256 * 256 * 256, 3 * 256 * 1024),
@@ -386,7 +388,7 @@
     field_first = jnp.concatenate([first_upper, first_lower])
     field_far = jnp.concatenate([far_upper, far_lower])
     other_first = other_core(field_first)
-    terms = gather_terms(GATHER_NEAR, info, tile_values[0], (features, field_other, field_first))
+    terms = gather_terms(GATHER_NEAR, info, tile_values[0], (in_hbm(features), field_other, field_first))
     far_upper, field_second, *terms = after(far_upper, field_second, *terms)
     other_second = other_core(field_second)
     other_far = other_core(field_far)

time: 179 us -> 178 us (level)
  the two profiles are of different devices: /device:TPU:2 before, /device:TPU:8 now
where the time goes in v4:
time: 178 us; the launch traced here: 177 us
  starting transfers between devices  117 us (66%)
  Pallas kernels  28.9 us (16%)
  waiting for transfers between devices  25.8 us (14%)
  other arithmetic  2.89 us (2%)
    ppermute x8, starting transfers between devices, along_loop(): return lax.ppermute(value, LOOP, pairs)  46.4 us
    all_to_all x3, starting transfers between devices, swap(): return lax.all_to_all(value, axes, 0, 0, tiled=True)  25.7 us
    ppermute x4, starting transfers between devices, across_triples(): return lax.ppermute(value, REP, pairs)  16.8 us
    ppermute x8, waiting for transfers between devices, along_loop(): return lax.ppermute(value, LOOP, pairs)  16.3 us
    ppermute x5, starting transfers between devices, other_core(): return lax.ppermute(value, 'core', [(0, 1), (1, 0)])  15.5 us
    ppermute x4, starting transfers between devices, in_triple(): lax.ppermute(value, 'z_lo', [(i, (i + by) % Z_LO) for i in range(Z_LO)])  12.4 us
    pallas_call x2, Pallas kernels, spread_terms(): pl.pallas_call(functools.partial(spread_kernel, at, n), grid_spec=pltpu.P...  8.33 us
    pallas_call x3, Pallas kernels, gather_terms(): pl.pallas_call(functools.partial(gather_kernel, n, len(before), at), grid...  7.79 us
  transfers between devices with their start and end apart: 24, of which 8 were waited for; matrix products, arithmetic and copies ran while one was open for 1% of the time, Pallas kernels for 14%

profile of v4, /device:TPU:8, one launch (start us, length us, event | category | flops | bytes accessed | tf_op | source)
XLA Modules:
  0.0 176.8 jit_solution(16583596922662912319)
XLA Ops:
  0.6 1.0 fusion.2
  1.6 7.9 %collective-permute-start = (f32[128,256]{1,0:T(8,128)S(1)}, f32[128,256]{1,0:T(8,128)S(1)}, u32[]{:S(2)}, u32[]{:S(2)}) collective-permute-start(f32[128,256]{1,0:T(8,128)S(1)} %get-tuple-element.105), channel_id=1, source_target_pairs={{0,192},{96,672},{192,384},{288,96},{384,576},{480,288},{576,0},{6... | collective-permute-start | bytes 393224 | tf_op jit(solution)/shard_map/ppermute | solution.py:284
  9.5 8.6 %collective-permute-start.6 = (f32[256,256]{1,0:T(8,128)}, f32[256,256]{1,0:T(8,128)S(1)}, u32[]{:S(2)}, u32[]{:S(2)}) collective-permute-start(f32[256,256]{1,0:T(8,128)} %refs_3_.1), channel_id=1, source_target_pairs={{0,576},{96,288},{192,0},{288,480},{384,192},{480,672},{576,384},{... | collective-permute-start | bytes 786440 | tf_op jit(solution)/shard_map/ppermute | solution.py:284
  18.1 2.4 %collective-permute-start.2 = (f32[128,256]{1,0:T(8,128)S(1)}, f32[128,256]{1,0:T(8,128)S(1)}, u32[]{:S(2)}, u32[]{:S(2)}) collective-permute-start(f32[128,256]{1,0:T(8,128)S(1)} %get-tuple-element.104), channel_id=1, source_target_pairs={{0,192},{96,672},{192,384},{288,96},{384,576},{480,288},{576,0},{6... | collective-permute-start | bytes 393224 | tf_op jit(solution)/shard_map/ppermute | solution.py:284
  20.7 0.1 stack.60
  20.8 0.8 pad_add_fusion.info
  21.5 6.9 %collective-permute-start.1 = (f32[128,256]{1,0:T(8,128)S(1)}, f32[128,256]{1,0:T(8,128)S(1)}, u32[]{:S(2)}, u32[]{:S(2)}) collective-permute-start(f32[128,256]{1,0:T(8,128)S(1)} %collective-permute-done), channel_id=1, source_target_pairs={{0,192},{96,672},{192,384},{288,96},{384,576},{480,288},{576,0},{6... | collective-permute-start | bytes 393224 | tf_op jit(solution)/shard_map/ppermute | solution.py:284
  28.5 1.9 %collective-permute-start.7 = (f32[256,256]{1,0:T(8,128)}, f32[256,256]{1,0:T(8,128)S(1)}, u32[]{:S(2)}, u32[]{:S(2)}) collective-permute-start(f32[256,256]{1,0:T(8,128)} %refs_3_.1), channel_id=1, source_target_pairs={{0,96},{96,0},{1,97},{97,1},{2,98},{98,2},{3,99},{99,3},{4,100},{1... | collective-permute-start | bytes 786440 | tf_op jit(solution)/shard_map/ppermute | solution.py:275
  30.4 1.4 collective-permute-done.2
  31.8 4.4 %collective-permute-start.3 = (f32[128,256]{1,0:T(8,128)S(1)}, f32[128,256]{1,0:T(8,128)S(1)}, u32[]{:S(2)}, u32[]{:S(2)}) collective-permute-start(f32[128,256]{1,0:T(8,128)S(1)} %collective-permute-done.2), channel_id=1, source_target_pairs={{0,192},{96,672},{192,384},{288,96},{384,576},{480,288},{576,0},{6... | collective-permute-start | bytes 393224 | tf_op jit(solution)/shard_map/ppermute | solution.py:284
  36.2 7.0 %collective-permute-start.5 = (f32[256,256]{1,0:T(8,128)S(1)}, f32[256,256]{1,0:T(8,128)S(1)}, u32[]{:S(2)}, u32[]{:S(2)}) collective-permute-start(f32[256,256]{1,0:T(8,128)S(1)} %constant_dynamic-update-slice_fusion.2.refs_5_), channel_id=1, source_target_pairs={{0,96},{96,0},{1,97},{97,1},{2,98},{98,2},{3,99},{99,3},{4,100},{1... | collective-permute-start | bytes 786440 | tf_op jit(solution)/shard_map/ppermute | solution.py:275
  43.3 0.0 collective-permute-done.1
  43.3 0.0 collective-permute-done.7.refs_4_
  43.3 2.7 %gather_terms.3 = (f32[256,256]{1,0:T(8,128)S(1)}, f32[256,256]{1,0:T(8,128)S(1)}, f32[256,256]{1,0:T(8,128)S(1)}, f32[256,256]{1,0:T(8,128)S(1)}, f32[256,256]{1,0:T(8,128)S(1)}) custom-call(s32[93]{0:T(128)S(1)} %pad_add_fusion.info, f32[32,128,128]{2,1,0:T(8,128)} %bitcast.28, f32[32,128,128]{2,1,0:T(8,128)} %bitcast.29, f32[32,128,128]{2,1,0:T(8,128)} %bitcast.30, ...), custom_call_target="tpu_custom_call" | custom-call | flops 1024 | bytes 1024 | tf_op jit(solution)/shard_map/gather_terms/pallas_call | solution.py:141
  46.1 0.0 collective-permute-done.6.refs_4_
  46.1 1.9 %collective-permute-start.8 = (f32[256,256]{1,0:T(8,128)S(1)}, f32[256,256]{1,0:T(8,128)S(1)}, u32[]{:S(2)}, u32[]{:S(2)}) collective-permute-start(f32[256,256]{1,0:T(8,128)S(1)} %collective-permute-done.6.refs_4_), channel_id=1, source_target_pairs={{0,96},{96,0},{1,97},{97,1},{2,98},{98,2},{3,99},{99,3},{4,100},{1... | collective-permute-start | bytes 786440 | tf_op jit(solution)/shard_map/ppermute | solution.py:275
  48.0 0.0 collective-permute-done.3
  48.1 2.4 %collective-permute-start.4 = (f32[256,256]{1,0:T(8,128)S(1)}, f32[256,256]{1,0:T(8,128)S(1)}, u32[]{:S(2)}, u32[]{:S(2)}) collective-permute-start(f32[256,256]{1,0:T(8,128)S(1)} %constant_dynamic-update-slice_fusion.refs_2_), channel_id=1, source_target_pairs={{0,96},{96,0},{1,97},{97,1},{2,98},{98,2},{3,99},{99,3},{4,100},{1... | collective-permute-start | bytes 786440 | tf_op jit(solution)/shard_map/ppermute | solution.py:275
  50.5 0.0 collective-permute-done.5.refs_3_
  50.5 0.0 collective-permute-done.8.refs_5_
  50.5 2.7 %gather_terms.4 = (f32[256,256]{1,0:T(8,128)S(1)}, f32[256,256]{1,0:T(8,128)S(1)}, f32[256,256]{1,0:T(8,128)S(1)}, f32[256,256]{1,0:T(8,128)S(1)}, f32[256,256]{1,0:T(8,128)S(1)}) custom-call(s32[93]{0:T(128)S(1)} %pad_add_fusion.info, f32[32,128,128]{2,1,0:T(8,128)} %bitcast.31, f32[32,128,128]{2,1,0:T(8,128)} %bitcast.32, f32[32,128,128]{2,1,0:T(8,128)} %bitcast.33, ...), custom_call_target="tpu_custom_call" | custom-call | flops 1024 | bytes 1024 | tf_op jit(solution)/shard_map/gather_terms/pallas_call | solution.py:141
  53.2 0.0 collective-permute-done.4.refs_3_
  53.2 2.4 %gather_terms.5 = (f32[256,256]{1,0:T(8,128)S(1)}, f32[256,256]{1,0:T(8,128)S(1)}, f32[256,256]{1,0:T(8,128)S(1)}, f32[256,256]{1,0:T(8,128)S(1)}, f32[256,256]{1,0:T(8,128)S(1)}) custom-call(s32[93]{0:T(128)S(1)} %pad_add_fusion.info, f32[32,128,128]{2,1,0:T(8,128)} %bitcast.34, f32[32,128,128]{2,1,0:T(8,128)} %bitcast.35, ...), custom_call_target="tpu_custom_call" | custom-call | flops 1024 | bytes 1024 | tf_op jit(solution)/shard_map/gather_terms/pallas_call | solution.py:141
  55.6 0.0 copy-start
  55.6 0.0 copy-start.1
  55.6 0.0 copy-start.2
  55.6 2.5 %collective-permute-start.9 = (f32[256,256]{1,0:T(8,128)S(1)}, f32[256,256]{1,0:T(8,128)S(1)}, u32[]{:S(2)}, u32[]{:S(2)}) collective-permute-start(f32[256,256]{1,0:T(8,128)S(1)} %get-tuple-element.74), channel_id=1, source_target_pairs={{0,93},{1,94},{2,5},{3,0},{4,1},{5,8},{6,3},{7,4},{8,11},{9,6},{10... | collective-permute-start | bytes 786440 | tf_op jit(solution)/shard_map/ppermute | solution.py:293
  58.1 7.6 %collective-permute-start.11 = (f32[256,256]{1,0:T(8,128)S(1)}, f32[256,256]{1,0:T(8,128)S(1)}, u32[]{:S(2)}, u32[]{:S(2)}) collective-permute-start(f32[256,256]{1,0:T(8,128)S(1)} %get-tuple-element.76), channel_id=1, source_target_pairs={{0,93},{1,4},{2,5},{3,0},{4,7},{5,8},{6,3},{7,10},{8,11},{9,6},{10... | collective-permute-start | bytes 786440 | tf_op jit(solution)/shard_map/ppermute | solution.py:293
  65.7 1.1 collective-permute-done.9
  66.8 1.9 %collective-permute-start.10 = (f32[256,256]{1,0:T(8,128)S(1)}, f32[256,256]{1,0:T(8,128)S(1)}, u32[]{:S(2)}, u32[]{:S(2)}) collective-permute-start(f32[256,256]{1,0:T(8,128)S(1)} %add.76), channel_id=1, source_target_pairs={{0,1},{1,2},{2,0},{3,4},{4,5},{5,3},{6,7},{7,8},{8,6},{9,10},{10,1... | collective-permute-start | bytes 786440 | tf_op jit(solution)/shard_map/ppermute | solution.py:288
  68.8 2.7 %collective-permute-done.11 = f32[256,256]{1,0:T(8,128)S(1)} collective-permute-done((f32[256,256]{1,0:T(8,128)S(1)}, f32[256,256]{1,0:T(8,128)S(1)}, u32[]{:S(2)}, u32[]{:S(2)}) %collective-permute-start.11) | collective-permute-done | bytes 262176 | tf_op jit(solution)/shard_map/ppermute | solution.py:293
  71.5 3.8 %collective-permute-start.12 = (f32[256,256]{1,0:T(8,128)S(1)}, f32[256,256]{1,0:T(8,128)S(1)}, u32[]{:S(2)}, u32[]{:S(2)}) collective-permute-start(f32[256,256]{1,0:T(8,128)S(1)} %add.77), channel_id=1, source_target_pairs={{0,2},{1,0},{2,1},{3,5},{4,3},{5,4},{6,8},{7,6},{8,7},{9,11},{10,9... | collective-permute-start | bytes 786440 | tf_op jit(solution)/shard_map/ppermute | solution.py:288
  75.3 5.2 %place_tiles.1 = (bf16[8,256,512]{2,1,0:T(8,128)(2,1)}, bf16[8,256,512]{2,1,0:T(8,128)(2,1)}) custom-call(s32[93]{0:T(128)S(1)} %pad_add_fusion.info, f32[32,128,128]{2,1,0:T(8,128)} %bitcast.36), custom_call_target="tpu_custom_call" | custom-call | bytes 6291456 | tf_op jit(solution)/shard_map/place_tiles/pallas_call | solution.py:78
  80.5 0.0 collective-permute-done.10.refs_0_
  80.5 1.3 collective-permute-done.12.refs_1_
  81.8 1.2 dense.1
  83.1 2.5 %collective-permute-start.14 = (f32[256,256]{1,0:T(8,128)S(1)}, f32[256,256]{1,0:T(8,128)S(1)}, u32[]{:S(2)}, u32[]{:S(2)}) collective-permute-start(f32[256,256]{1,0:T(8,128)S(1)} %get-tuple-element.84.refs_8_), channel_id=1, source_target_pairs={{0,1},{1,2},{2,0},{3,4},{4,5},{5,3},{6,7},{7,8},{8,6},{9,10},{10,1... | collective-permute-start | bytes 786440 | tf_op jit(solution)/shard_map/ppermute | solution.py:288
  85.5 4.3 %collective-permute-start.13 = (f32[256,256]{1,0:T(8,128)S(1)}, f32[256,256]{1,0:T(8,128)S(1)}, u32[]{:S(2)}, u32[]{:S(2)}) collective-permute-start(f32[256,256]{1,0:T(8,128)S(1)} %get-tuple-element.84.refs_8_), channel_id=1, source_target_pairs={{0,2},{1,0},{2,1},{3,5},{4,3},{5,4},{6,8},{7,6},{8,7},{9,11},{10,9... | collective-permute-start | bytes 786440 | tf_op jit(solution)/shard_map/ppermute | solution.py:288
  89.8 1.0 weight_terms.1
  90.8 11.7 %all-to-all-start = ((f32[32,8,256]{2,1,0:T(8,128)}), f32[32,8,256]{2,1,0:T(8,128)S(1)}, u32[]{:S(2)}, u32[]{:S(2)}) async-start(f32[32,8,256]{2,1,0:T(8,128)} %bitcast.37), calls=%async_computation | async-start | bytes 524288 | tf_op jit(solution)/shard_map/all_to_all | solution.py:297
  102.5 0.0 collective-permute-done.14.refs_10_
  102.5 0.0 collective-permute-done.13.refs_9_
  102.5 3.4 %collective-permute-start.15 = (f32[256,256]{1,0:T(8,128)S(1)}, f32[256,256]{1,0:T(8,128)S(1)}, u32[]{:S(2)}, u32[]{:S(2)}) collective-permute-start(f32[256,256]{1,0:T(8,128)S(1)} %collective-permute-done.13.refs_9_), channel_id=1, source_target_pairs={{0,3},{1,4},{2,95},{3,6},{4,7},{5,2},{6,9},{7,10},{8,5},{9,12},{10... | collective-permute-start | bytes 786440 | tf_op jit(solution)/shard_map/ppermute | solution.py:293
  105.9 3.4 %collective-permute-start.16 = (f32[256,256]{1,0:T(8,128)S(1)}, f32[256,256]{1,0:T(8,128)S(1)}, u32[]{:S(2)}, u32[]{:S(2)}) collective-permute-start(f32[256,256]{1,0:T(8,128)S(1)} %collective-permute-done.14.refs_10_), channel_id=1, source_target_pairs={{0,3},{1,94},{2,95},{3,6},{4,1},{5,2},{6,9},{7,4},{8,5},{9,12},{10... | collective-permute-start | bytes 786440 | tf_op jit(solution)/shard_map/ppermute | solution.py:293
  109.3 4.3 %all-to-all-done.parts = f32[32,8,256]{2,1,0:T(8,128)S(1)} async-done(((f32[32,8,256]{2,1,0:T(8,128)}), f32[32,8,256]{2,1,0:T(8,128)S(1)}, u32[]{:S(2)}, u32[]{:S(2)}) %all-to-all-start) | async-done | bytes 262176 | tf_op jit(solution)/shard_map/all_to_all | solution.py:297
  113.6 0.8 sum_and_copy.2
  114.4 8.5 %all-to-all-start.1 = ((f32[24,8,384]{2,1,0:T(8,128)}), f32[24,8,384]{2,1,0:T(8,128)}, u32[]{:S(2)}, u32[]{:S(2)}) async-start(f32[24,8,384]{2,1,0:T(8,128)} %sum_and_copy.2), calls=%async_computation.1 | async-start | bytes 589824 | tf_op jit(solution)/shard_map/all_to_all | solution.py:297
  123.0 0.0 collective-permute-done.16.refs_12_
  123.0 4.3 %spread_terms.3 = f32[4,256,256]{2,1,0:T(8,128)} custom-call(s32[93]{0:T(128)S(1)} %pad_add_fusion.info, bf16[8,256,512]{2,1,0:T(8,128)(2,1)} %get-tuple-element.82.refs_0_.refs_1_.refs_2_.refs_3_, bf16[8,256,512]{2,1,0:T(8,128)(2,1)} %get-tuple-element.82.refs_0_.refs_1_.refs_2_.refs_3_, ...), custom_call_target="tpu_custom_call" | custom-call | flops 1099511627776 | bytes 4294967296 | tf_op jit(solution)/shard_map/spread_terms/pallas_call | solution.py:232
  127.2 2.2 %collective-permute-start.17 = (f32[4,256,256]{2,1,0:T(8,128)}, f32[4,256,256]{2,1,0:T(8,128)}, u32[]{:S(2)}, u32[]{:S(2)}) collective-permute-start(f32[4,256,256]{2,1,0:T(8,128)} %spread_terms.3), channel_id=1, source_target_pairs={{0,96},{96,0},{1,97},{97,1},{2,98},{98,2},{3,99},{99,3},{4,100},{1... | collective-permute-start | bytes 3145736 | tf_op jit(solution)/shard_map/ppermute | solution.py:275
  129.4 4.1 %spread_terms.2 = (f32[256,256]{1,0:T(8,128)}, f32[256,256]{1,0:T(8,128)}, f32[256,256]{1,0:T(8,128)}, f32[256,256]{1,0:T(8,128)}) custom-call(s32[93]{0:T(128)S(1)} %pad_add_fusion.info, bf16[8,256,512]{2,1,0:T(8,128)(2,1)} %get-tuple-element.82.refs_0_.refs_1_.refs_2_.refs_3_, bf16[8,256,512]{2,1,0:T(8,128)(2,1)} %get-tuple-element.82.refs_0_.refs_1_.refs_2_.refs_3_, ...), custom_call_target="tpu_custom_call" | custom-call | flops 1099511627776 | bytes 4294967296 | tf_op jit(solution)/shard_map/spread_terms/pallas_call | solution.py:232
  133.5 1.3 fusion
  134.8 5.4 %collective-permute-start.19 = (f32[256,256]{1,0:T(8,128)S(1)}, f32[256,256]{1,0:T(8,128)S(1)}, u32[]{:S(2)}, u32[]{:S(2)}) collective-permute-start(f32[256,256]{1,0:T(8,128)S(1)} %get-tuple-element.102), channel_id=1, source_target_pairs={{0,192},{96,672},{192,384},{288,96},{384,576},{480,288},{576,0},{6... | collective-permute-start | bytes 786440 | tf_op jit(solution)/shard_map/ppermute | solution.py:284
  140.2 3.5 %collective-permute-start.18 = (f32[256,256]{1,0:T(8,128)S(1)}, f32[256,256]{1,0:T(8,128)S(1)}, u32[]{:S(2)}, u32[]{:S(2)}) collective-permute-start(f32[256,256]{1,0:T(8,128)S(1)} %get-tuple-element.103), channel_id=1, source_target_pairs={{0,576},{96,288},{192,0},{288,480},{384,192},{480,672},{576,384},{... | collective-permute-start | bytes 786440 | tf_op jit(solution)/shard_map/ppermute | solution.py:284
  143.7 0.0 all-to-all-done.1.parts
  143.7 1.8 sum_and_copy.3
  145.4 5.5 %all-to-all-start.2 = ((f32[32,8,384]{2,1,0:T(8,128)}), f32[32,8,384]{2,1,0:T(8,128)}, u32[]{:S(2)}, u32[]{:S(2)}) async-start(f32[32,8,384]{2,1,0:T(8,128)} %sum_and_copy.3), calls=%async_computation.2 | async-start | bytes 786432 | tf_op jit(solution)/shard_map/all_to_all | solution.py:297
  150.9 1.4 collective-permute-done.19.second
  152.4 6.4 %collective-permute-done.18.far = f32[256,256]{1,0:T(8,128)S(1)} collective-permute-done((f32[256,256]{1,0:T(8,128)S(1)}, f32[256,256]{1,0:T(8,128)S(1)}, u32[]{:S(2)}, u32[]{:S(2)}) %collective-permute-start.18) | collective-permute-done | bytes 262176 | tf_op jit(solution)/shard_map/ppermute | solution.py:284
  158.8 1.1 turn_terms.1
  159.9 7.3 %collective-permute-start.20 = (f32[256,256]{1,0:T(8,128)S(1)}, f32[256,256]{1,0:T(8,128)S(1)}, u32[]{:S(2)}, u32[]{:S(2)}) collective-permute-start(f32[256,256]{1,0:T(8,128)S(1)} %get-tuple-element.99), channel_id=1, source_target_pairs={{0,576},{96,288},{192,0},{288,480},{384,192},{480,672},{576,384},{... | collective-permute-start | bytes 786440 | tf_op jit(solution)/shard_map/ppermute | solution.py:284
  167.2 1.7 read_sums.1
  169.0 7.0 %collective-permute-done.20 = f32[256,256]{1,0:T(8,128)S(1)} collective-permute-done((f32[256,256]{1,0:T(8,128)S(1)}, f32[256,256]{1,0:T(8,128)S(1)}, u32[]{:S(2)}, u32[]{:S(2)}) %collective-permute-start.20) | collective-permute-done | bytes 262176 | tf_op jit(solution)/shard_map/ppermute | solution.py:284
  176.0 0.7 add.80
  (17 shorter events, 0.1 us)
Async XLA Ops:
  1.6 19.9 %collective-permute-start = (f32[128,256]{1,0:T(8,128)S(1)}, f32[128,256]{1,0:T(8,128)S(1)}, u32[]{:S(2)}, u32[]{:S(2)}) collective-permute-start(f32[128,256]{1,0:T(8,128)S(1)} %get-tuple-element.105), channel_id=1, source_target_pairs={{0,192},{96,672},{192,384},{288,96},{384,576},{480,288},{576,0},{6... | collective-permute-start | bytes 393224 | tf_op jit(solution)/shard_map/ppermute | solution.py:284
  9.5 36.6 %collective-permute-start.6 = (f32[256,256]{1,0:T(8,128)}, f32[256,256]{1,0:T(8,128)S(1)}, u32[]{:S(2)}, u32[]{:S(2)}) collective-permute-start(f32[256,256]{1,0:T(8,128)} %refs_3_.1), channel_id=1, source_target_pairs={{0,576},{96,288},{192,0},{288,480},{384,192},{480,672},{576,384},{... | collective-permute-start | bytes 786440 | tf_op jit(solution)/shard_map/ppermute | solution.py:284
  18.1 13.7 %collective-permute-start.2 = (f32[128,256]{1,0:T(8,128)S(1)}, f32[128,256]{1,0:T(8,128)S(1)}, u32[]{:S(2)}, u32[]{:S(2)}) collective-permute-start(f32[128,256]{1,0:T(8,128)S(1)} %get-tuple-element.104), channel_id=1, source_target_pairs={{0,192},{96,672},{192,384},{288,96},{384,576},{480,288},{576,0},{6... | collective-permute-start | bytes 393224 | tf_op jit(solution)/shard_map/ppermute | solution.py:284
  21.5 21.8 %collective-permute-start.1 = (f32[128,256]{1,0:T(8,128)S(1)}, f32[128,256]{1,0:T(8,128)S(1)}, u32[]{:S(2)}, u32[]{:S(2)}) collective-permute-start(f32[128,256]{1,0:T(8,128)S(1)} %collective-permute-done), channel_id=1, source_target_pairs={{0,192},{96,672},{192,384},{288,96},{384,576},{480,288},{576,0},{6... | collective-permute-start | bytes 393224 | tf_op jit(solution)/shard_map/ppermute | solution.py:284
  28.5 14.9 %collective-permute-start.7 = (f32[256,256]{1,0:T(8,128)}, f32[256,256]{1,0:T(8,128)S(1)}, u32[]{:S(2)}, u32[]{:S(2)}) collective-permute-start(f32[256,256]{1,0:T(8,128)} %refs_3_.1), channel_id=1, source_target_pairs={{0,96},{96,0},{1,97},{97,1},{2,98},{98,2},{3,99},{99,3},{4,100},{1... | collective-permute-start | bytes 786440 | tf_op jit(solution)/shard_map/ppermute | solution.py:275
  31.8 16.2 %collective-permute-start.3 = (f32[128,256]{1,0:T(8,128)S(1)}, f32[128,256]{1,0:T(8,128)S(1)}, u32[]{:S(2)}, u32[]{:S(2)}) collective-permute-start(f32[128,256]{1,0:T(8,128)S(1)} %collective-permute-done.2), channel_id=1, source_target_pairs={{0,192},{96,672},{192,384},{288,96},{384,576},{480,288},{576,0},{6... | collective-permute-start | bytes 393224 | tf_op jit(solution)/shard_map/ppermute | solution.py:284
  36.2 14.2 %collective-permute-start.5 = (f32[256,256]{1,0:T(8,128)S(1)}, f32[256,256]{1,0:T(8,128)S(1)}, u32[]{:S(2)}, u32[]{:S(2)}) collective-permute-start(f32[256,256]{1,0:T(8,128)S(1)} %constant_dynamic-update-slice_fusion.2.refs_5_), channel_id=1, source_target_pairs={{0,96},{96,0},{1,97},{97,1},{2,98},{98,2},{3,99},{99,3},{4,100},{1... | collective-permute-start | bytes 786440 | tf_op jit(solution)/shard_map/ppermute | solution.py:275
  46.1 4.4 %collective-permute-start.8 = (f32[256,256]{1,0:T(8,128)S(1)}, f32[256,256]{1,0:T(8,128)S(1)}, u32[]{:S(2)}, u32[]{:S(2)}) collective-permute-start(f32[256,256]{1,0:T(8,128)S(1)} %collective-permute-done.6.refs_4_), channel_id=1, source_target_pairs={{0,96},{96,0},{1,97},{97,1},{2,98},{98,2},{3,99},{99,3},{4,100},{1... | collective-permute-start | bytes 786440 | tf_op jit(solution)/shard_map/ppermute | solution.py:275
  48.1 5.1 %collective-permute-start.4 = (f32[256,256]{1,0:T(8,128)S(1)}, f32[256,256]{1,0:T(8,128)S(1)}, u32[]{:S(2)}, u32[]{:S(2)}) collective-permute-start(f32[256,256]{1,0:T(8,128)S(1)} %constant_dynamic-update-slice_fusion.refs_2_), channel_id=1, source_target_pairs={{0,96},{96,0},{1,97},{97,1},{2,98},{98,2},{3,99},{99,3},{4,100},{1... | collective-permute-start | bytes 786440 | tf_op jit(solution)/shard_map/ppermute | solution.py:275
  55.6 26.2 %copy-start = (f32[256,256]{1,0:T(8,128)S(1)}, f32[256,256]{1,0:T(8,128)}, u32[]{:S(2)}) copy-start(f32[256,256]{1,0:T(8,128)} %refs_2_.1) | copy-start | bytes 786436
  55.6 26.2 %copy-start.1 = (f32[256,256]{1,0:T(8,128)S(1)}, f32[256,256]{1,0:T(8,128)}, u32[]{:S(2)}) copy-start(f32[256,256]{1,0:T(8,128)} %refs_4_.1) | copy-start | bytes 786436
  55.6 26.2 %copy-start.2 = (f32[256]{0:T(256)S(1)}, f32[256]{0:T(256)}, u32[]{:S(2)}) copy-start(f32[256]{0:T(256)} %param.10) | copy-start | bytes 3076
  55.6 11.2 %collective-permute-start.9 = (f32[256,256]{1,0:T(8,128)S(1)}, f32[256,256]{1,0:T(8,128)S(1)}, u32[]{:S(2)}, u32[]{:S(2)}) collective-permute-start(f32[256,256]{1,0:T(8,128)S(1)} %get-tuple-element.74), channel_id=1, source_target_pairs={{0,93},{1,94},{2,5},{3,0},{4,1},{5,8},{6,3},{7,4},{8,11},{9,6},{10... | collective-permute-start | bytes 786440 | tf_op jit(solution)/shard_map/ppermute | solution.py:293
  58.1 13.4 %collective-permute-start.11 = (f32[256,256]{1,0:T(8,128)S(1)}, f32[256,256]{1,0:T(8,128)S(1)}, u32[]{:S(2)}, u32[]{:S(2)}) collective-permute-start(f32[256,256]{1,0:T(8,128)S(1)} %get-tuple-element.76), channel_id=1, source_target_pairs={{0,93},{1,4},{2,5},{3,0},{4,7},{5,8},{6,3},{7,10},{8,11},{9,6},{10... | collective-permute-start | bytes 786440 | tf_op jit(solution)/shard_map/ppermute | solution.py:293
  66.8 13.6 %collective-permute-start.10 = (f32[256,256]{1,0:T(8,128)S(1)}, f32[256,256]{1,0:T(8,128)S(1)}, u32[]{:S(2)}, u32[]{:S(2)}) collective-permute-start(f32[256,256]{1,0:T(8,128)S(1)} %add.76), channel_id=1, source_target_pairs={{0,1},{1,2},{2,0},{3,4},{4,5},{5,3},{6,7},{7,8},{8,6},{9,10},{10,1... | collective-permute-start | bytes 786440 | tf_op jit(solution)/shard_map/ppermute | solution.py:288
  71.5 10.3 %collective-permute-start.12 = (f32[256,256]{1,0:T(8,128)S(1)}, f32[256,256]{1,0:T(8,128)S(1)}, u32[]{:S(2)}, u32[]{:S(2)}) collective-permute-start(f32[256,256]{1,0:T(8,128)S(1)} %add.77), channel_id=1, source_target_pairs={{0,2},{1,0},{2,1},{3,5},{4,3},{5,4},{6,8},{7,6},{8,7},{9,11},{10,9... | collective-permute-start | bytes 786440 | tf_op jit(solution)/shard_map/ppermute | solution.py:288
  83.1 19.5 %collective-permute-start.14 = (f32[256,256]{1,0:T(8,128)S(1)}, f32[256,256]{1,0:T(8,128)S(1)}, u32[]{:S(2)}, u32[]{:S(2)}) collective-permute-start(f32[256,256]{1,0:T(8,128)S(1)} %get-tuple-element.84.refs_8_), channel_id=1, source_target_pairs={{0,1},{1,2},{2,0},{3,4},{4,5},{5,3},{6,7},{7,8},{8,6},{9,10},{10,1... | collective-permute-start | bytes 786440 | tf_op jit(solution)/shard_map/ppermute | solution.py:288
  85.5 17.0 %collective-permute-start.13 = (f32[256,256]{1,0:T(8,128)S(1)}, f32[256,256]{1,0:T(8,128)S(1)}, u32[]{:S(2)}, u32[]{:S(2)}) collective-permute-start(f32[256,256]{1,0:T(8,128)S(1)} %get-tuple-element.84.refs_8_), channel_id=1, source_target_pairs={{0,2},{1,0},{2,1},{3,5},{4,3},{5,4},{6,8},{7,6},{8,7},{9,11},{10,9... | collective-permute-start | bytes 786440 | tf_op jit(solution)/shard_map/ppermute | solution.py:288
  90.8 22.8 %all-to-all-start = ((f32[32,8,256]{2,1,0:T(8,128)}), f32[32,8,256]{2,1,0:T(8,128)S(1)}, u32[]{:S(2)}, u32[]{:S(2)}) async-start(f32[32,8,256]{2,1,0:T(8,128)} %bitcast.37), calls=%async_computation | async-start | bytes 524288 | tf_op jit(solution)/shard_map/all_to_all | solution.py:297
  102.5 20.4 %collective-permute-start.15 = (f32[256,256]{1,0:T(8,128)S(1)}, f32[256,256]{1,0:T(8,128)S(1)}, u32[]{:S(2)}, u32[]{:S(2)}) collective-permute-start(f32[256,256]{1,0:T(8,128)S(1)} %collective-permute-done.13.refs_9_), channel_id=1, source_target_pairs={{0,3},{1,4},{2,95},{3,6},{4,7},{5,2},{6,9},{7,10},{8,5},{9,12},{10... | collective-permute-start | bytes 786440 | tf_op jit(solution)/shard_map/ppermute | solution.py:293
  105.9 17.0 %collective-permute-start.16 = (f32[256,256]{1,0:T(8,128)S(1)}, f32[256,256]{1,0:T(8,128)S(1)}, u32[]{:S(2)}, u32[]{:S(2)}) collective-permute-start(f32[256,256]{1,0:T(8,128)S(1)} %collective-permute-done.14.refs_10_), channel_id=1, source_target_pairs={{0,3},{1,94},{2,95},{3,6},{4,1},{5,2},{6,9},{7,4},{8,5},{9,12},{10... | collective-permute-start | bytes 786440 | tf_op jit(solution)/shard_map/ppermute | solution.py:293
  114.4 29.3 %all-to-all-start.1 = ((f32[24,8,384]{2,1,0:T(8,128)}), f32[24,8,384]{2,1,0:T(8,128)}, u32[]{:S(2)}, u32[]{:S(2)}) async-start(f32[24,8,384]{2,1,0:T(8,128)} %sum_and_copy.2), calls=%async_computation.1 | async-start | bytes 589824 | tf_op jit(solution)/shard_map/all_to_all | solution.py:297
  127.2 6.2 %collective-permute-start.17 = (f32[4,256,256]{2,1,0:T(8,128)}, f32[4,256,256]{2,1,0:T(8,128)}, u32[]{:S(2)}, u32[]{:S(2)}) collective-permute-start(f32[4,256,256]{2,1,0:T(8,128)} %spread_terms.3), channel_id=1, source_target_pairs={{0,96},{96,0},{1,97},{97,1},{2,98},{98,2},{3,99},{99,3},{4,100},{1... | collective-permute-start | bytes 3145736 | tf_op jit(solution)/shard_map/ppermute | solution.py:275
  133.5 25.3 %copy-start.3 = (f32[256,256]{1,0:T(8,128)S(1)}, f32[256,256]{1,0:T(8,128)}, u32[]{:S(2)}) copy-start(f32[256,256]{1,0:T(8,128)} %get-tuple-element.90.kept_first) | copy-start | bytes 786436
  133.5 25.3 %copy-start.4 = (f32[256,256]{1,0:T(8,128)S(1)}, f32[256,256]{1,0:T(8,128)}, u32[]{:S(2)}) copy-start(f32[256,256]{1,0:T(8,128)} %get-tuple-element.92.kept) | copy-start | bytes 786436
  134.8 17.6 %collective-permute-start.19 = (f32[256,256]{1,0:T(8,128)S(1)}, f32[256,256]{1,0:T(8,128)S(1)}, u32[]{:S(2)}, u32[]{:S(2)}) collective-permute-start(f32[256,256]{1,0:T(8,128)S(1)} %get-tuple-element.102), channel_id=1, source_target_pairs={{0,192},{96,672},{192,384},{288,96},{384,576},{480,288},{576,0},{6... | collective-permute-start | bytes 786440 | tf_op jit(solution)/shard_map/ppermute | solution.py:284
  140.2 18.6 %collective-permute-start.18 = (f32[256,256]{1,0:T(8,128)S(1)}, f32[256,256]{1,0:T(8,128)S(1)}, u32[]{:S(2)}, u32[]{:S(2)}) collective-permute-start(f32[256,256]{1,0:T(8,128)S(1)} %get-tuple-element.103), channel_id=1, source_target_pairs={{0,576},{96,288},{192,0},{288,480},{384,192},{480,672},{576,384},{... | collective-permute-start | bytes 786440 | tf_op jit(solution)/shard_map/ppermute | solution.py:284
  145.4 21.8 %all-to-all-start.2 = ((f32[32,8,384]{2,1,0:T(8,128)}), f32[32,8,384]{2,1,0:T(8,128)}, u32[]{:S(2)}, u32[]{:S(2)}) async-start(f32[32,8,384]{2,1,0:T(8,128)} %sum_and_copy.3), calls=%async_computation.2 | async-start | bytes 786432 | tf_op jit(solution)/shard_map/all_to_all | solution.py:297
  159.9 16.1 %collective-permute-start.20 = (f32[256,256]{1,0:T(8,128)S(1)}, f32[256,256]{1,0:T(8,128)S(1)}, u32[]{:S(2)}, u32[]{:S(2)}) collective-permute-start(f32[256,256]{1,0:T(8,128)S(1)} %get-tuple-element.99), channel_id=1, source_target_pairs={{0,576},{96,288},{192,0},{288,480},{384,192},{480,672},{576,384},{... | collective-permute-start | bytes 786440 | tf_op jit(solution)/shard_map/ppermute | solution.py:284

commit v5 on v4

--- a/solution.py
+++ b/solution.py
@@ -380,7 +380,8 @@
 
     first_upper = along_loop(features[:TILE], 1)
     first_lower = along_loop(features[TILE:], 1)
-    field_second = along_loop(features, -1)
+    second_payload, info = after(features, info)
+    field_second = along_loop(second_payload, -1)
     first_upper, own_field, info = after(first_upper, features, info)
     field_other = other_core(own_field)
     far_upper = along_loop(first_upper, 1)

time: 178 us -> 176 us (0.989)
  the two profiles are of different devices: /device:TPU:8 before, /device:TPU:4 now
where the time goes in v5:
time: 176 us; the launch traced here: 174 us
  starting transfers between devices  115 us (65%)
  Pallas kernels  28.9 us (16%)
  waiting for transfers between devices  25.2 us (14%)
  other arithmetic  2.89 us (2%)
    ppermute x8, starting transfers between devices, along_loop(): return lax.ppermute(value, LOOP, pairs)  47.1 us
    all_to_all x3, starting transfers between devices, swap(): return lax.all_to_all(value, axes, 0, 0, tiled=True)  24.1 us
    ppermute x4, starting transfers between devices, in_triple(): lax.ppermute(value, 'z_lo', [(i, (i + by) % Z_LO) for i in range(Z_LO)])  16.8 us
    ppermute x4, starting transfers between devices, across_triples(): return lax.ppermute(value, REP, pairs)  15.5 us
    ppermute x8, waiting for transfers between devices, along_loop(): return lax.ppermute(value, LOOP, pairs)  14.8 us
    ppermute x5, starting transfers between devices, other_core(): return lax.ppermute(value, 'core', [(0, 1), (1, 0)])  11.6 us
    pallas_call x2, Pallas kernels, spread_terms(): pl.pallas_call(functools.partial(spread_kernel, at, n), grid_spec=pltpu.P...  8.34 us
    pallas_call x3, Pallas kernels, gather_terms(): pl.pallas_call(functools.partial(gather_kernel, n, len(before), at), grid...  7.79 us
  transfers between devices with their start and end apart: 24, of which 8 were waited for; matrix products, arithmetic and copies ran while one was open for 1% of the time, Pallas kernels for 15%

profile of v5, /device:TPU:4, one launch (start us, length us, event | category | flops | bytes accessed | tf_op | source)
XLA Modules:
  0.0 174.4 jit_solution(10354009474874517080)
XLA Ops:
  0.6 1.0 fusion.2
  1.6 7.9 %collective-permute-start = (f32[128,256]{1,0:T(8,128)S(1)}, f32[128,256]{1,0:T(8,128)S(1)}, u32[]{:S(2)}, u32[]{:S(2)}) collective-permute-start(f32[128,256]{1,0:T(8,128)S(1)} %get-tuple-element.109), channel_id=1, source_target_pairs={{0,192},{96,672},{192,384},{288,96},{384,576},{480,288},{576,0},{6... | collective-permute-start | bytes 393224 | tf_op jit(solution)/shard_map/ppermute | solution.py:284
  9.5 9.1 %collective-permute-start.2 = (f32[128,256]{1,0:T(8,128)S(1)}, f32[128,256]{1,0:T(8,128)S(1)}, u32[]{:S(2)}, u32[]{:S(2)}) collective-permute-start(f32[128,256]{1,0:T(8,128)S(1)} %get-tuple-element.108), channel_id=1, source_target_pairs={{0,192},{96,672},{192,384},{288,96},{384,576},{480,288},{576,0},{6... | collective-permute-start | bytes 393224 | tf_op jit(solution)/shard_map/ppermute | solution.py:284
  18.7 0.1 stack.60
  18.8 0.8 pad_add_fusion.info
  19.6 1.9 %collective-permute-start.6 = (f32[256,256]{1,0:T(8,128)}, f32[256,256]{1,0:T(8,128)S(1)}, u32[]{:S(2)}, u32[]{:S(2)}) collective-permute-start(f32[256,256]{1,0:T(8,128)} %refs_3_.1), channel_id=1, source_target_pairs={{0,576},{96,288},{192,0},{288,480},{384,192},{480,672},{576,384},{... | collective-permute-start | bytes 786440 | tf_op jit(solution)/shard_map/ppermute | solution.py:284
  21.5 0.0 collective-permute-done
  21.5 5.8 %collective-permute-start.1 = (f32[128,256]{1,0:T(8,128)S(1)}, f32[128,256]{1,0:T(8,128)S(1)}, u32[]{:S(2)}, u32[]{:S(2)}) collective-permute-start(f32[128,256]{1,0:T(8,128)S(1)} %collective-permute-done), channel_id=1, source_target_pairs={{0,192},{96,672},{192,384},{288,96},{384,576},{480,288},{576,0},{6... | collective-permute-start | bytes 393224 | tf_op jit(solution)/shard_map/ppermute | solution.py:284
  27.3 3.2 %collective-permute-start.7 = (f32[256,256]{1,0:T(8,128)}, f32[256,256]{1,0:T(8,128)S(1)}, u32[]{:S(2)}, u32[]{:S(2)}) collective-permute-start(f32[256,256]{1,0:T(8,128)} %refs_3_.1), channel_id=1, source_target_pairs={{0,96},{96,0},{1,97},{97,1},{2,98},{98,2},{3,99},{99,3},{4,100},{1... | collective-permute-start | bytes 786440 | tf_op jit(solution)/shard_map/ppermute | solution.py:275
  30.6 0.8 collective-permute-done.2
  31.4 6.4 %collective-permute-start.3 = (f32[128,256]{1,0:T(8,128)S(1)}, f32[128,256]{1,0:T(8,128)S(1)}, u32[]{:S(2)}, u32[]{:S(2)}) collective-permute-start(f32[128,256]{1,0:T(8,128)S(1)} %collective-permute-done.2), channel_id=1, source_target_pairs={{0,192},{96,672},{192,384},{288,96},{384,576},{480,288},{576,0},{6... | collective-permute-start | bytes 393224 | tf_op jit(solution)/shard_map/ppermute | solution.py:284
  37.9 1.9 %collective-permute-start.5 = (f32[256,256]{1,0:T(8,128)S(1)}, f32[256,256]{1,0:T(8,128)S(1)}, u32[]{:S(2)}, u32[]{:S(2)}) collective-permute-start(f32[256,256]{1,0:T(8,128)S(1)} %constant_dynamic-update-slice_fusion.2.refs_5_), channel_id=1, source_target_pairs={{0,96},{96,0},{1,97},{97,1},{2,98},{98,2},{3,99},{99,3},{4,100},{1... | collective-permute-start | bytes 786440 | tf_op jit(solution)/shard_map/ppermute | solution.py:275
  39.8 0.0 collective-permute-done.1
  39.9 0.0 collective-permute-done.7.refs_4_
  39.9 2.7 %gather_terms.3 = (f32[256,256]{1,0:T(8,128)S(1)}, f32[256,256]{1,0:T(8,128)S(1)}, f32[256,256]{1,0:T(8,128)S(1)}, f32[256,256]{1,0:T(8,128)S(1)}, f32[256,256]{1,0:T(8,128)S(1)}) custom-call(s32[93]{0:T(128)S(1)} %pad_add_fusion.info, f32[32,128,128]{2,1,0:T(8,128)} %bitcast.28, f32[32,128,128]{2,1,0:T(8,128)} %bitcast.29, f32[32,128,128]{2,1,0:T(8,128)} %bitcast.30, ...), custom_call_target="tpu_custom_call" | custom-call | flops 1024 | bytes 1024 | tf_op jit(solution)/shard_map/gather_terms/pallas_call | solution.py:141
  42.6 0.0 collective-permute-done.6.refs_4_
  42.6 2.4 %collective-permute-start.8 = (f32[256,256]{1,0:T(8,128)S(1)}, f32[256,256]{1,0:T(8,128)S(1)}, u32[]{:S(2)}, u32[]{:S(2)}) collective-permute-start(f32[256,256]{1,0:T(8,128)S(1)} %collective-permute-done.6.refs_4_), channel_id=1, source_target_pairs={{0,96},{96,0},{1,97},{97,1},{2,98},{98,2},{3,99},{99,3},{4,100},{1... | collective-permute-start | bytes 786440 | tf_op jit(solution)/shard_map/ppermute | solution.py:275
  45.0 0.0 collective-permute-done.3
  45.1 1.9 %collective-permute-start.4 = (f32[256,256]{1,0:T(8,128)S(1)}, f32[256,256]{1,0:T(8,128)S(1)}, u32[]{:S(2)}, u32[]{:S(2)}) collective-permute-start(f32[256,256]{1,0:T(8,128)S(1)} %constant_dynamic-update-slice_fusion.refs_2_), channel_id=1, source_target_pairs={{0,96},{96,0},{1,97},{97,1},{2,98},{98,2},{3,99},{99,3},{4,100},{1... | collective-permute-start | bytes 786440 | tf_op jit(solution)/shard_map/ppermute | solution.py:275
  47.0 0.0 collective-permute-done.5.refs_3_
  47.0 0.0 collective-permute-done.8.refs_5_
  47.0 2.7 %gather_terms.4 = (f32[256,256]{1,0:T(8,128)S(1)}, f32[256,256]{1,0:T(8,128)S(1)}, f32[256,256]{1,0:T(8,128)S(1)}, f32[256,256]{1,0:T(8,128)S(1)}, f32[256,256]{1,0:T(8,128)S(1)}) custom-call(s32[93]{0:T(128)S(1)} %pad_add_fusion.info, f32[32,128,128]{2,1,0:T(8,128)} %bitcast.31, f32[32,128,128]{2,1,0:T(8,128)} %bitcast.32, f32[32,128,128]{2,1,0:T(8,128)} %bitcast.33, ...), custom_call_target="tpu_custom_call" | custom-call | flops 1024 | bytes 1024 | tf_op jit(solution)/shard_map/gather_terms/pallas_call | solution.py:141
  49.7 0.0 collective-permute-done.4.refs_3_
  49.7 2.4 %gather_terms.5 = (f32[256,256]{1,0:T(8,128)S(1)}, f32[256,256]{1,0:T(8,128)S(1)}, f32[256,256]{1,0:T(8,128)S(1)}, f32[256,256]{1,0:T(8,128)S(1)}, f32[256,256]{1,0:T(8,128)S(1)}) custom-call(s32[93]{0:T(128)S(1)} %pad_add_fusion.info, f32[32,128,128]{2,1,0:T(8,128)} %bitcast.34, f32[32,128,128]{2,1,0:T(8,128)} %bitcast.35, ...), custom_call_target="tpu_custom_call" | custom-call | flops 1024 | bytes 1024 | tf_op jit(solution)/shard_map/gather_terms/pallas_call | solution.py:141
  52.1 0.0 copy-start
  52.1 0.0 copy-start.1
  52.1 0.0 copy-start.2
  52.1 5.5 %collective-permute-start.9 = (f32[256,256]{1,0:T(8,128)S(1)}, f32[256,256]{1,0:T(8,128)S(1)}, u32[]{:S(2)}, u32[]{:S(2)}) collective-permute-start(f32[256,256]{1,0:T(8,128)S(1)} %get-tuple-element.78), channel_id=1, source_target_pairs={{0,93},{1,94},{2,5},{3,0},{4,1},{5,8},{6,3},{7,4},{8,11},{9,6},{10... | collective-permute-start | bytes 786440 | tf_op jit(solution)/shard_map/ppermute | solution.py:293
  57.6 3.3 %collective-permute-start.11 = (f32[256,256]{1,0:T(8,128)S(1)}, f32[256,256]{1,0:T(8,128)S(1)}, u32[]{:S(2)}, u32[]{:S(2)}) collective-permute-start(f32[256,256]{1,0:T(8,128)S(1)} %get-tuple-element.80), channel_id=1, source_target_pairs={{0,93},{1,4},{2,5},{3,0},{4,7},{5,8},{6,3},{7,10},{8,11},{9,6},{10... | collective-permute-start | bytes 786440 | tf_op jit(solution)/shard_map/ppermute | solution.py:293
  60.9 3.3 %collective-permute-done.9 = f32[256,256]{1,0:T(8,128)S(1)} collective-permute-done((f32[256,256]{1,0:T(8,128)S(1)}, f32[256,256]{1,0:T(8,128)S(1)}, u32[]{:S(2)}, u32[]{:S(2)}) %collective-permute-start.9) | collective-permute-done | bytes 262176 | tf_op jit(solution)/shard_map/ppermute | solution.py:293
  64.3 3.1 %collective-permute-start.10 = (f32[256,256]{1,0:T(8,128)S(1)}, f32[256,256]{1,0:T(8,128)S(1)}, u32[]{:S(2)}, u32[]{:S(2)}) collective-permute-start(f32[256,256]{1,0:T(8,128)S(1)} %add.76), channel_id=1, source_target_pairs={{0,1},{1,2},{2,0},{3,4},{4,5},{5,3},{6,7},{7,8},{8,6},{9,10},{10,1... | collective-permute-start | bytes 786440 | tf_op jit(solution)/shard_map/ppermute | solution.py:288
  67.3 2.1 %collective-permute-done.11 = f32[256,256]{1,0:T(8,128)S(1)} collective-permute-done((f32[256,256]{1,0:T(8,128)S(1)}, f32[256,256]{1,0:T(8,128)S(1)}, u32[]{:S(2)}, u32[]{:S(2)}) %collective-permute-start.11) | collective-permute-done | bytes 262176 | tf_op jit(solution)/shard_map/ppermute | solution.py:293
  69.5 7.0 %collective-permute-start.12 = (f32[256,256]{1,0:T(8,128)S(1)}, f32[256,256]{1,0:T(8,128)S(1)}, u32[]{:S(2)}, u32[]{:S(2)}) collective-permute-start(f32[256,256]{1,0:T(8,128)S(1)} %add.77), channel_id=1, source_target_pairs={{0,2},{1,0},{2,1},{3,5},{4,3},{5,4},{6,8},{7,6},{8,7},{9,11},{10,9... | collective-permute-start | bytes 786440 | tf_op jit(solution)/shard_map/ppermute | solution.py:288
  76.4 5.2 %place_tiles.1 = (bf16[8,256,512]{2,1,0:T(8,128)(2,1)}, bf16[8,256,512]{2,1,0:T(8,128)(2,1)}) custom-call(s32[93]{0:T(128)S(1)} %pad_add_fusion.info, f32[32,128,128]{2,1,0:T(8,128)} %bitcast.36), custom_call_target="tpu_custom_call" | custom-call | bytes 6291456 | tf_op jit(solution)/shard_map/place_tiles/pallas_call | solution.py:78
  81.6 0.4 collective-permute-done.12.refs_1_
  82.1 1.2 dense.1
  83.3 2.5 %collective-permute-start.14 = (f32[256,256]{1,0:T(8,128)S(1)}, f32[256,256]{1,0:T(8,128)S(1)}, u32[]{:S(2)}, u32[]{:S(2)}) collective-permute-start(f32[256,256]{1,0:T(8,128)S(1)} %get-tuple-element.88.refs_8_), channel_id=1, source_target_pairs={{0,1},{1,2},{2,0},{3,4},{4,5},{5,3},{6,7},{7,8},{8,6},{9,10},{10,1... | collective-permute-start | bytes 786440 | tf_op jit(solution)/shard_map/ppermute | solution.py:288
  85.8 4.2 %collective-permute-start.13 = (f32[256,256]{1,0:T(8,128)S(1)}, f32[256,256]{1,0:T(8,128)S(1)}, u32[]{:S(2)}, u32[]{:S(2)}) collective-permute-start(f32[256,256]{1,0:T(8,128)S(1)} %get-tuple-element.88.refs_8_), channel_id=1, source_target_pairs={{0,2},{1,0},{2,1},{3,5},{4,3},{5,4},{6,8},{7,6},{8,7},{9,11},{10,9... | collective-permute-start | bytes 786440 | tf_op jit(solution)/shard_map/ppermute | solution.py:288
  90.0 1.0 weight_terms.1
  91.1 9.4 %all-to-all-start = ((f32[32,8,256]{2,1,0:T(8,128)}), f32[32,8,256]{2,1,0:T(8,128)S(1)}, u32[]{:S(2)}, u32[]{:S(2)}) async-start(f32[32,8,256]{2,1,0:T(8,128)} %bitcast.37), calls=%async_computation | async-start | bytes 524288 | tf_op jit(solution)/shard_map/all_to_all | solution.py:297
  100.4 0.0 collective-permute-done.14.refs_10_
  100.4 3.4 %collective-permute-start.15 = (f32[256,256]{1,0:T(8,128)S(1)}, f32[256,256]{1,0:T(8,128)S(1)}, u32[]{:S(2)}, u32[]{:S(2)}) collective-permute-start(f32[256,256]{1,0:T(8,128)S(1)} %collective-permute-done.13.refs_9_), channel_id=1, source_target_pairs={{0,3},{1,4},{2,95},{3,6},{4,7},{5,2},{6,9},{7,10},{8,5},{9,12},{10... | collective-permute-start | bytes 786440 | tf_op jit(solution)/shard_map/ppermute | solution.py:293
  103.8 3.4 %collective-permute-start.16 = (f32[256,256]{1,0:T(8,128)S(1)}, f32[256,256]{1,0:T(8,128)S(1)}, u32[]{:S(2)}, u32[]{:S(2)}) collective-permute-start(f32[256,256]{1,0:T(8,128)S(1)} %collective-permute-done.14.refs_10_), channel_id=1, source_target_pairs={{0,3},{1,94},{2,95},{3,6},{4,1},{5,2},{6,9},{7,4},{8,5},{9,12},{10... | collective-permute-start | bytes 786440 | tf_op jit(solution)/shard_map/ppermute | solution.py:293
  107.2 4.5 %all-to-all-done.parts = f32[32,8,256]{2,1,0:T(8,128)S(1)} async-done(((f32[32,8,256]{2,1,0:T(8,128)}), f32[32,8,256]{2,1,0:T(8,128)S(1)}, u32[]{:S(2)}, u32[]{:S(2)}) %all-to-all-start) | async-done | bytes 262176 | tf_op jit(solution)/shard_map/all_to_all | solution.py:297
  111.7 0.8 sum_and_copy.2
  112.4 7.5 %all-to-all-start.1 = ((f32[24,8,384]{2,1,0:T(8,128)}), f32[24,8,384]{2,1,0:T(8,128)}, u32[]{:S(2)}, u32[]{:S(2)}) async-start(f32[24,8,384]{2,1,0:T(8,128)} %sum_and_copy.2), calls=%async_computation.1 | async-start | bytes 589824 | tf_op jit(solution)/shard_map/all_to_all | solution.py:297
  119.9 0.1 collective-permute-done.16.refs_12_
  120.0 4.3 %spread_terms.3 = f32[4,256,256]{2,1,0:T(8,128)} custom-call(s32[93]{0:T(128)S(1)} %pad_add_fusion.info, bf16[8,256,512]{2,1,0:T(8,128)(2,1)} %get-tuple-element.86.refs_0_.refs_1_.refs_2_.refs_3_, bf16[8,256,512]{2,1,0:T(8,128)(2,1)} %get-tuple-element.86.refs_0_.refs_1_.refs_2_.refs_3_, ...), custom_call_target="tpu_custom_call" | custom-call | flops 1099511627776 | bytes 4294967296 | tf_op jit(solution)/shard_map/spread_terms/pallas_call | solution.py:232
  124.2 2.1 %collective-permute-start.17 = (f32[4,256,256]{2,1,0:T(8,128)}, f32[4,256,256]{2,1,0:T(8,128)}, u32[]{:S(2)}, u32[]{:S(2)}) collective-permute-start(f32[4,256,256]{2,1,0:T(8,128)} %spread_terms.3), channel_id=1, source_target_pairs={{0,96},{96,0},{1,97},{97,1},{2,98},{98,2},{3,99},{99,3},{4,100},{1... | collective-permute-start | bytes 3145736 | tf_op jit(solution)/shard_map/ppermute | solution.py:275
  126.4 4.1 %spread_terms.2 = (f32[256,256]{1,0:T(8,128)}, f32[256,256]{1,0:T(8,128)}, f32[256,256]{1,0:T(8,128)}, f32[256,256]{1,0:T(8,128)}) custom-call(s32[93]{0:T(128)S(1)} %pad_add_fusion.info, bf16[8,256,512]{2,1,0:T(8,128)(2,1)} %get-tuple-element.86.refs_0_.refs_1_.refs_2_.refs_3_, bf16[8,256,512]{2,1,0:T(8,128)(2,1)} %get-tuple-element.86.refs_0_.refs_1_.refs_2_.refs_3_, ...), custom_call_target="tpu_custom_call" | custom-call | flops 1099511627776 | bytes 4294967296 | tf_op jit(solution)/shard_map/spread_terms/pallas_call | solution.py:232
  130.4 0.0 collective-permute-done.17.given_first.given
  130.4 1.3 fusion
  131.8 5.9 %collective-permute-start.19 = (f32[256,256]{1,0:T(8,128)S(1)}, f32[256,256]{1,0:T(8,128)S(1)}, u32[]{:S(2)}, u32[]{:S(2)}) collective-permute-start(f32[256,256]{1,0:T(8,128)S(1)} %get-tuple-element.106), channel_id=1, source_target_pairs={{0,192},{96,672},{192,384},{288,96},{384,576},{480,288},{576,0},{6... | collective-permute-start | bytes 786440 | tf_op jit(solution)/shard_map/ppermute | solution.py:284
  137.7 2.9 %collective-permute-start.18 = (f32[256,256]{1,0:T(8,128)S(1)}, f32[256,256]{1,0:T(8,128)S(1)}, u32[]{:S(2)}, u32[]{:S(2)}) collective-permute-start(f32[256,256]{1,0:T(8,128)S(1)} %get-tuple-element.107), channel_id=1, source_target_pairs={{0,576},{96,288},{192,0},{288,480},{384,192},{480,672},{576,384},{... | collective-permute-start | bytes 786440 | tf_op jit(solution)/shard_map/ppermute | solution.py:284
  140.6 0.0 all-to-all-done.1.parts
  140.6 1.8 %sum_and_copy.3 = f32[32,8,384]{2,1,0:T(8,128)} custom-call(f32[24,8,384]{2,1,0:T(8,128)} %all-to-all-done.1.parts), custom_call_target="tpu_custom_call" | custom-call | flops 1024 | bytes 1024 | tf_op jit(solution)/shard_map/sum_and_copy/pallas_call | solution.py:314
  142.4 7.3 %all-to-all-start.2 = ((f32[32,8,384]{2,1,0:T(8,128)}), f32[32,8,384]{2,1,0:T(8,128)}, u32[]{:S(2)}, u32[]{:S(2)}) async-start(f32[32,8,384]{2,1,0:T(8,128)} %sum_and_copy.3), calls=%async_computation.2 | async-start | bytes 786432 | tf_op jit(solution)/shard_map/all_to_all | solution.py:297
  149.7 6.2 %collective-permute-done.18.far = f32[256,256]{1,0:T(8,128)S(1)} collective-permute-done((f32[256,256]{1,0:T(8,128)S(1)}, f32[256,256]{1,0:T(8,128)S(1)}, u32[]{:S(2)}, u32[]{:S(2)}) %collective-permute-start.18) | collective-permute-done | bytes 262176 | tf_op jit(solution)/shard_map/ppermute | solution.py:284
  156.0 1.1 turn_terms.1
  157.1 7.1 %collective-permute-start.20 = (f32[256,256]{1,0:T(8,128)S(1)}, f32[256,256]{1,0:T(8,128)S(1)}, u32[]{:S(2)}, u32[]{:S(2)}) collective-permute-start(f32[256,256]{1,0:T(8,128)S(1)} %get-tuple-element.103), channel_id=1, source_target_pairs={{0,576},{96,288},{192,0},{288,480},{384,192},{480,672},{576,384},{... | collective-permute-start | bytes 786440 | tf_op jit(solution)/shard_map/ppermute | solution.py:284
  164.2 0.0 all-to-all-done.2.whole
  164.2 1.7 %read_sums.1 = (f32[256,256]{1,0:T(8,128)}, f32[1,256]{1,0:T(1,128)}) custom-call(f32[32,8,384]{2,1,0:T(8,128)} %all-to-all-done.2.whole), custom_call_target="tpu_custom_call" | custom-call | tf_op jit(solution)/shard_map/read_sums/pallas_call | solution.py:333
  165.9 7.7 %collective-permute-done.20 = f32[256,256]{1,0:T(8,128)S(1)} collective-permute-done((f32[256,256]{1,0:T(8,128)S(1)}, f32[256,256]{1,0:T(8,128)S(1)}, u32[]{:S(2)}, u32[]{:S(2)}) %collective-permute-start.20) | collective-permute-done | bytes 262176 | tf_op jit(solution)/shard_map/ppermute | solution.py:284
  173.7 0.7 add.80
  (17 shorter events, 0.1 us)
Async XLA Ops:
  1.6 19.9 %collective-permute-start = (f32[128,256]{1,0:T(8,128)S(1)}, f32[128,256]{1,0:T(8,128)S(1)}, u32[]{:S(2)}, u32[]{:S(2)}) collective-permute-start(f32[128,256]{1,0:T(8,128)S(1)} %get-tuple-element.109), channel_id=1, source_target_pairs={{0,192},{96,672},{192,384},{288,96},{384,576},{480,288},{576,0},{6... | collective-permute-start | bytes 393224 | tf_op jit(solution)/shard_map/ppermute | solution.py:284
  9.5 21.9 %collective-permute-start.2 = (f32[128,256]{1,0:T(8,128)S(1)}, f32[128,256]{1,0:T(8,128)S(1)}, u32[]{:S(2)}, u32[]{:S(2)}) collective-permute-start(f32[128,256]{1,0:T(8,128)S(1)} %get-tuple-element.108), channel_id=1, source_target_pairs={{0,192},{96,672},{192,384},{288,96},{384,576},{480,288},{576,0},{6... | collective-permute-start | bytes 393224 | tf_op jit(solution)/shard_map/ppermute | solution.py:284
  19.6 23.0 %collective-permute-start.6 = (f32[256,256]{1,0:T(8,128)}, f32[256,256]{1,0:T(8,128)S(1)}, u32[]{:S(2)}, u32[]{:S(2)}) collective-permute-start(f32[256,256]{1,0:T(8,128)} %refs_3_.1), channel_id=1, source_target_pairs={{0,576},{96,288},{192,0},{288,480},{384,192},{480,672},{576,384},{... | collective-permute-start | bytes 786440 | tf_op jit(solution)/shard_map/ppermute | solution.py:284
  21.5 18.3 %collective-permute-start.1 = (f32[128,256]{1,0:T(8,128)S(1)}, f32[128,256]{1,0:T(8,128)S(1)}, u32[]{:S(2)}, u32[]{:S(2)}) collective-permute-start(f32[128,256]{1,0:T(8,128)S(1)} %collective-permute-done), channel_id=1, source_target_pairs={{0,192},{96,672},{192,384},{288,96},{384,576},{480,288},{576,0},{6... | collective-permute-start | bytes 393224 | tf_op jit(solution)/shard_map/ppermute | solution.py:284
  27.3 12.5 %collective-permute-start.7 = (f32[256,256]{1,0:T(8,128)}, f32[256,256]{1,0:T(8,128)S(1)}, u32[]{:S(2)}, u32[]{:S(2)}) collective-permute-start(f32[256,256]{1,0:T(8,128)} %refs_3_.1), channel_id=1, source_target_pairs={{0,96},{96,0},{1,97},{97,1},{2,98},{98,2},{3,99},{99,3},{4,100},{1... | collective-permute-start | bytes 786440 | tf_op jit(solution)/shard_map/ppermute | solution.py:275
  31.4 13.6 %collective-permute-start.3 = (f32[128,256]{1,0:T(8,128)S(1)}, f32[128,256]{1,0:T(8,128)S(1)}, u32[]{:S(2)}, u32[]{:S(2)}) collective-permute-start(f32[128,256]{1,0:T(8,128)S(1)} %collective-permute-done.2), channel_id=1, source_target_pairs={{0,192},{96,672},{192,384},{288,96},{384,576},{480,288},{576,0},{6... | collective-permute-start | bytes 393224 | tf_op jit(solution)/shard_map/ppermute | solution.py:284
  37.9 9.1 %collective-permute-start.5 = (f32[256,256]{1,0:T(8,128)S(1)}, f32[256,256]{1,0:T(8,128)S(1)}, u32[]{:S(2)}, u32[]{:S(2)}) collective-permute-start(f32[256,256]{1,0:T(8,128)S(1)} %constant_dynamic-update-slice_fusion.2.refs_5_), channel_id=1, source_target_pairs={{0,96},{96,0},{1,97},{97,1},{2,98},{98,2},{3,99},{99,3},{4,100},{1... | collective-permute-start | bytes 786440 | tf_op jit(solution)/shard_map/ppermute | solution.py:275
  42.6 4.4 %collective-permute-start.8 = (f32[256,256]{1,0:T(8,128)S(1)}, f32[256,256]{1,0:T(8,128)S(1)}, u32[]{:S(2)}, u32[]{:S(2)}) collective-permute-start(f32[256,256]{1,0:T(8,128)S(1)} %collective-permute-done.6.refs_4_), channel_id=1, source_target_pairs={{0,96},{96,0},{1,97},{97,1},{2,98},{98,2},{3,99},{99,3},{4,100},{1... | collective-permute-start | bytes 786440 | tf_op jit(solution)/shard_map/ppermute | solution.py:275
  45.1 4.6 %collective-permute-start.4 = (f32[256,256]{1,0:T(8,128)S(1)}, f32[256,256]{1,0:T(8,128)S(1)}, u32[]{:S(2)}, u32[]{:S(2)}) collective-permute-start(f32[256,256]{1,0:T(8,128)S(1)} %constant_dynamic-update-slice_fusion.refs_2_), channel_id=1, source_target_pairs={{0,96},{96,0},{1,97},{97,1},{2,98},{98,2},{3,99},{99,3},{4,100},{1... | collective-permute-start | bytes 786440 | tf_op jit(solution)/shard_map/ppermute | solution.py:275
  52.1 30.0 %copy-start = (f32[256,256]{1,0:T(8,128)S(1)}, f32[256,256]{1,0:T(8,128)}, u32[]{:S(2)}) copy-start(f32[256,256]{1,0:T(8,128)} %refs_2_.1) | copy-start | bytes 786436
  52.1 30.0 %copy-start.1 = (f32[256,256]{1,0:T(8,128)S(1)}, f32[256,256]{1,0:T(8,128)}, u32[]{:S(2)}) copy-start(f32[256,256]{1,0:T(8,128)} %refs_4_.1) | copy-start | bytes 786436
  52.1 29.9 %copy-start.2 = (f32[256]{0:T(256)S(1)}, f32[256]{0:T(256)}, u32[]{:S(2)}) copy-start(f32[256]{0:T(256)} %param.10) | copy-start | bytes 3076
  52.1 12.1 %collective-permute-start.9 = (f32[256,256]{1,0:T(8,128)S(1)}, f32[256,256]{1,0:T(8,128)S(1)}, u32[]{:S(2)}, u32[]{:S(2)}) collective-permute-start(f32[256,256]{1,0:T(8,128)S(1)} %get-tuple-element.78), channel_id=1, source_target_pairs={{0,93},{1,94},{2,5},{3,0},{4,1},{5,8},{6,3},{7,4},{8,11},{9,6},{10... | collective-permute-start | bytes 786440 | tf_op jit(solution)/shard_map/ppermute | solution.py:293
  57.6 11.8 %collective-permute-start.11 = (f32[256,256]{1,0:T(8,128)S(1)}, f32[256,256]{1,0:T(8,128)S(1)}, u32[]{:S(2)}, u32[]{:S(2)}) collective-permute-start(f32[256,256]{1,0:T(8,128)S(1)} %get-tuple-element.80), channel_id=1, source_target_pairs={{0,93},{1,4},{2,5},{3,0},{4,7},{5,8},{6,3},{7,10},{8,11},{9,6},{10... | collective-permute-start | bytes 786440 | tf_op jit(solution)/shard_map/ppermute | solution.py:293
  64.3 17.4 %collective-permute-start.10 = (f32[256,256]{1,0:T(8,128)S(1)}, f32[256,256]{1,0:T(8,128)S(1)}, u32[]{:S(2)}, u32[]{:S(2)}) collective-permute-start(f32[256,256]{1,0:T(8,128)S(1)} %add.76), channel_id=1, source_target_pairs={{0,1},{1,2},{2,0},{3,4},{4,5},{5,3},{6,7},{7,8},{8,6},{9,10},{10,1... | collective-permute-start | bytes 786440 | tf_op jit(solution)/shard_map/ppermute | solution.py:288
  69.5 12.6 %collective-permute-start.12 = (f32[256,256]{1,0:T(8,128)S(1)}, f32[256,256]{1,0:T(8,128)S(1)}, u32[]{:S(2)}, u32[]{:S(2)}) collective-permute-start(f32[256,256]{1,0:T(8,128)S(1)} %add.77), channel_id=1, source_target_pairs={{0,2},{1,0},{2,1},{3,5},{4,3},{5,4},{6,8},{7,6},{8,7},{9,11},{10,9... | collective-permute-start | bytes 786440 | tf_op jit(solution)/shard_map/ppermute | solution.py:288
  83.3 17.1 %collective-permute-start.14 = (f32[256,256]{1,0:T(8,128)S(1)}, f32[256,256]{1,0:T(8,128)S(1)}, u32[]{:S(2)}, u32[]{:S(2)}) collective-permute-start(f32[256,256]{1,0:T(8,128)S(1)} %get-tuple-element.88.refs_8_), channel_id=1, source_target_pairs={{0,1},{1,2},{2,0},{3,4},{4,5},{5,3},{6,7},{7,8},{8,6},{9,10},{10,1... | collective-permute-start | bytes 786440 | tf_op jit(solution)/shard_map/ppermute | solution.py:288
  85.8 14.6 %collective-permute-start.13 = (f32[256,256]{1,0:T(8,128)S(1)}, f32[256,256]{1,0:T(8,128)S(1)}, u32[]{:S(2)}, u32[]{:S(2)}) collective-permute-start(f32[256,256]{1,0:T(8,128)S(1)} %get-tuple-element.88.refs_8_), channel_id=1, source_target_pairs={{0,2},{1,0},{2,1},{3,5},{4,3},{5,4},{6,8},{7,6},{8,7},{9,11},{10,9... | collective-permute-start | bytes 786440 | tf_op jit(solution)/shard_map/ppermute | solution.py:288
  91.1 20.6 %all-to-all-start = ((f32[32,8,256]{2,1,0:T(8,128)}), f32[32,8,256]{2,1,0:T(8,128)S(1)}, u32[]{:S(2)}, u32[]{:S(2)}) async-start(f32[32,8,256]{2,1,0:T(8,128)} %bitcast.37), calls=%async_computation | async-start | bytes 524288 | tf_op jit(solution)/shard_map/all_to_all | solution.py:297
  100.4 19.5 %collective-permute-start.15 = (f32[256,256]{1,0:T(8,128)S(1)}, f32[256,256]{1,0:T(8,128)S(1)}, u32[]{:S(2)}, u32[]{:S(2)}) collective-permute-start(f32[256,256]{1,0:T(8,128)S(1)} %collective-permute-done.13.refs_9_), channel_id=1, source_target_pairs={{0,3},{1,4},{2,95},{3,6},{4,7},{5,2},{6,9},{7,10},{8,5},{9,12},{10... | collective-permute-start | bytes 786440 | tf_op jit(solution)/shard_map/ppermute | solution.py:293
  103.8 16.2 %collective-permute-start.16 = (f32[256,256]{1,0:T(8,128)S(1)}, f32[256,256]{1,0:T(8,128)S(1)}, u32[]{:S(2)}, u32[]{:S(2)}) collective-permute-start(f32[256,256]{1,0:T(8,128)S(1)} %collective-permute-done.14.refs_10_), channel_id=1, source_target_pairs={{0,3},{1,94},{2,95},{3,6},{4,1},{5,2},{6,9},{7,4},{8,5},{9,12},{10... | collective-permute-start | bytes 786440 | tf_op jit(solution)/shard_map/ppermute | solution.py:293
  112.4 28.2 %all-to-all-start.1 = ((f32[24,8,384]{2,1,0:T(8,128)}), f32[24,8,384]{2,1,0:T(8,128)}, u32[]{:S(2)}, u32[]{:S(2)}) async-start(f32[24,8,384]{2,1,0:T(8,128)} %sum_and_copy.2), calls=%async_computation.1 | async-start | bytes 589824 | tf_op jit(solution)/shard_map/all_to_all | solution.py:297
  124.2 6.2 %collective-permute-start.17 = (f32[4,256,256]{2,1,0:T(8,128)}, f32[4,256,256]{2,1,0:T(8,128)}, u32[]{:S(2)}, u32[]{:S(2)}) collective-permute-start(f32[4,256,256]{2,1,0:T(8,128)} %spread_terms.3), channel_id=1, source_target_pairs={{0,96},{96,0},{1,97},{97,1},{2,98},{98,2},{3,99},{99,3},{4,100},{1... | collective-permute-start | bytes 3145736 | tf_op jit(solution)/shard_map/ppermute | solution.py:275
  130.4 25.6 %copy-start.3 = (f32[256,256]{1,0:T(8,128)S(1)}, f32[256,256]{1,0:T(8,128)}, u32[]{:S(2)}) copy-start(f32[256,256]{1,0:T(8,128)} %get-tuple-element.94.kept_first) | copy-start | bytes 786436
  130.4 25.6 %copy-start.4 = (f32[256,256]{1,0:T(8,128)S(1)}, f32[256,256]{1,0:T(8,128)}, u32[]{:S(2)}) copy-start(f32[256,256]{1,0:T(8,128)} %get-tuple-element.96.kept) | copy-start | bytes 786436
  131.8 18.0 %collective-permute-start.19 = (f32[256,256]{1,0:T(8,128)S(1)}, f32[256,256]{1,0:T(8,128)S(1)}, u32[]{:S(2)}, u32[]{:S(2)}) collective-permute-start(f32[256,256]{1,0:T(8,128)S(1)} %get-tuple-element.106), channel_id=1, source_target_pairs={{0,192},{96,672},{192,384},{288,96},{384,576},{480,288},{576,0},{6... | collective-permute-start | bytes 786440 | tf_op jit(solution)/shard_map/ppermute | solution.py:284
  137.7 18.3 %collective-permute-start.18 = (f32[256,256]{1,0:T(8,128)S(1)}, f32[256,256]{1,0:T(8,128)S(1)}, u32[]{:S(2)}, u32[]{:S(2)}) collective-permute-start(f32[256,256]{1,0:T(8,128)S(1)} %get-tuple-element.107), channel_id=1, source_target_pairs={{0,576},{96,288},{192,0},{288,480},{384,192},{480,672},{576,384},{... | collective-permute-start | bytes 786440 | tf_op jit(solution)/shard_map/ppermute | solution.py:284
  142.4 21.8 %all-to-all-start.2 = ((f32[32,8,384]{2,1,0:T(8,128)}), f32[32,8,384]{2,1,0:T(8,128)}, u32[]{:S(2)}, u32[]{:S(2)}) async-start(f32[32,8,384]{2,1,0:T(8,128)} %sum_and_copy.3), calls=%async_computation.2 | async-start | bytes 786432 | tf_op jit(solution)/shard_map/all_to_all | solution.py:297
  157.1 16.6 %collective-permute-start.20 = (f32[256,256]{1,0:T(8,128)S(1)}, f32[256,256]{1,0:T(8,128)S(1)}, u32[]{:S(2)}, u32[]{:S(2)}) collective-permute-start(f32[256,256]{1,0:T(8,128)S(1)} %get-tuple-element.103), channel_id=1, source_target_pairs={{0,576},{96,288},{192,0},{288,480},{384,192},{480,672},{576,384},{... | collective-permute-start | bytes 786440 | tf_op jit(solution)/shard_map/ppermute | solution.py:284
